TPU v7x, 256 devices: a whole 4x4x8 slice. The times are simulated.
256 devices in a mesh: pb: 32 (over z, x), kv: 2 (over core), ha: 4 (over y).
Axes of the slice: x: 4, y: 4, z: 8, core: 2. Of those that a mesh axis runs over, the one named last changes fastest.
Arguments:
- queries: bfloat16 [2, 4096, 3072], P('kv', 'pb', 'ha'), may hold values from -40 to 40
- keys: bfloat16 [2, 4096, 3072], P('kv', 'pb', 'ha'), may hold values from -40 to 40
- values: bfloat16 [2, 4096, 3072], P('kv', 'pb', 'ha'), may hold values from -6 to 6
- out_grad: bfloat16 [2, 4096, 3072], P('kv', 'pb', 'ha'), may hold values from -6 to 6
- block_order: int32 [2, 64], P('kv'), may hold values from 0 to 63, each once within a row
Outputs:
- attended: bfloat16 [2, 4096, 3072], P('kv', 'pb', 'ha')
- q_grad: bfloat16 [2, 4096, 3072], P('kv', 'pb', 'ha')
- k_grad: bfloat16 [2, 4096, 3072], P('kv', 'pb', 'ha')
- v_grad: bfloat16 [2, 4096, 3072], P('kv', 'pb', 'ha')
Inputs may be any that keep to these rules, and one draw needn't show every extreme that they name: Each row of block_order holds every block number once.
All inputs are finite; a program needn't handle non-finite values.
Results may differ from a plain program's by a relative error of at most 0.02.
Values may be sent and summed in bfloat16 or wider, within the bound.
No kernel may reach another device: no remote copies, remote signals or barrier semaphores. Data moves between devices by JAX's collectives and lax.ppermute only.
A program may use at most 128 MiB of HBM per device.

v0:
```python
import math

import jax
import jax.numpy as jnp
from jax import lax
from jax.sharding import PartitionSpec as P

DH = 128
BLK = 64


def block_positions(order_row, start, count):
    picked = lax.dynamic_slice_in_dim(order_row, start // BLK, count // BLK, 0)
    within = jnp.tile(jnp.arange(BLK, dtype=jnp.int32), count // BLK)
    return jnp.repeat(picked * BLK, BLK) + within


def head_slice(array, head):
    return lax.dynamic_slice_in_dim(array, head * DH, DH, 1)


def masked_scores(query_rows, key_rows, allowed, score_scale):
    scores = jnp.dot(query_rows, key_rows.T, preferred_element_type=jnp.float32) * score_scale
    return jnp.where(allowed, scores, jnp.float32(-1e30))


def forward_output(expo, totals, value_rows):
    numer = jnp.dot(expo.astype(jnp.bfloat16), value_rows, preferred_element_type=jnp.float32)
    return (numer / totals[:, None]).astype(jnp.bfloat16)


def backward_head(
    query_rows, key_rows, value_rows, grad_rows, expo, totals, attended_head, score_scale
):
    probs = expo / totals[:, None]
    dsum = jnp.sum(grad_rows.astype(jnp.float32) * attended_head.astype(jnp.float32), axis=1)
    dprob = jnp.dot(grad_rows, value_rows.T, preferred_element_type=jnp.float32)
    dscore = (probs * (dprob - dsum[:, None])).astype(jnp.bfloat16)
    probs_low = probs.astype(jnp.bfloat16)
    q_head = (jnp.dot(dscore, key_rows, preferred_element_type=jnp.float32) * score_scale).astype(
        jnp.bfloat16
    )
    k_head = (
        lax.dot_general(
            dscore, query_rows, (((0,), (0,)), ((), ())), preferred_element_type=jnp.float32
        )
        * score_scale
    )
    v_head = lax.dot_general(
        probs_low, grad_rows, (((0,), (0,)), ((), ())), preferred_element_type=jnp.float32
    )
    return (q_head, k_head, v_head)


def shards(queries, keys, values, out_grad, block_order):
    q_rows = queries.shape[1]
    width = queries.shape[2]
    head_count = width // DH
    score_scale = 1.0 / math.sqrt(DH)
    total_rows = q_rows * lax.axis_size("pb")
    q_mat = queries[0]
    grad_mat = out_grad[0]
    order_row = block_order[0]
    q_pos = block_positions(order_row, lax.axis_index("pb") * q_rows, q_rows)
    k_pos = block_positions(order_row, 0, total_rows)
    allowed = k_pos[None, :] <= q_pos[:, None]
    empty_out = jnp.zeros((q_rows, width), jnp.bfloat16)
    empty_terms = jnp.zeros((total_rows, width), jnp.float32)
    first_k, first_v = (
        lax.all_gather(keys, "pb", axis=1, tiled=True),
        lax.all_gather(values, "pb", axis=1, tiled=True),
    )
    key_first = first_k[0]
    value_first = first_v[0]
    empty_stats = jnp.zeros((head_count, q_rows), jnp.float32)

    def forward_step(head, carried):
        att_all, maxima, sums = carried
        query_rows = head_slice(q_mat, head)
        key_rows = head_slice(key_first, head)
        value_rows = head_slice(value_first, head)
        scores = masked_scores(query_rows, key_rows, allowed, score_scale)
        row_max = jnp.max(scores, axis=1)
        expo = jnp.exp(scores - row_max[:, None])
        totals = jnp.sum(expo, axis=1)
        attended_head = forward_output(expo, totals, value_rows)
        att_all = lax.dynamic_update_slice_in_dim(att_all, attended_head, head * DH, 1)
        maxima = lax.dynamic_update_slice_in_dim(maxima, row_max[None], head, 0)
        sums = lax.dynamic_update_slice_in_dim(sums, totals[None], head, 0)
        return (att_all, maxima, sums)

    attended, maxima, sums = lax.fori_loop(
        0, head_count, forward_step, (empty_out, empty_stats, empty_stats)
    )
    second_k, second_v = (
        lax.all_gather(keys, "pb", axis=1, tiled=True),
        lax.all_gather(values, "pb", axis=1, tiled=True),
    )
    key_second = second_k[0]
    value_second = second_v[0]

    def backward_step(head, carried):
        qg_all, kt_all, vt_all = carried
        query_rows = head_slice(q_mat, head)
        key_rows = head_slice(key_second, head)
        value_rows = head_slice(value_second, head)
        grad_rows = head_slice(grad_mat, head)
        scores = masked_scores(query_rows, key_rows, allowed, score_scale)
        row_max = lax.dynamic_slice_in_dim(maxima, head, 1, 0)[0]
        totals = lax.dynamic_slice_in_dim(sums, head, 1, 0)[0]
        expo = jnp.exp(scores - row_max[:, None])
        attended_head = head_slice(attended, head)
        q_head, k_head, v_head = backward_head(
            query_rows, key_rows, value_rows, grad_rows, expo, totals, attended_head, score_scale
        )
        qg_all = lax.dynamic_update_slice_in_dim(qg_all, q_head, head * DH, 1)
        kt_all = lax.dynamic_update_slice_in_dim(kt_all, k_head, head * DH, 1)
        vt_all = lax.dynamic_update_slice_in_dim(vt_all, v_head, head * DH, 1)
        return (qg_all, kt_all, vt_all)

    q_grad, k_terms, v_terms = lax.fori_loop(
        0, head_count, backward_step, (empty_out, empty_terms, empty_terms)
    )
    k_grad, v_grad = (
        lax.psum_scatter(
            k_terms.astype(jnp.bfloat16), "pb", scatter_dimension=0, tiled=True
        ).astype(jnp.float32),
        lax.psum_scatter(
            v_terms.astype(jnp.bfloat16), "pb", scatter_dimension=0, tiled=True
        ).astype(jnp.float32),
    )
    return (
        attended[None],
        q_grad[None],
        k_grad.astype(jnp.bfloat16)[None],
        v_grad.astype(jnp.bfloat16)[None],
    )


def solution(mesh):
    placed = (
        P("kv", "pb", "ha"),
        P("kv", "pb", "ha"),
        P("kv", "pb", "ha"),
        P("kv", "pb", "ha"),
        P("kv", None),
    )
    return jax.shard_map(
        shards,
        mesh=mesh,
        in_specs=placed,
        out_specs=(
            P("kv", "pb", "ha"),
            P("kv", "pb", "ha"),
            P("kv", "pb", "ha"),
            P("kv", "pb", "ha"),
        ),
        check_vma=False,
    )
```

profile of v0, /device:TPU:8, one launch (start us, length us, event | category | flops | bytes accessed | tf_op | source)
XLA Modules:
  0.0 733.4 jit_solution(12284813428806300715)
XLA Ops:
  10.4 91.7 %all-gather.3.cloned.1.call-done = bf16[1,4096,768]{2,1,0:T(8,128)(2,1)} async-done(((bf16[1,128,768]{2,1,0:T(8,128)(2,1)}), bf16[1,4096,768]{2,1,0:T(8,128)(2,1)}) %all-gather.3.cloned.1.call-update) | async-done | bytes 6291472 | tf_op jit(solution)/shard_map/all_gather | solution.py:70
  102.2 88.3 %all-gather.5.cloned.1.call-done = bf16[1,4096,768]{2,1,0:T(8,128)(2,1)} async-done(((bf16[1,128,768]{2,1,0:T(8,128)(2,1)}), bf16[1,4096,768]{2,1,0:T(8,128)(2,1)}) %all-gather.5.cloned.1.call-update) | async-done | bytes 6291472 | tf_op jit(solution)/shard_map/all_gather | solution.py:71
  190.5 24.7 %while.36 = (s32[]{:T(128)}, bf16[128,768]{1,0:T(8,128)(2,1)S(1)}, f32[6,128]{1,0:T(8,128)S(1)}, f32[6,128]{1,0:T(8,128)S(1)}, bf16[128,768]{1,0:T(8,128)(2,1)},...) while((s32[]{:T(128)}, bf16[128,768]{1,0:T(8,128)(2,1)S(1)}, ...), condition=%wide.region_3.4_spmd.clone, body=%wide.region_0.3_spmd.clone.sunk | while | flops 272662272 | bytes 8477883 | solution.py:92
  198.7 1.8 fusion.65
  200.9 1.8 fusion.67
  206.9 1.8 fusion.65
  211.0 1.8 fusion.65
  215.1 3.0 broadcast_in_dim.72.clone
  218.1 3.0 broadcast_in_dim.72
  221.1 55.8 %while.37 = (s32[]{:T(128)}, bf16[128,768]{1,0:T(8,128)(2,1)S(1)}, bf16[4096,768]{1,0:T(8,128)(2,1)}, bf16[4096,768]{1,0:T(8,128)(2,1)}, bf16[128,768]{1,0:T(8,1...) while((s32[]{:T(128)}, bf16[128,768]{1,0:T(8,128)(2,1)S(1)}, ...), condition=%wide.region_6.7_spmd.clone, body=%wide.region_4.6_spmd.clone.sunk | while | flops 676429696 | bytes 17032924 | solution.py:121
  221.3 1.9 fusion.79
  228.1 2.3 fusion.82
  230.5 1.9 fusion.79
  237.4 2.3 fusion.82
  239.8 1.9 fusion.79
  246.7 2.3 fusion.82
  249.2 1.9 fusion.79
  256.0 2.3 fusion.82
  258.5 1.9 fusion.79
  265.3 2.3 fusion.82
  267.8 1.9 fusion.79
  274.6 2.3 fusion.82
  278.3 220.6 %reduce-scatter.5.cloned.1.call-done = bf16[128,768]{1,0:T(8,128)(2,1)} async-done(((bf16[4096,768]{1,0:T(8,128)(2,1)}), bf16[128,768]{1,0:T(8,128)(2,1)}) %reduce-scatter.5.cloned.1.call-update) | async-done | bytes 196624 | tf_op jit(solution)/shard_map/reduce_scatter | solution.py:128
  498.9 228.0 %reduce-scatter.3.cloned.1.call-done = bf16[128,768]{1,0:T(8,128)(2,1)} async-done(((bf16[4096,768]{1,0:T(8,128)(2,1)}), bf16[128,768]{1,0:T(8,128)(2,1)}) %reduce-scatter.3.cloned.1.call-update) | async-done | bytes 196624 | tf_op jit(solution)/shard_map/reduce_scatter | solution.py:125
  (80 shorter events, 52.1 us)
Async XLA Ops:
  7.2 95.0 %all-gather.3.cloned.1.call-start = ((), (), s32[]{:S(2)}) async-start(), calls=%async_computation.2 | async-start | bytes 6488064 | tf_op jit(solution)/shard_map/all_gather | solution.py:70
  7.9 182.5 %all-gather.5.cloned.1.call-start = ((), (), s32[]{:S(2)}) async-start(), calls=%async_computation.3 | async-start | bytes 6488064 | tf_op jit(solution)/shard_map/all_gather | solution.py:71
  8.6 490.2 %reduce-scatter.5.cloned.1.call-start = ((), (), s32[]{:S(2)}) async-start(), calls=%async_computation.5 | async-start | bytes 6488064 | tf_op jit(solution)/shard_map/reduce_scatter | solution.py:128
  218.1 3.0 copy-start
  277.0 0.7 copy-start.1
  277.0 0.7 copy-start.2
  277.7 449.2 %reduce-scatter.3.cloned.1.call-start = ((), (), s32[]{:S(2)}) async-start(), calls=%async_computation.4 | async-start | bytes 6488064 | tf_op jit(solution)/shard_map/reduce_scatter | solution.py:125
Sparse Core Ops, SparseCore 0:
  10.6 91.5 all-gather.2
  104.7 85.6 all-gather.4
  277.1 221.7 reduce-scatter.4
  503.8 223.0 reduce-scatter.2
where the time goes:
time: 735 us; the launch traced here: 733 us
  waiting for transfers between devices  631 us (86%)
  matrix products  76.4 us (10%)
  between operations  13.8 us (2%)
  local copies, waits for them, and re-layouts  7.39 us (1%)
    reduce_scatter x1, waiting for transfers between devices, shards(): lax.psum_scatter(k_terms.astype(jnp.bfloat16), 'pb', scatter_dimension=0,...  228 us
    reduce_scatter x1, waiting for transfers between devices, shards(): lax.psum_scatter(v_terms.astype(jnp.bfloat16), 'pb', scatter_dimension=0,...  221 us
    all_gather x1, waiting for transfers between devices, shards(): lax.all_gather(keys, 'pb', axis=1, tiled=True)  91.7 us
    all_gather x1, waiting for transfers between devices, shards(): lax.all_gather(values, 'pb', axis=1, tiled=True)  88.3 us
    dot_general x12, matrix products, masked_scores(): jnp.dot(query_rows, key_rows.T, preferred_element_type=jnp.float32)  22.3 us
  transfers between devices with their start and end apart: 4, of which 4 were waited for; matrix products, arithmetic and copies ran while one was open for 0% of the time, Pallas kernels for 0%

commit v1 on v0

v1 whole, which is shorter than its diff:
```python
import math

import jax
import jax.numpy as jnp
import numpy as np
from jax import lax
from jax.experimental import pallas as pl
from jax.experimental.pallas import tpu as pltpu
from jax.sharding import Mesh
from jax.sharding import PartitionSpec as P

DH = 128
BLK = 64
SCALE = 1.0 / math.sqrt(DH)
SCALE2 = SCALE * math.log2(math.e)
GROUP = 4
ROWS = GROUP * BLK
WIDE = 512
F32 = jnp.float32
BF16 = jnp.bfloat16


def mm(a, b):
    return jnp.dot(a, b, preferred_element_type=F32)


def mm_nt(a, b):
    return lax.dot_general(a, b, (((1,), (1,)), ((), ())), preferred_element_type=F32)


def mm_tn(a, b):
    return lax.dot_general(a, b, (((0,), (0,)), ((), ())), preferred_element_type=F32)


def attention_kernel(
    nz, nx, order, me, qg, kv0, kv1, kv3, kv2a, kv2b,
    oq, o0, o1, o2, o3,
    ks, vs, qs, gs, scr, dka, dva, qacc, oacc, rowpos, sblk, spos,
):
    x = me[0]
    per_part = 2 * nz
    half = per_part // 2
    seq = ks.shape[0]

    def block_of(part, j):
        src = lax.rem(x - part + nx, nx)
        return order[((j // 2) * nx + src) * 2 + j % 2]

    def part_rows(part, j):
        if part == 2:
            ref, i = (kv2a, j) if j < half else (kv2b, j - half)
        else:
            ref, i = (kv0, kv1, None, kv3)[part], j
        return ref, i * BLK

    for part in range(nx):
        for j in range(per_part):
            p = block_of(part, j)
            ref, start = part_rows(part, j)
            at = pl.ds(pl.multiple_of(p * BLK, BLK), BLK)
            ks[at, :] = ref[start:start + BLK, :DH]
            vs[at, :] = ref[start:start + BLK, DH:]

    own = [block_of(0, j) for j in range(per_part)]
    for j in range(per_part):
        rank = jnp.int32(0)
        for i in range(per_part):
            if i != j:
                rank = rank + (own[i] < own[j]).astype(jnp.int32)
        sblk[rank] = jnp.int32(j)
        spos[rank] = own[j]
        at = pl.ds(pl.multiple_of(rank * BLK, BLK), BLK)
        qs[at, :] = qg[j * BLK:(j + 1) * BLK, :DH]
        gs[at, :] = qg[j * BLK:(j + 1) * BLK, DH:]

    dka[...] = jnp.zeros_like(dka)
    dva[...] = jnp.zeros_like(dva)

    def group_step(g, carry):
        base = g * GROUP
        lowest = spos[base]
        highest = spos[base + GROUP - 1]
        full = (lowest * BLK) // WIDE
        count = ((highest + 1) * BLK + WIDE - 1) // WIDE
        for k in range(GROUP):
            within = lax.broadcasted_iota(jnp.int32, (BLK, DH), 0)
            rowpos[k * BLK:(k + 1) * BLK, :] = within + spos[base + k] * BLK
        at = pl.ds(pl.multiple_of(base * BLK, ROWS), ROWS)
        q = qs[at, :]
        gr = gs[at, :]

        def chunk(c):
            return pl.ds(pl.multiple_of(c * WIDE, WIDE), WIDE)

        def fold(op, s):
            r = s[:, :DH]
            for i in range(1, WIDE // DH):
                r = op(r, s[:, i * DH:(i + 1) * DH])
            return r

        def score_step(masked):
            def step(c, m):
                s = mm_nt(q, ks[chunk(c), :])
                if masked:
                    pos = rowpos[:, :1]
                    key = lax.broadcasted_iota(jnp.int32, (ROWS, WIDE), 1) + c * WIDE
                    s = jnp.where(key <= pos, s, F32(-1e30))
                scr[:, chunk(c)] = s
                return jnp.maximum(m, fold(jnp.maximum, s))
            return step

        m = jnp.full((ROWS, DH), -1e30, F32)
        m = lax.fori_loop(0, full, score_step(False), m)
        m = lax.fori_loop(full, count, score_step(True), m)
        top = jnp.max(m, axis=1, keepdims=True)

        oacc[...] = jnp.zeros_like(oacc)

        def expo_step(c, tot):
            e = jnp.exp2((scr[:, chunk(c)] - top) * F32(SCALE2))
            scr[:, chunk(c)] = e
            oacc[...] += mm(e.astype(BF16), vs[chunk(c), :])
            return tot + fold(jnp.add, e)

        tot = lax.fori_loop(0, count, expo_step, jnp.zeros((ROWS, DH), F32))
        total = jnp.sum(tot, axis=1, keepdims=True)
        inv = 1.0 / total
        att = (oacc[...] / total).astype(BF16)
        dsum = jnp.sum(gr.astype(F32) * att.astype(F32), axis=1, keepdims=True)
        qacc[...] = jnp.zeros_like(qacc)

        def back_step(c, carry):
            dp = mm_nt(gr, vs[chunk(c), :])
            p = scr[:, chunk(c)] * inv
            ds = (p * (dp - dsum)).astype(BF16)
            pb = p.astype(BF16)
            qacc[...] += mm(ds, ks[chunk(c), :])
            dka[chunk(c), :] += mm_tn(ds, q)
            dva[chunk(c), :] += mm_tn(pb, gr)
            return carry

        lax.fori_loop(0, count, back_step, 0)
        dq = (qacc[...] * F32(SCALE)).astype(BF16)
        for k in range(GROUP):
            to = pl.ds(pl.multiple_of(sblk[base + k] * BLK, BLK), BLK)
            oq[to, :DH] = att[k * BLK:(k + 1) * BLK, :]
            oq[to, DH:] = dq[k * BLK:(k + 1) * BLK, :]
        return carry

    lax.fori_loop(0, per_part // GROUP, group_step, 0)

    outs = (o0, o1, o2, o3)
    for part in range(nx):
        for j in range(per_part):
            p = block_of(part, j)
            at = pl.ds(pl.multiple_of(p * BLK, BLK), BLK)
            outs[part][j * BLK:(j + 1) * BLK, :DH] = (dka[at, :] * F32(SCALE)).astype(BF16)
            outs[part][j * BLK:(j + 1) * BLK, DH:] = dva[at, :].astype(BF16)


def attention(nz, nx, order, me, qg, parts):
    rows = qg.shape[0]
    seq = rows * nx
    vm = pl.BlockSpec(memory_space=pltpu.VMEM)
    sm = pl.BlockSpec(memory_space=pltpu.SMEM)
    out = jax.ShapeDtypeStruct((rows, 2 * DH), BF16)
    return pl.pallas_call(
        lambda *refs: attention_kernel(nz, nx, *refs),
        out_shape=(out,) * 5,
        in_specs=[sm, sm] + [vm] * 6,
        out_specs=(vm,) * 5,
        scratch_shapes=[
            pltpu.VMEM((seq, DH), BF16),
            pltpu.VMEM((seq, DH), BF16),
            pltpu.VMEM((rows, DH), BF16),
            pltpu.VMEM((rows, DH), BF16),
            pltpu.VMEM((ROWS, seq), F32),
            pltpu.VMEM((seq, DH), F32),
            pltpu.VMEM((seq, DH), F32),
            pltpu.VMEM((ROWS, DH), F32),
            pltpu.VMEM((ROWS, DH), F32),
            pltpu.VMEM((ROWS, DH), jnp.int32),
            pltpu.SMEM((rows // BLK,), jnp.int32),
            pltpu.SMEM((rows // BLK,), jnp.int32),
        ],
        compiler_params=pltpu.CompilerParams(vmem_limit_bytes=48 * 2**20),
        name="attention",
    )(order, me, qg, *parts)


def by_head(a, b, slots):
    rows, width = a.shape
    heads = width // DH
    both = jnp.concatenate(
        [a.reshape(rows, heads, 1, DH), b.reshape(rows, heads, 1, DH)], axis=2
    ).reshape(rows, heads, 2 * DH)
    both = both.transpose(1, 0, 2)
    return jnp.pad(both, ((0, slots - heads), (0, 0), (0, 0)))


def from_heads(stacked, heads):
    rows = stacked.shape[1]
    a = stacked[:heads, :, :DH].transpose(1, 0, 2).reshape(rows, heads * DH)
    b = stacked[:heads, :, DH:].transpose(1, 0, 2).reshape(rows, heads * DH)
    return a, b


def make_shards(nz, nx):
    def to(step):
        return [(i, (i + step) % nx) for i in range(nx)]

    def exchange(v):
        return lax.all_to_all(v, "z", 0, 0, tiled=True)

    def shards(queries, keys, values, out_grad, block_order):
        rows, width = queries.shape[1:]
        heads = width // DH
        kv = exchange(by_head(keys[0], values[0], nz)).reshape(nz * rows, 2 * DH)
        right = lax.ppermute(kv, "x", to(1))
        left = lax.ppermute(kv, "x", to(-1))
        qg = exchange(by_head(queries[0], out_grad[0], nz)).reshape(nz * rows, 2 * DH)
        cut = nz * rows // 2
        far_a = lax.ppermute(right[:cut], "x", to(1))
        far_b = lax.ppermute(left[cut:], "x", to(-1))
        me = lax.axis_index("x").astype(jnp.int32).reshape(1)
        oq, o0, o1, o2, o3 = attention(
            nz, nx, block_order[0], me, qg, (kv, right, left, far_a, far_b)
        )
        a1 = lax.ppermute(o1, "x", to(-1))
        a3 = lax.ppermute(o3, "x", to(1))
        a2 = lax.ppermute(o2, "x", to(2))
        att, q_grad = from_heads(exchange(oq.reshape(nz, rows, 2 * DH)), heads)
        total = (
            o0.astype(F32) + a1.astype(F32) + a2.astype(F32) + a3.astype(F32)
        ).astype(BF16)
        k_grad, v_grad = from_heads(exchange(total.reshape(nz, rows, 2 * DH)), heads)
        return att[None], q_grad[None], k_grad[None], v_grad[None]

    return shards


def solution(mesh):
    sizes = dict(mesh.shape)
    nx = 4
    nz = sizes["pb"] // nx
    fine = Mesh(
        np.asarray(mesh.devices).reshape(nz, nx, sizes["kv"], sizes["ha"]), ("z", "x", "kv", "ha")
    )
    split = P("kv", ("z", "x"), "ha")
    return jax.shard_map(
        make_shards(nz, nx),
        mesh=fine,
        in_specs=(split, split, split, split, P("kv", None)),
        out_specs=(split,) * 4,
        check_vma=False,
    )
```

time: 735 us -> 153 us (0.21)
  waiting for transfers between devices: 631 us -> 73.6 us
  matrix products: 76.4 us -> 0 us
  starting transfers between devices: 0.12 us -> 37.3 us
  Pallas kernels: 0 us -> 23.4 us
  between operations: 13.8 us -> 0.79 us
  local copies, waits for them, and re-layouts: 7.39 us -> 15.4 us
    reduce_scatter x2 -> x0, waiting for transfers between devices: 449 us -> none  [the longest x1 228 us: shards(): lax.psum_scatter(k_terms.astype(jnp.bfloat16), 'pb', scatter_dimension=0,...]
    all_gather x2 -> x0, waiting for transfers between devices: 180 us -> none  [the longest x1 91.7 us: shards(): lax.all_gather(keys, 'pb', axis=1, tiled=True)]
    dot_general x42 -> x0, matrix products: 76.4 us -> none  [the longest x12 22.3 us: masked_scores(): jnp.dot(query_rows, key_rows.T, preferred_element_type=jnp.float32)]
    ppermute x0 -> x7, waiting for transfers between devices: none -> 42.1 us  [the longest x1 18 us: shards(): a1 = lax.ppermute(o1, 'x', to(-1))]
    all_to_all x0 -> x4, waiting for transfers between devices: none -> 31.5 us  [exchange(): return lax.all_to_all(v, 'z', 0, 0, tiled=True)]
    all_to_all x0 -> x4, starting transfers between devices: none -> 25.6 us  [exchange(): return lax.all_to_all(v, 'z', 0, 0, tiled=True)]
    pallas_call x0 -> x1, Pallas kernels: none -> 23.4 us  [attention(): pl.pallas_call(lambda *refs: attention_kernel(nz, nx, *refs), out_shape=(...]
    ppermute x0 -> x7, starting transfers between devices: none -> 11.8 us  [the longest x1 3.77 us: shards(): far_b = lax.ppermute(left[cut:], 'x', to(-1))]
  transfers between devices with their start and end apart: 4 -> 11, of which waited for: 4 -> 7; matrix products, arithmetic and copies ran while one was open for 0% -> 4% of each run, Pallas kernels for 0% -> 0%
where the time goes in v1:
time: 153 us; the launch traced here: 151 us
  waiting for transfers between devices  73.6 us (48%)
  starting transfers between devices  37.3 us (24%)
  Pallas kernels  23.4 us (15%)
  local copies, waits for them, and re-layouts  15.4 us (10%)
    all_to_all x4, waiting for transfers between devices, exchange(): return lax.all_to_all(v, 'z', 0, 0, tiled=True)  31.5 us
    all_to_all x4, starting transfers between devices, exchange(): return lax.all_to_all(v, 'z', 0, 0, tiled=True)  25.6 us
    pallas_call x1, Pallas kernels, attention(): pl.pallas_call(lambda *refs: attention_kernel(nz, nx, *refs), out_shape=(...  23.4 us
    ppermute x1, waiting for transfers between devices, shards(): a1 = lax.ppermute(o1, 'x', to(-1))  18 us
    ppermute x1, waiting for transfers between devices, shards(): left = lax.ppermute(kv, 'x', to(-1))  11.4 us
    unnamed x32, local copies, waits for them, and re-layouts  10.4 us
    ppermute x1, waiting for transfers between devices, shards(): a3 = lax.ppermute(o3, 'x', to(1))  4.39 us
    ppermute x1, waiting for transfers between devices, shards(): far_a = lax.ppermute(right[:cut], 'x', to(1))  4.36 us
  transfers between devices with their start and end apart: 11, of which 7 were waited for; matrix products, arithmetic and copies ran while one was open for 4% of the time, Pallas kernels for 0%

profile of v1, /device:TPU:8, one launch (start us, length us, event | category | flops | bytes accessed | tf_op | source)
XLA Modules:
  0.0 150.9 jit_solution(1061952135243549120)
XLA Ops:
  0.6 1.1 copy.29
  2.0 0.9 pad.8
  2.9 8.6 %all-to-all-start.1 = ((bf16[8,128,256]{1,2,0:T(8,128)(2,1)}), bf16[8,128,256]{1,2,0:T(8,128)(2,1)S(1)}, u32[]{:S(2)}, u32[]{:S(2)}) async-start(bf16[8,128,256]{1,2,0:T(8,128)(2,1)} %pad.8), calls=%async_computation.1 | async-start | bytes 1048576 | tf_op jit(solution)/shard_map/all_to_all | solution.py:213
  12.7 0.9 pad.7
  13.5 15.5 %all-to-all-done.1 = bf16[8,128,256]{1,2,0:T(8,128)(2,1)S(1)} async-done(((bf16[8,128,256]{1,2,0:T(8,128)(2,1)}), bf16[8,128,256]{1,2,0:T(8,128)(2,1)S(1)}, u32[]{:S(2)}, u32[]{:S(2)}) %all-to-all-start.1) | async-done | bytes 524320 | tf_op jit(solution)/shard_map/all_to_all | solution.py:213
  29.0 3.5 %all-to-all-start = ((bf16[8,128,256]{1,2,0:T(8,128)(2,1)}), bf16[8,128,256]{1,2,0:T(8,128)(2,1)S(1)}, u32[]{:S(2)}, u32[]{:S(2)}) async-start(bf16[8,128,256]{1,2,0:T(8,128)(2,1)} %pad.7), calls=%async_computation | async-start | bytes 1048576 | tf_op jit(solution)/shard_map/all_to_all | solution.py:213
  32.7 2.8 %collective-permute-start.1 = (bf16[1024,256]{1,0:T(8,128)(2,1)S(1)}, bf16[1024,256]{1,0:T(8,128)(2,1)S(1)}, u32[]{:S(2)}, u32[]{:S(2)}) collective-permute-start(bf16[1024,256]{1,0:T(8,128)(2,1)S(1)} %bitcast.28), channel_id=1, source_target_pairs={{0,24},{8,0},{16,8},{24,16},{1,25},{9,1},{17,9},{25,17},{2,26},{10... | collective-permute-start | bytes 1572872 | tf_op jit(solution)/shard_map/ppermute | solution.py:220
  35.5 11.4 %collective-permute-done.1.refs_5_ = bf16[1024,256]{1,0:T(8,128)(2,1)S(1)} collective-permute-done((bf16[1024,256]{1,0:T(8,128)(2,1)S(1)}, bf16[1024,256]{1,0:T(8,128)(2,1)S(1)}, u32[]{:S(2)}, u32[]{:S(2)}) %collective-permute-start.1) | collective-permute-done | bytes 524320 | tf_op jit(solution)/shard_map/ppermute | solution.py:220
  46.9 3.8 %collective-permute-start.3 = (bf16[512,256]{1,0:T(8,128)(2,1)S(1)}, bf16[512,256]{1,0:T(8,128)(2,1)S(1)}, u32[]{:S(2)}, u32[]{:S(2)}) collective-permute-start(bf16[512,256]{1,0:T(8,128)(2,1)S(1)} %slice.25), channel_id=1, source_target_pairs={{0,24},{8,0},{16,8},{24,16},{1,25},{9,1},{17,9},{25,17},{2,26},{10... | collective-permute-start | bytes 786440 | tf_op jit(solution)/shard_map/ppermute | solution.py:224
  51.6 3.9 %collective-permute-done.3.refs_7_ = bf16[512,256]{1,0:T(8,128)(2,1)S(1)} collective-permute-done((bf16[512,256]{1,0:T(8,128)(2,1)S(1)}, bf16[512,256]{1,0:T(8,128)(2,1)S(1)}, u32[]{:S(2)}, u32[]{:S(2)}) %collective-permute-start.3) | collective-permute-done | bytes 262176 | tf_op jit(solution)/shard_map/ppermute | solution.py:224
  55.6 4.4 %collective-permute-done.2.refs_6_ = bf16[512,256]{1,0:T(8,128)(2,1)S(1)} collective-permute-done((bf16[512,256]{1,0:T(8,128)(2,1)}, bf16[512,256]{1,0:T(8,128)(2,1)S(1)}, u32[]{:S(2)}, u32[]{:S(2)}) %collective-permute-start.2) | collective-permute-done | bytes 262176 | tf_op jit(solution)/shard_map/ppermute | solution.py:223
  61.3 0.9 copy-done.1
  62.3 23.4 %attention.1 = (bf16[1024,256]{1,0:T(8,128)(2,1)S(1)}, bf16[1024,256]{1,0:T(8,128)(2,1)S(1)}, bf16[1024,256]{1,0:T(8,128)(2,1)S(1)}, bf16[1024,256]{1,0:T(8,128)(2,1)S(1)}, bf16[1024,256]{1,0:T(8,128)(2,1)S(1)}) custom-call(s32[64]{0:T(128)S(1)} %bitcast.33, s32[1]{0:T(128)} %bitcast.1.refs_1_, bf16[1024,256]{1,0:T(8,128)(2,1)S(1)} %bitcast.31, ...), custom_call_target="tpu_custom_call" | custom-call | tf_op jit(solution)/shard_map/attention/pallas_call | solution.py:167
  88.1 1.0 copy.33
  89.1 6.6 %all-to-all-start.2 = ((bf16[8,128,256]{1,2,0:T(8,128)(2,1)}), bf16[8,128,256]{1,2,0:T(8,128)(2,1)S(1)}, u32[]{:S(2)}, u32[]{:S(2)}) async-start(bf16[8,128,256]{1,2,0:T(8,128)(2,1)} %copy.33), calls=%async_computation.2 | async-start | bytes 1048576 | tf_op jit(solution)/shard_map/all_to_all | solution.py:213
  95.9 3.8 %collective-permute-start.5 = (bf16[1024,256]{1,0:T(8,128)(2,1)S(1)}, bf16[1024,256]{1,0:T(8,128)(2,1)S(1)}, u32[]{:S(2)}, u32[]{:S(2)}) collective-permute-start(bf16[1024,256]{1,0:T(8,128)(2,1)S(1)} %copy-done.6), channel_id=1, source_target_pairs={{0,16},{8,24},{16,0},{24,8},{1,17},{9,25},{17,1},{25,9},{2,18},{10... | collective-permute-start | bytes 1572872 | tf_op jit(solution)/shard_map/ppermute | solution.py:231
  99.7 1.3 collective-permute-start.6
  101.0 18.0 %collective-permute-done.4 = bf16[1024,256]{1,0:T(8,128)(2,1)S(1)} collective-permute-done((bf16[1024,256]{1,0:T(8,128)(2,1)S(1)}, bf16[1024,256]{1,0:T(8,128)(2,1)S(1)}, u32[]{:S(2)}, u32[]{:S(2)}) %collective-permute-start.4) | collective-permute-done | bytes 524320 | tf_op jit(solution)/shard_map/ppermute | solution.py:229
  119.0 4.4 %collective-permute-done.6 = bf16[1024,256]{1,0:T(8,128)(2,1)S(1)} collective-permute-done((bf16[1024,256]{1,0:T(8,128)(2,1)S(1)}, bf16[1024,256]{1,0:T(8,128)(2,1)S(1)}, u32[]{:S(2)}, u32[]{:S(2)}) %collective-permute-start.6) | collective-permute-done | bytes 524320 | tf_op jit(solution)/shard_map/ppermute | solution.py:230
  123.7 1.0 copy.34
  124.7 6.8 %all-to-all-start.3 = ((bf16[8,128,256]{1,2,0:T(8,128)(2,1)}), bf16[8,128,256]{1,2,0:T(8,128)(2,1)S(1)}, u32[]{:S(2)}, u32[]{:S(2)}) async-start(bf16[8,128,256]{1,2,0:T(8,128)(2,1)} %copy.34), calls=%async_computation.3 | async-start | bytes 1048576 | tf_op jit(solution)/shard_map/all_to_all | solution.py:213
  131.6 0.8 copy.36
  133.2 16.0 %all-to-all-done.3 = bf16[8,128,256]{1,2,0:T(8,128)(2,1)S(1)} async-done(((bf16[8,128,256]{1,2,0:T(8,128)(2,1)}), bf16[8,128,256]{1,2,0:T(8,128)(2,1)S(1)}, u32[]{:S(2)}, u32[]{:S(2)}) %all-to-all-start.3) | async-done | bytes 524320 | tf_op jit(solution)/shard_map/all_to_all | solution.py:213
  149.3 0.8 copy.38
  (46 shorter events, 8.4 us)
Async XLA Ops:
  0.6 1.1 copy-start.9
  2.9 8.6 %copy-start.10 = (bf16[1,128,768]{2,1,0:T(8,128)(2,1)S(1)}, bf16[1,128,768]{2,1,0:T(8,128)(2,1)}, u32[]{:S(2)}) copy-start(bf16[1,128,768]{2,1,0:T(8,128)(2,1)} %param.5) | copy-start | bytes 589828
  2.9 26.1 %all-to-all-start.1 = ((bf16[8,128,256]{1,2,0:T(8,128)(2,1)}), bf16[8,128,256]{1,2,0:T(8,128)(2,1)S(1)}, u32[]{:S(2)}, u32[]{:S(2)}) async-start(bf16[8,128,256]{1,2,0:T(8,128)(2,1)} %pad.8), calls=%async_computation.1 | async-start | bytes 1048576 | tf_op jit(solution)/shard_map/all_to_all | solution.py:213
  11.5 0.9 copy-start.11
  29.0 22.5 %all-to-all-start = ((bf16[8,128,256]{1,2,0:T(8,128)(2,1)}), bf16[8,128,256]{1,2,0:T(8,128)(2,1)S(1)}, u32[]{:S(2)}, u32[]{:S(2)}) async-start(bf16[8,128,256]{1,2,0:T(8,128)(2,1)} %pad.7), calls=%async_computation | async-start | bytes 1048576 | tf_op jit(solution)/shard_map/all_to_all | solution.py:213
  32.7 14.2 %collective-permute-start.1 = (bf16[1024,256]{1,0:T(8,128)(2,1)S(1)}, bf16[1024,256]{1,0:T(8,128)(2,1)S(1)}, u32[]{:S(2)}, u32[]{:S(2)}) collective-permute-start(bf16[1024,256]{1,0:T(8,128)(2,1)S(1)} %bitcast.28), channel_id=1, source_target_pairs={{0,24},{8,0},{16,8},{24,16},{1,25},{9,1},{17,9},{25,17},{2,26},{10... | collective-permute-start | bytes 1572872 | tf_op jit(solution)/shard_map/ppermute | solution.py:220
  35.5 15.2 %collective-permute-start = (bf16[1024,256]{1,0:T(8,128)(2,1)S(1)}, bf16[1024,256]{1,0:T(8,128)(2,1)S(1)}, u32[]{:S(2)}, u32[]{:S(2)}) collective-permute-start(bf16[1024,256]{1,0:T(8,128)(2,1)S(1)} %bitcast.29), channel_id=1, source_target_pairs={{0,8},{8,16},{16,24},{24,0},{1,9},{9,17},{17,25},{25,1},{2,10},{10... | collective-permute-start | bytes 1572872 | tf_op jit(solution)/shard_map/ppermute | solution.py:219
  46.9 8.7 %collective-permute-start.3 = (bf16[512,256]{1,0:T(8,128)(2,1)S(1)}, bf16[512,256]{1,0:T(8,128)(2,1)S(1)}, u32[]{:S(2)}, u32[]{:S(2)}) collective-permute-start(bf16[512,256]{1,0:T(8,128)(2,1)S(1)} %slice.25), channel_id=1, source_target_pairs={{0,24},{8,0},{16,8},{24,16},{1,25},{9,1},{17,9},{25,17},{2,26},{10... | collective-permute-start | bytes 786440 | tf_op jit(solution)/shard_map/ppermute | solution.py:224
  51.4 8.5 %collective-permute-start.2 = (bf16[512,256]{1,0:T(8,128)(2,1)}, bf16[512,256]{1,0:T(8,128)(2,1)S(1)}, u32[]{:S(2)}, u32[]{:S(2)}) collective-permute-start(bf16[512,256]{1,0:T(8,128)(2,1)} %slice.24), channel_id=1, source_target_pairs={{0,8},{8,16},{16,24},{24,0},{1,9},{9,17},{17,25},{25,1},{2,10},{10... | collective-permute-start | bytes 786440 | tf_op jit(solution)/shard_map/ppermute | solution.py:223
  59.9 0.7 copy-start
  60.6 0.7 copy-start.2
  61.3 0.9 copy-start.1
  85.7 0.8 copy-start.3
  86.5 0.8 copy-start.5
  87.3 0.8 copy-start.7
  88.1 7.7 %copy-start.8 = (bf16[1024,256]{1,0:T(8,128)(2,1)S(1)}, bf16[1024,256]{1,0:T(8,128)(2,1)}, u32[]{:S(2)}) copy-start(bf16[1024,256]{1,0:T(8,128)(2,1)} %copy-done.7) | copy-start | bytes 1572868
  89.1 6.8 %copy-start.6 = (bf16[1024,256]{1,0:T(8,128)(2,1)S(1)}, bf16[1024,256]{1,0:T(8,128)(2,1)}, u32[]{:S(2)}) copy-start(bf16[1024,256]{1,0:T(8,128)(2,1)} %copy-done.5) | copy-start | bytes 1572868
  89.1 10.5 %copy-start.4 = (bf16[1024,256]{1,0:T(8,128)(2,1)S(1)}, bf16[1024,256]{1,0:T(8,128)(2,1)}, u32[]{:S(2)}) copy-start(bf16[1024,256]{1,0:T(8,128)(2,1)} %copy-done.3) | copy-start | bytes 1572868
  89.1 35.5 %all-to-all-start.2 = ((bf16[8,128,256]{1,2,0:T(8,128)(2,1)}), bf16[8,128,256]{1,2,0:T(8,128)(2,1)S(1)}, u32[]{:S(2)}, u32[]{:S(2)}) async-start(bf16[8,128,256]{1,2,0:T(8,128)(2,1)} %copy.33), calls=%async_computation.2 | async-start | bytes 1048576 | tf_op jit(solution)/shard_map/all_to_all | solution.py:213
  95.8 23.2 %collective-permute-start.4 = (bf16[1024,256]{1,0:T(8,128)(2,1)S(1)}, bf16[1024,256]{1,0:T(8,128)(2,1)S(1)}, u32[]{:S(2)}, u32[]{:S(2)}) collective-permute-start(bf16[1024,256]{1,0:T(8,128)(2,1)S(1)} %copy-done.8), channel_id=1, source_target_pairs={{0,24},{8,0},{16,8},{24,16},{1,25},{9,1},{17,9},{25,17},{2,26},{10... | collective-permute-start | bytes 1572872 | tf_op jit(solution)/shard_map/ppermute | solution.py:229
  95.9 23.1 %collective-permute-start.5 = (bf16[1024,256]{1,0:T(8,128)(2,1)S(1)}, bf16[1024,256]{1,0:T(8,128)(2,1)S(1)}, u32[]{:S(2)}, u32[]{:S(2)}) collective-permute-start(bf16[1024,256]{1,0:T(8,128)(2,1)S(1)} %copy-done.6), channel_id=1, source_target_pairs={{0,16},{8,24},{16,0},{24,8},{1,17},{9,25},{17,1},{25,9},{2,18},{10... | collective-permute-start | bytes 1572872 | tf_op jit(solution)/shard_map/ppermute | solution.py:231
  99.7 23.8 %collective-permute-start.6 = (bf16[1024,256]{1,0:T(8,128)(2,1)S(1)}, bf16[1024,256]{1,0:T(8,128)(2,1)S(1)}, u32[]{:S(2)}, u32[]{:S(2)}) collective-permute-start(bf16[1024,256]{1,0:T(8,128)(2,1)S(1)} %copy-done.4), channel_id=1, source_target_pairs={{0,8},{8,16},{16,24},{24,0},{1,9},{9,17},{17,25},{25,1},{2,10},{10... | collective-permute-start | bytes 1572872 | tf_op jit(solution)/shard_map/ppermute | solution.py:230
  124.7 24.5 %all-to-all-start.3 = ((bf16[8,128,256]{1,2,0:T(8,128)(2,1)}), bf16[8,128,256]{1,2,0:T(8,128)(2,1)S(1)}, u32[]{:S(2)}, u32[]{:S(2)}) async-start(bf16[8,128,256]{1,2,0:T(8,128)(2,1)} %copy.34), calls=%async_computation.3 | async-start | bytes 1048576 | tf_op jit(solution)/shard_map/all_to_all | solution.py:213

commit v2 on v1

v2 whole, which is shorter than its diff:
```python
import math

import jax
import jax.numpy as jnp
import numpy as np
from jax import lax
from jax.experimental import pallas as pl
from jax.experimental.pallas import tpu as pltpu
from jax.sharding import Mesh
from jax.sharding import PartitionSpec as P

DH = 128
BLK = 64
SCALE = 1.0 / math.sqrt(DH)
SCALE2 = SCALE * math.log2(math.e)
GROUP = 8
ROWS = GROUP * BLK
WIDE = 2048
F32 = jnp.float32
BF16 = jnp.bfloat16


def mm(a, b):
    return jnp.dot(a, b, preferred_element_type=F32)


def mm_nt(a, b):
    return lax.dot_general(a, b, (((1,), (1,)), ((), ())), preferred_element_type=F32)


def attention_kernel(
    nz, nx, order, me, qg, kv0, kv1, kv3, kv2a, kv2b,
    oq, o0, o1a, o1b, o2a, o2b, o3a, o3b,
    ks, vs, qs, gs, scr, dkt, dvt, qacc, oacc, rowpos, sblk, spos,
):
    x = me[0]
    per_part = 2 * nz
    half = per_part // 2

    def block_of(part, j):
        src = lax.rem(x - part + nx, nx)
        return order[((j // 2) * nx + src) * 2 + j % 2]

    def block_rows(p):
        return pl.ds(pl.multiple_of(p * BLK, BLK), BLK)

    def part_ref(full, a, b, j):
        if full is not None:
            return full, j * BLK
        return (a, j * BLK) if j < half else (b, (j - half) * BLK)

    for part in range(nx):
        for j in range(per_part):
            ref, start = part_ref((kv0, kv1, None, kv3)[part], kv2a, kv2b, j)
            at = block_rows(block_of(part, j))
            ks[at, :] = ref[start:start + BLK, :DH]
            vs[at, :] = ref[start:start + BLK, DH:]

    own = [block_of(0, j) for j in range(per_part)]
    for j in range(per_part):
        rank = jnp.int32(0)
        for i in range(per_part):
            if i != j:
                rank = rank + (own[i] < own[j]).astype(jnp.int32)
        sblk[rank] = jnp.int32(j)
        spos[rank] = own[j]
        at = block_rows(rank)
        qs[at, :] = qg[j * BLK:(j + 1) * BLK, :DH]
        gs[at, :] = qg[j * BLK:(j + 1) * BLK, DH:]

    dkt[...] = jnp.zeros_like(dkt)
    dvt[...] = jnp.zeros_like(dvt)

    def chunk(c):
        return pl.ds(pl.multiple_of(c * WIDE, WIDE), WIDE)

    def fold(op, s):
        r = s[:, :DH]
        for i in range(1, WIDE // DH):
            r = op(r, s[:, i * DH:(i + 1) * DH])
        return r

    def group_step(g, carry):
        base = g * GROUP
        count = ((spos[base + GROUP - 1] + 1) * BLK + WIDE - 1) // WIDE
        for k in range(GROUP):
            within = lax.broadcasted_iota(jnp.int32, (BLK, DH), 0)
            rowpos[k * BLK:(k + 1) * BLK, :] = within + spos[base + k] * BLK
        at = pl.ds(pl.multiple_of(base * BLK, ROWS), ROWS)
        q = qs[at, :]
        gr = gs[at, :]
        q_t = q.T
        g_t = gr.T

        def score_step(c, m):
            s = mm_nt(q, ks[chunk(c), :])
            key = lax.broadcasted_iota(jnp.int32, (ROWS, WIDE), 1) + c * WIDE
            s = jnp.where(key <= rowpos[:, :1], s, F32(-1e30))
            scr[:, chunk(c)] = s
            return jnp.maximum(m, fold(jnp.maximum, s))

        m = lax.fori_loop(0, count, score_step, jnp.full((ROWS, DH), -1e30, F32))
        top = jnp.max(m, axis=1, keepdims=True)
        oacc[...] = jnp.zeros_like(oacc)

        def expo_step(c, tot):
            e = jnp.exp2((scr[:, chunk(c)] - top) * F32(SCALE2))
            scr[:, chunk(c)] = e
            oacc[...] += mm(e.astype(BF16), vs[chunk(c), :])
            return tot + fold(jnp.add, e)

        tot = lax.fori_loop(0, count, expo_step, jnp.zeros((ROWS, DH), F32))
        total = jnp.sum(tot, axis=1, keepdims=True)
        inv = 1.0 / total
        att = (oacc[...] / total).astype(BF16)
        dsum = jnp.sum(gr.astype(F32) * att.astype(F32), axis=1, keepdims=True)
        qacc[...] = jnp.zeros_like(qacc)

        def back_step(c, carry):
            dp = mm_nt(gr, vs[chunk(c), :])
            p = scr[:, chunk(c)] * inv
            ds = (p * (dp - dsum)).astype(BF16)
            qacc[...] += mm(ds, ks[chunk(c), :])
            dkt[:, chunk(c)] += mm(q_t, ds)
            dvt[:, chunk(c)] += mm(g_t, p.astype(BF16))
            return carry

        lax.fori_loop(0, count, back_step, 0)
        dq = (qacc[...] * F32(SCALE)).astype(BF16)
        for k in range(GROUP):
            to = block_rows(sblk[base + k])
            oq[to, :DH] = att[k * BLK:(k + 1) * BLK, :]
            oq[to, DH:] = dq[k * BLK:(k + 1) * BLK, :]
        return carry

    lax.fori_loop(0, per_part // GROUP, group_step, 0)

    for t in range(ks.shape[0] // DH):
        at = slice(t * DH, (t + 1) * DH)
        ks[at, :] = (dkt[:, at] * F32(SCALE)).T.astype(BF16)
        vs[at, :] = dvt[:, at].T.astype(BF16)

    halves = ((None, None), (o1a, o1b), (o2a, o2b), (o3a, o3b))
    for part in range(nx):
        for j in range(per_part):
            ref, start = part_ref(o0 if part == 0 else None, *halves[part], j)
            at = block_rows(block_of(part, j))
            ref[start:start + BLK, :DH] = ks[at, :]
            ref[start:start + BLK, DH:] = vs[at, :]


def attention(nz, nx, order, me, qg, parts):
    rows = qg.shape[0]
    seq = rows * nx
    vm = pl.BlockSpec(memory_space=pltpu.VMEM)
    sm = pl.BlockSpec(memory_space=pltpu.SMEM)
    whole = jax.ShapeDtypeStruct((rows, 2 * DH), BF16)
    half = jax.ShapeDtypeStruct((rows // 2, 2 * DH), BF16)
    return pl.pallas_call(
        lambda *refs: attention_kernel(nz, nx, *refs),
        out_shape=(whole,) * 2 + (half,) * 6,
        in_specs=[sm, sm] + [vm] * 6,
        out_specs=(vm,) * 8,
        scratch_shapes=[
            pltpu.VMEM((seq, DH), BF16),
            pltpu.VMEM((seq, DH), BF16),
            pltpu.VMEM((rows, DH), BF16),
            pltpu.VMEM((rows, DH), BF16),
            pltpu.VMEM((ROWS, seq), F32),
            pltpu.VMEM((DH, seq), F32),
            pltpu.VMEM((DH, seq), F32),
            pltpu.VMEM((ROWS, DH), F32),
            pltpu.VMEM((ROWS, DH), F32),
            pltpu.VMEM((ROWS, DH), jnp.int32),
            pltpu.SMEM((rows // BLK,), jnp.int32),
            pltpu.SMEM((rows // BLK,), jnp.int32),
        ],
        compiler_params=pltpu.CompilerParams(vmem_limit_bytes=48 * 2**20),
        name="attention",
    )(order, me, qg, *parts)


def run_copies(copies, sems):
    started = [pltpu.make_async_copy(src, dst, sems.at[i]) for i, (src, dst) in enumerate(copies)]
    for copy in started:
        copy.start()
    for copy in started:
        copy.wait()


def by_head(a, b, slots):
    rows, width = a.shape
    heads = width // DH

    def kernel(a_ref, b_ref, out, sems):
        copies = []
        for slot in range(slots):
            cols = slice((slot % heads) * DH, (slot % heads + 1) * DH)
            copies.append((a_ref.at[:, cols], out.at[slot, :, :DH]))
            copies.append((b_ref.at[:, cols], out.at[slot, :, DH:]))
        run_copies(copies, sems)

    anywhere = pl.BlockSpec(memory_space=pl.ANY)
    return pl.pallas_call(
        kernel,
        out_shape=jax.ShapeDtypeStruct((slots, rows, 2 * DH), BF16),
        in_specs=[anywhere, anywhere],
        out_specs=anywhere,
        scratch_shapes=[pltpu.SemaphoreType.DMA((2 * slots,))],
        name="by_head",
    )(a, b)


def from_heads(stacked, heads):
    rows = stacked.shape[1]

    def kernel(stack, a_ref, b_ref, sems):
        copies = []
        for head in range(heads):
            cols = slice(head * DH, (head + 1) * DH)
            copies.append((stack.at[head, :, :DH], a_ref.at[:, cols]))
            copies.append((stack.at[head, :, DH:], b_ref.at[:, cols]))
        run_copies(copies, sems)

    anywhere = pl.BlockSpec(memory_space=pl.ANY)
    out = jax.ShapeDtypeStruct((rows, heads * DH), BF16)
    return pl.pallas_call(
        kernel,
        out_shape=(out, out),
        in_specs=[anywhere],
        out_specs=(anywhere, anywhere),
        scratch_shapes=[pltpu.SemaphoreType.DMA((2 * heads,))],
        name="from_heads",
    )(stacked)


def make_shards(nz, nx):
    def to(step):
        return [(i, (i + step) % nx) for i in range(nx)]

    def exchange(v):
        return lax.all_to_all(v, "z", 0, 0, tiled=True)

    def shards(queries, keys, values, out_grad, block_order):
        rows, width = queries.shape[1:]
        heads = width // DH
        kv = exchange(by_head(keys[0], values[0], nz)).reshape(nz * rows, 2 * DH)
        right = lax.ppermute(kv, "x", to(1))
        left = lax.ppermute(kv, "x", to(-1))
        qg = exchange(by_head(queries[0], out_grad[0], nz)).reshape(nz * rows, 2 * DH)
        cut = nz * rows // 2
        far_a = lax.ppermute(right[:cut], "x", to(1))
        far_b = lax.ppermute(left[cut:], "x", to(-1))
        me = lax.axis_index("x").astype(jnp.int32).reshape(1)
        oq, o0, o1a, o1b, o2a, o2b, o3a, o3b = attention(
            nz, nx, block_order[0], me, qg, (kv, right, left, far_a, far_b)
        )
        via_right = lax.ppermute(o2a, "x", to(1))
        via_left = lax.ppermute(o2b, "x", to(-1))
        r3b = lax.ppermute(o3b, "x", to(1))
        r1a = lax.ppermute(o1a, "x", to(-1))
        r3a = lax.ppermute(o3a + via_right, "x", to(1))
        r1b = lax.ppermute(o1b + via_left, "x", to(-1))
        att, q_grad = from_heads(exchange(oq.reshape(nz, rows, 2 * DH)), heads)
        total_a = (o0[:cut].astype(F32) + r1a.astype(F32) + r3a.astype(F32)).astype(BF16)
        total_b = (o0[cut:].astype(F32) + r1b.astype(F32) + r3b.astype(F32)).astype(BF16)
        total = jnp.concatenate([total_a, total_b], axis=0)
        k_grad, v_grad = from_heads(exchange(total.reshape(nz, rows, 2 * DH)), heads)
        return att[None], q_grad[None], k_grad[None], v_grad[None]

    return shards


def solution(mesh):
    sizes = dict(mesh.shape)
    nx = 4
    nz = sizes["pb"] // nx
    fine = Mesh(
        np.asarray(mesh.devices).reshape(nz, nx, sizes["kv"], sizes["ha"]), ("z", "x", "kv", "ha")
    )
    split = P("kv", ("z", "x"), "ha")
    return jax.shard_map(
        make_shards(nz, nx),
        mesh=fine,
        in_specs=(split, split, split, split, P("kv", None)),
        out_specs=(split,) * 4,
        check_vma=False,
    )
```

time: 153 us -> 156 us (1.020); the launches traced: 151 us -> 157 us
  Pallas kernels: 23.4 us -> 75.6 us
  waiting for transfers between devices: 73.6 us -> 30.7 us
  local copies, waits for them, and re-layouts: 15.4 us -> 5.42 us
  starting transfers between devices: 37.3 us -> 43.1 us
    pallas_call x0 -> x4, Pallas kernels: none -> 60.5 us  [the longest x2 34.3 us: by_head(): pl.pallas_call(kernel, out_shape=jax.ShapeDtypeStruct((slots, rows, 2 * D...]
    all_to_all x4, waiting for transfers between devices: 31.5 us -> 4.22 us  [exchange(): return lax.all_to_all(v, 'z', 0, 0, tiled=True)]
    ppermute x3 -> x6, waiting for transfers between devices: 22.4 us -> 8.6 us  [the longest x1 3.68 us: shards(): r1a = lax.ppermute(o1a, 'x', to(-1))]
    pallas_call x1, Pallas kernels: 23.4 us -> 15.1 us  [attention(): pl.pallas_call(lambda *refs: attention_kernel(nz, nx, *refs), out_shape=(...]
    unnamed x32 -> x18, local copies, waits for them, and re-layouts: 10.4 us -> 5.39 us
    ppermute x3 -> x6, starting transfers between devices: 5.15 us -> 8.9 us  [the longest x1 2.31 us: shards(): via_right = lax.ppermute(o2a, 'x', to(1))]
    reshape x2 -> x0, local copies, waits for them, and re-layouts: 2.03 us -> none  [the longest x1 1.02 us: shards(): att, q_grad = from_heads(exchange(oq.reshape(nz, rows, 2 * DH)), heads)]
    all_to_all x4, starting transfers between devices: 25.6 us -> 27.6 us  [exchange(): return lax.all_to_all(v, 'z', 0, 0, tiled=True)]
  transfers between devices with their start and end apart: 11 -> 14, of which waited for: 7 -> 9; matrix products, arithmetic and copies ran while one was open for 4% -> 1% of each run, Pallas kernels for 0% -> 19%
where the time goes in v2:
time: 156 us; the launch traced here: 157 us
  Pallas kernels  75.6 us (48%)
  starting transfers between devices  43.1 us (28%)
  waiting for transfers between devices  30.7 us (20%)
  local copies, waits for them, and re-layouts  5.42 us (3%)
    pallas_call x2, Pallas kernels, by_head(): pl.pallas_call(kernel, out_shape=jax.ShapeDtypeStruct((slots, rows, 2 * D...  34.3 us
    all_to_all x4, starting transfers between devices, exchange(): return lax.all_to_all(v, 'z', 0, 0, tiled=True)  27.6 us
    pallas_call x2, Pallas kernels, from_heads(): pl.pallas_call(kernel, out_shape=(out, out), in_specs=[anywhere], out_spe...  26.2 us
    pallas_call x1, Pallas kernels, attention(): pl.pallas_call(lambda *refs: attention_kernel(nz, nx, *refs), out_shape=(...  15.1 us
    ppermute x1, waiting for transfers between devices, shards(): left = lax.ppermute(kv, 'x', to(-1))  10.3 us
    unnamed x18, local copies, waits for them, and re-layouts  5.39 us
    all_to_all x4, waiting for transfers between devices, exchange(): return lax.all_to_all(v, 'z', 0, 0, tiled=True)  4.22 us
    ppermute x1, waiting for transfers between devices, shards(): far_a = lax.ppermute(right[:cut], 'x', to(1))  3.79 us
  transfers between devices with their start and end apart: 14, of which 9 were waited for; matrix products, arithmetic and copies ran while one was open for 1% of the time, Pallas kernels for 19%

profile of v2, /device:TPU:8, one launch (start us, length us, event | category | flops | bytes accessed | tf_op | source)
XLA Modules:
  0.0 156.8 jit_solution(3230882904876921266)
XLA Ops:
  0.6 17.1 %by_head.3 = bf16[8,128,256]{2,1,0:T(8,128)(2,1)} custom-call(bf16[128,768]{1,0:T(8,128)(2,1)} %bitcast.19, bf16[128,768]{1,0:T(8,128)(2,1)} %bitcast.20), custom_call_target="tpu_custom_call" | custom-call | tf_op jit(solution)/shard_map/by_head/pallas_call | solution.py:204
  17.8 8.5 %all-to-all-start.1 = ((bf16[8,128,256]{2,1,0:T(8,128)(2,1)}), bf16[8,128,256]{2,1,0:T(8,128)(2,1)S(1)}, u32[]{:S(2)}, u32[]{:S(2)}) async-start(bf16[8,128,256]{2,1,0:T(8,128)(2,1)} %by_head.3), calls=%async_computation.1 | async-start | bytes 1048576 | tf_op jit(solution)/shard_map/all_to_all | solution.py:242
  26.2 17.1 %by_head.2 = bf16[8,128,256]{2,1,0:T(8,128)(2,1)} custom-call(bf16[128,768]{1,0:T(8,128)(2,1)} %bitcast.21, bf16[128,768]{1,0:T(8,128)(2,1)} %bitcast.22), custom_call_target="tpu_custom_call" | custom-call | tf_op jit(solution)/shard_map/by_head/pallas_call | solution.py:204
  43.7 6.9 %all-to-all-start = ((bf16[8,128,256]{2,1,0:T(8,128)(2,1)}), bf16[8,128,256]{2,1,0:T(8,128)(2,1)S(1)}, u32[]{:S(2)}, u32[]{:S(2)}) async-start(bf16[8,128,256]{2,1,0:T(8,128)(2,1)} %by_head.2), calls=%async_computation | async-start | bytes 1048576 | tf_op jit(solution)/shard_map/all_to_all | solution.py:242
  50.6 2.8 %collective-permute-start.1 = (bf16[1024,256]{1,0:T(8,128)(2,1)S(1)}, bf16[1024,256]{1,0:T(8,128)(2,1)S(1)}, u32[]{:S(2)}, u32[]{:S(2)}) collective-permute-start(bf16[1024,256]{1,0:T(8,128)(2,1)S(1)} %bitcast.14), channel_id=1, source_target_pairs={{0,24},{8,0},{16,8},{24,16},{1,25},{9,1},{17,9},{25,17},{2,26},{10... | collective-permute-start | bytes 1572872 | tf_op jit(solution)/shard_map/ppermute | solution.py:249
  53.4 10.3 %collective-permute-done.1.refs_5_ = bf16[1024,256]{1,0:T(8,128)(2,1)S(1)} collective-permute-done((bf16[1024,256]{1,0:T(8,128)(2,1)S(1)}, bf16[1024,256]{1,0:T(8,128)(2,1)S(1)}, u32[]{:S(2)}, u32[]{:S(2)}) %collective-permute-start.1) | collective-permute-done | bytes 524320 | tf_op jit(solution)/shard_map/ppermute | solution.py:249
  63.7 3.8 %collective-permute-start.3 = (bf16[512,256]{1,0:T(8,128)(2,1)S(1)}, bf16[512,256]{1,0:T(8,128)(2,1)S(1)}, u32[]{:S(2)}, u32[]{:S(2)}) collective-permute-start(bf16[512,256]{1,0:T(8,128)(2,1)S(1)} %slice.17), channel_id=1, source_target_pairs={{0,24},{8,0},{16,8},{24,16},{1,25},{9,1},{17,9},{25,17},{2,26},{10... | collective-permute-start | bytes 786440 | tf_op jit(solution)/shard_map/ppermute | solution.py:253
  67.6 3.8 %collective-permute-done.3.refs_7_ = bf16[512,256]{1,0:T(8,128)(2,1)S(1)} collective-permute-done((bf16[512,256]{1,0:T(8,128)(2,1)S(1)}, bf16[512,256]{1,0:T(8,128)(2,1)S(1)}, u32[]{:S(2)}, u32[]{:S(2)}) %collective-permute-start.3) | collective-permute-done | bytes 262176 | tf_op jit(solution)/shard_map/ppermute | solution.py:253
  71.4 3.8 %collective-permute-done.2.refs_6_ = bf16[512,256]{1,0:T(8,128)(2,1)S(1)} collective-permute-done((bf16[512,256]{1,0:T(8,128)(2,1)S(1)}, bf16[512,256]{1,0:T(8,128)(2,1)S(1)}, u32[]{:S(2)}, u32[]{:S(2)}) %collective-permute-start.2) | collective-permute-done | bytes 262176 | tf_op jit(solution)/shard_map/ppermute | solution.py:252
  76.5 0.9 copy-done.1
  77.5 15.1 %attention.1 = (bf16[1024,256]{1,0:T(8,128)(2,1)}, bf16[1024,256]{1,0:T(8,128)(2,1)S(1)}, bf16[512,256]{1,0:T(8,128)(2,1)S(1)}, bf16[512,256]{1,0:T(8,128)(2,1)S...) custom-call(s32[64]{0:T(128)S(1)} %bitcast.18, ...), custom_call_target="tpu_custom_call" | custom-call | tf_op jit(solution)/shard_map/attention/pallas_call | solution.py:159
  94.0 2.3 %collective-permute-start.5 = (bf16[512,256]{1,0:T(8,128)(2,1)}, bf16[512,256]{1,0:T(8,128)(2,1)S(1)}, u32[]{:S(2)}, u32[]{:S(2)}) collective-permute-start(bf16[512,256]{1,0:T(8,128)(2,1)} %get-tuple-element.22), channel_id=1, source_target_pairs={{0,8},{8,16},{16,24},{24,0},{1,9},{9,17},{17,25},{25,1},{2,10},{10... | collective-permute-start | bytes 786440 | tf_op jit(solution)/shard_map/ppermute | solution.py:258
  97.2 7.1 %all-to-all-start.2 = ((bf16[8,128,256]{2,1,0:T(8,128)(2,1)}), bf16[8,128,256]{2,1,0:T(8,128)(2,1)S(1)}, u32[]{:S(2)}, u32[]{:S(2)}) async-start(bf16[8,128,256]{2,1,0:T(8,128)(2,1)} %bitcast.8), calls=%async_computation.2 | async-start | bytes 1048576 | tf_op jit(solution)/shard_map/all_to_all | solution.py:242
  104.6 2.0 %collective-permute-start.9 = (bf16[512,256]{1,0:T(8,128)(2,1)S(1)}, bf16[512,256]{1,0:T(8,128)(2,1)S(1)}, u32[]{:S(2)}, u32[]{:S(2)}) collective-permute-start(bf16[512,256]{1,0:T(8,128)(2,1)S(1)} %copy-done.4), channel_id=1, source_target_pairs={{0,8},{8,16},{16,24},{24,0},{1,9},{9,17},{17,25},{25,1},{2,10},{10... | collective-permute-start | bytes 786440 | tf_op jit(solution)/shard_map/ppermute | solution.py:260
  106.7 1.2 collective-permute-start.6
  107.9 2.2 %collective-permute-start.8 = (bf16[512,256]{1,0:T(8,128)(2,1)S(1)}, bf16[512,256]{1,0:T(8,128)(2,1)S(1)}, u32[]{:S(2)}, u32[]{:S(2)}) collective-permute-start(bf16[512,256]{1,0:T(8,128)(2,1)S(1)} %add.21), channel_id=1, source_target_pairs={{0,24},{8,0},{16,8},{24,16},{1,25},{9,1},{17,9},{25,17},{2,26},{10... | collective-permute-start | bytes 786440 | tf_op jit(solution)/shard_map/ppermute | solution.py:263
  110.1 3.7 %collective-permute-done.4 = bf16[512,256]{1,0:T(8,128)(2,1)S(1)} collective-permute-done((bf16[512,256]{1,0:T(8,128)(2,1)S(1)}, bf16[512,256]{1,0:T(8,128)(2,1)S(1)}, u32[]{:S(2)}, u32[]{:S(2)}) %collective-permute-start.4) | collective-permute-done | bytes 262176 | tf_op jit(solution)/shard_map/ppermute | solution.py:261
  113.8 1.3 collective-permute-done.9
  115.1 3.6 %collective-permute-done.6 = bf16[512,256]{1,0:T(8,128)(2,1)S(1)} collective-permute-done((bf16[512,256]{1,0:T(8,128)(2,1)S(1)}, bf16[512,256]{1,0:T(8,128)(2,1)S(1)}, u32[]{:S(2)}, u32[]{:S(2)}) %collective-permute-start.6) | collective-permute-done | bytes 262176 | tf_op jit(solution)/shard_map/ppermute | solution.py:262
  119.8 1.5 all-to-all-done.2.stack
  122.1 5.2 %all-to-all-start.3 = ((bf16[8,128,256]{2,1,0:T(8,128)(2,1)}), bf16[8,128,256]{2,1,0:T(8,128)(2,1)S(1)}, u32[]{:S(2)}, u32[]{:S(2)}) async-start(bf16[8,128,256]{2,1,0:T(8,128)(2,1)} %bitcast.11), calls=%async_computation.3 | async-start | bytes 1048576 | tf_op jit(solution)/shard_map/all_to_all | solution.py:242
  127.2 13.1 %from_heads.2 = (bf16[128,768]{1,0:T(8,128)(2,1)}, bf16[128,768]{1,0:T(8,128)(2,1)}) custom-call(bf16[8,128,256]{2,1,0:T(8,128)(2,1)} %copy-done.7), custom_call_target="tpu_custom_call" | custom-call | tf_op jit(solution)/shard_map/from_heads/pallas_call | solution.py:227
  140.4 2.4 %all-to-all-done.3.stack = bf16[8,128,256]{2,1,0:T(8,128)(2,1)S(1)} async-done(((bf16[8,128,256]{2,1,0:T(8,128)(2,1)}), bf16[8,128,256]{2,1,0:T(8,128)(2,1)S(1)}, u32[]{:S(2)}, u32[]{:S(2)}) %all-to-all-start.3) | async-done | bytes 524320 | tf_op jit(solution)/shard_map/all_to_all | solution.py:242
  143.5 13.1 %from_heads.3 = (bf16[128,768]{1,0:T(8,128)(2,1)}, bf16[128,768]{1,0:T(8,128)(2,1)}) custom-call(bf16[8,128,256]{2,1,0:T(8,128)(2,1)} %copy-done.8), custom_call_target="tpu_custom_call" | custom-call | tf_op jit(solution)/shard_map/from_heads/pallas_call | solution.py:227
  (33 shorter events, 7.3 us)
Async XLA Ops:
  17.8 26.0 %all-to-all-start.1 = ((bf16[8,128,256]{2,1,0:T(8,128)(2,1)}), bf16[8,128,256]{2,1,0:T(8,128)(2,1)S(1)}, u32[]{:S(2)}, u32[]{:S(2)}) async-start(bf16[8,128,256]{2,1,0:T(8,128)(2,1)} %by_head.3), calls=%async_computation.1 | async-start | bytes 1048576 | tf_op jit(solution)/shard_map/all_to_all | solution.py:242
  43.7 23.9 %all-to-all-start = ((bf16[8,128,256]{2,1,0:T(8,128)(2,1)}), bf16[8,128,256]{2,1,0:T(8,128)(2,1)S(1)}, u32[]{:S(2)}, u32[]{:S(2)}) async-start(bf16[8,128,256]{2,1,0:T(8,128)(2,1)} %by_head.2), calls=%async_computation | async-start | bytes 1048576 | tf_op jit(solution)/shard_map/all_to_all | solution.py:242
  50.6 13.1 %collective-permute-start.1 = (bf16[1024,256]{1,0:T(8,128)(2,1)S(1)}, bf16[1024,256]{1,0:T(8,128)(2,1)S(1)}, u32[]{:S(2)}, u32[]{:S(2)}) collective-permute-start(bf16[1024,256]{1,0:T(8,128)(2,1)S(1)} %bitcast.14), channel_id=1, source_target_pairs={{0,24},{8,0},{16,8},{24,16},{1,25},{9,1},{17,9},{25,17},{2,26},{10... | collective-permute-start | bytes 1572872 | tf_op jit(solution)/shard_map/ppermute | solution.py:249
  53.4 14.1 %collective-permute-start = (bf16[1024,256]{1,0:T(8,128)(2,1)S(1)}, bf16[1024,256]{1,0:T(8,128)(2,1)S(1)}, u32[]{:S(2)}, u32[]{:S(2)}) collective-permute-start(bf16[1024,256]{1,0:T(8,128)(2,1)S(1)} %bitcast.15), channel_id=1, source_target_pairs={{0,8},{8,16},{16,24},{24,0},{1,9},{9,17},{17,25},{25,1},{2,10},{10... | collective-permute-start | bytes 1572872 | tf_op jit(solution)/shard_map/ppermute | solution.py:248
  63.7 7.7 %collective-permute-start.3 = (bf16[512,256]{1,0:T(8,128)(2,1)S(1)}, bf16[512,256]{1,0:T(8,128)(2,1)S(1)}, u32[]{:S(2)}, u32[]{:S(2)}) collective-permute-start(bf16[512,256]{1,0:T(8,128)(2,1)S(1)} %slice.17), channel_id=1, source_target_pairs={{0,24},{8,0},{16,8},{24,16},{1,25},{9,1},{17,9},{25,17},{2,26},{10... | collective-permute-start | bytes 786440 | tf_op jit(solution)/shard_map/ppermute | solution.py:253
  67.5 7.7 %collective-permute-start.2 = (bf16[512,256]{1,0:T(8,128)(2,1)S(1)}, bf16[512,256]{1,0:T(8,128)(2,1)S(1)}, u32[]{:S(2)}, u32[]{:S(2)}) collective-permute-start(bf16[512,256]{1,0:T(8,128)(2,1)S(1)} %slice.16), channel_id=1, source_target_pairs={{0,8},{8,16},{16,24},{24,0},{1,9},{9,17},{17,25},{25,1},{2,10},{10... | collective-permute-start | bytes 786440 | tf_op jit(solution)/shard_map/ppermute | solution.py:252
  75.2 0.7 copy-start
  75.9 0.7 copy-start.2
  76.5 0.9 copy-start.1
  92.6 0.7 copy-start.3
  93.3 0.7 copy-start.5
  94.0 12.6 %collective-permute-start.5 = (bf16[512,256]{1,0:T(8,128)(2,1)}, bf16[512,256]{1,0:T(8,128)(2,1)S(1)}, u32[]{:S(2)}, u32[]{:S(2)}) collective-permute-start(bf16[512,256]{1,0:T(8,128)(2,1)} %get-tuple-element.22), channel_id=1, source_target_pairs={{0,8},{8,16},{16,24},{24,0},{1,9},{9,17},{17,25},{25,1},{2,10},{10... | collective-permute-start | bytes 786440 | tf_op jit(solution)/shard_map/ppermute | solution.py:258
  96.3 11.5 %collective-permute-start.7 = (bf16[512,256]{1,0:T(8,128)(2,1)}, bf16[512,256]{1,0:T(8,128)(2,1)S(1)}, u32[]{:S(2)}, u32[]{:S(2)}) collective-permute-start(bf16[512,256]{1,0:T(8,128)(2,1)} %get-tuple-element.24), channel_id=1, source_target_pairs={{0,24},{8,0},{16,8},{24,16},{1,25},{9,1},{17,9},{25,17},{2,26},{10... | collective-permute-start | bytes 786440 | tf_op jit(solution)/shard_map/ppermute | solution.py:259
  97.2 7.1 %copy-start.6 = (bf16[512,256]{1,0:T(8,128)(2,1)S(1)}, bf16[512,256]{1,0:T(8,128)(2,1)}, u32[]{:S(2)}) copy-start(bf16[512,256]{1,0:T(8,128)(2,1)} %copy-done.5) | copy-start | bytes 786436
  97.2 7.3 %copy-start.4 = (bf16[512,256]{1,0:T(8,128)(2,1)S(1)}, bf16[512,256]{1,0:T(8,128)(2,1)}, u32[]{:S(2)}) copy-start(bf16[512,256]{1,0:T(8,128)(2,1)} %copy-done.3) | copy-start | bytes 786436
  97.2 24.0 %all-to-all-start.2 = ((bf16[8,128,256]{2,1,0:T(8,128)(2,1)}), bf16[8,128,256]{2,1,0:T(8,128)(2,1)S(1)}, u32[]{:S(2)}, u32[]{:S(2)}) async-start(bf16[8,128,256]{2,1,0:T(8,128)(2,1)} %bitcast.8), calls=%async_computation.2 | async-start | bytes 1048576 | tf_op jit(solution)/shard_map/all_to_all | solution.py:242
  104.3 9.5 %collective-permute-start.4 = (bf16[512,256]{1,0:T(8,128)(2,1)S(1)}, bf16[512,256]{1,0:T(8,128)(2,1)S(1)}, u32[]{:S(2)}, u32[]{:S(2)}) collective-permute-start(bf16[512,256]{1,0:T(8,128)(2,1)S(1)} %copy-done.6), channel_id=1, source_target_pairs={{0,24},{8,0},{16,8},{24,16},{1,25},{9,1},{17,9},{25,17},{2,26},{10... | collective-permute-start | bytes 786440 | tf_op jit(solution)/shard_map/ppermute | solution.py:261
  104.6 10.5 %collective-permute-start.9 = (bf16[512,256]{1,0:T(8,128)(2,1)S(1)}, bf16[512,256]{1,0:T(8,128)(2,1)S(1)}, u32[]{:S(2)}, u32[]{:S(2)}) collective-permute-start(bf16[512,256]{1,0:T(8,128)(2,1)S(1)} %copy-done.4), channel_id=1, source_target_pairs={{0,8},{8,16},{16,24},{24,0},{1,9},{9,17},{17,25},{25,1},{2,10},{10... | collective-permute-start | bytes 786440 | tf_op jit(solution)/shard_map/ppermute | solution.py:260
  106.7 12.1 %collective-permute-start.6 = (bf16[512,256]{1,0:T(8,128)(2,1)S(1)}, bf16[512,256]{1,0:T(8,128)(2,1)S(1)}, u32[]{:S(2)}, u32[]{:S(2)}) collective-permute-start(bf16[512,256]{1,0:T(8,128)(2,1)S(1)} %add.19), channel_id=1, source_target_pairs={{0,8},{8,16},{16,24},{24,0},{1,9},{9,17},{17,25},{25,1},{2,10},{10... | collective-permute-start | bytes 786440 | tf_op jit(solution)/shard_map/ppermute | solution.py:262
  107.9 10.8 %collective-permute-start.8 = (bf16[512,256]{1,0:T(8,128)(2,1)S(1)}, bf16[512,256]{1,0:T(8,128)(2,1)S(1)}, u32[]{:S(2)}, u32[]{:S(2)}) collective-permute-start(bf16[512,256]{1,0:T(8,128)(2,1)S(1)} %add.21), channel_id=1, source_target_pairs={{0,24},{8,0},{16,8},{24,16},{1,25},{9,1},{17,9},{25,17},{2,26},{10... | collective-permute-start | bytes 786440 | tf_op jit(solution)/shard_map/ppermute | solution.py:263
  121.3 0.8 copy-start.7
  122.1 20.6 %all-to-all-start.3 = ((bf16[8,128,256]{2,1,0:T(8,128)(2,1)}), bf16[8,128,256]{2,1,0:T(8,128)(2,1)S(1)}, u32[]{:S(2)}, u32[]{:S(2)}) async-start(bf16[8,128,256]{2,1,0:T(8,128)(2,1)} %bitcast.11), calls=%async_computation.3 | async-start | bytes 1048576 | tf_op jit(solution)/shard_map/all_to_all | solution.py:242
  142.7 0.8 copy-start.8

commit v3 on v2

--- a/solution.py
+++ b/solution.py
@@ -29,17 +29,27 @@
 
 
 def attention_kernel(
-    nz, nx, order, me, qg, kv0, kv1, kv3, kv2a, kv2b,
+    nz, nx, order, me, in0, in1, in2, in3, in4, in5, in6, in7,
     oq, o0, o1a, o1b, o2a, o2b, o3a, o3b,
     ks, vs, qs, gs, scr, dkt, dvt, qacc, oacc, rowpos, sblk, spos,
+    kv0, kv1a, kv1b, kv3a, kv3b, kv2a, kv2b, qg, stage, stage_q, in_sems, out_sems,
 ):
+    arrays = (in0, in1, in2, in3, in4, in5, in6, in7)
+    landed = (kv0, kv1a, kv1b, kv3a, kv3b, kv2a, kv2b, qg)
+    fetch = [
+        pltpu.make_async_copy(src, dst, in_sems.at[i])
+        for i, (src, dst) in enumerate(zip(arrays, landed, strict=True))
+    ]
+    for copy in fetch:
+        copy.start()
     x = me[0]
+    busy = me[1]
     per_part = 2 * nz
     half = per_part // 2
 
     def block_of(part, j):
         src = lax.rem(x - part + nx, nx)
-        return order[((j // 2) * nx + src) * 2 + j % 2]
+        return order[(me[2 + j // 2] * nx + src) * 2 + j % 2]
 
     def block_rows(p):
         return pl.ds(pl.multiple_of(p * BLK, BLK), BLK)
@@ -49,13 +59,18 @@
             return full, j * BLK
         return (a, j * BLK) if j < half else (b, (j - half) * BLK)
 
-    for part in range(nx):
+    pieces = ((None, None), (kv1a, kv1b), (kv2a, kv2b), (kv3a, kv3b))
+    arrivals = {0: (0,), 1: (1, 2), 3: (3, 4), 2: (5, 6)}
+    for part in (0, 1, 3, 2):
+        for i in arrivals[part]:
+            fetch[i].wait()
         for j in range(per_part):
-            ref, start = part_ref((kv0, kv1, None, kv3)[part], kv2a, kv2b, j)
+            ref, start = part_ref(kv0 if part == 0 else None, *pieces[part], j)
             at = block_rows(block_of(part, j))
             ks[at, :] = ref[start:start + BLK, :DH]
             vs[at, :] = ref[start:start + BLK, DH:]
 
+    fetch[7].wait()
     own = [block_of(0, j) for j in range(per_part)]
     for j in range(per_part):
         rank = jnp.int32(0)
@@ -129,38 +144,47 @@
         dq = (qacc[...] * F32(SCALE)).astype(BF16)
         for k in range(GROUP):
             to = block_rows(sblk[base + k])
-            oq[to, :DH] = att[k * BLK:(k + 1) * BLK, :]
-            oq[to, DH:] = dq[k * BLK:(k + 1) * BLK, :]
+            stage_q[to, :DH] = att[k * BLK:(k + 1) * BLK, :]
+            stage_q[to, DH:] = dq[k * BLK:(k + 1) * BLK, :]
         return carry
 
-    lax.fori_loop(0, per_part // GROUP, group_step, 0)
+    lax.fori_loop(0, (per_part // GROUP) * busy, group_step, 0)
 
     for t in range(ks.shape[0] // DH):
         at = slice(t * DH, (t + 1) * DH)
         ks[at, :] = (dkt[:, at] * F32(SCALE)).T.astype(BF16)
         vs[at, :] = dvt[:, at].T.astype(BF16)
 
-    halves = ((None, None), (o1a, o1b), (o2a, o2b), (o3a, o3b))
-    for part in range(nx):
-        for j in range(per_part):
-            ref, start = part_ref(o0 if part == 0 else None, *halves[part], j)
-            at = block_rows(block_of(part, j))
-            ref[start:start + BLK, :DH] = ks[at, :]
-            ref[start:start + BLK, DH:] = vs[at, :]
-
-
-def attention(nz, nx, order, me, qg, parts):
+    sends = [pltpu.make_async_copy(stage_q, oq, out_sems.at[8])]
+    sends[0].start()
+    slots = (
+        (o2a, 2, 0), (o2b, 2, half), (o3b, 3, half), (o1a, 1, 0), (o3a, 3, 0), (o1b, 1, half),
+        (o0.at[:half * BLK], 0, 0), (o0.at[half * BLK:], 0, half),
+    )
+    for i, (out, part, first) in enumerate(slots):
+        for j in range(half):
+            at = block_rows(block_of(part, first + j))
+            stage[i, j * BLK:(j + 1) * BLK, :DH] = ks[at, :]
+            stage[i, j * BLK:(j + 1) * BLK, DH:] = vs[at, :]
+        sends.append(pltpu.make_async_copy(stage.at[i], out, out_sems.at[i]))
+        sends[-1].start()
+    for copy in sends:
+        copy.wait()
+
+
+def attention(nz, nx, order, me, qg, kv, near, far):
     rows = qg.shape[0]
     seq = rows * nx
-    vm = pl.BlockSpec(memory_space=pltpu.VMEM)
     sm = pl.BlockSpec(memory_space=pltpu.SMEM)
-    whole = jax.ShapeDtypeStruct((rows, 2 * DH), BF16)
-    half = jax.ShapeDtypeStruct((rows // 2, 2 * DH), BF16)
+    anywhere = pl.BlockSpec(memory_space=pl.ANY)
+    hbm = pl.BlockSpec(memory_space=pltpu.HBM)
+    whole = pltpu.HBM((rows, 2 * DH), BF16)
+    half = pltpu.HBM((rows // 2, 2 * DH), BF16)
     return pl.pallas_call(
         lambda *refs: attention_kernel(nz, nx, *refs),
         out_shape=(whole,) * 2 + (half,) * 6,
-        in_specs=[sm, sm] + [vm] * 6,
-        out_specs=(vm,) * 8,
+        in_specs=[sm, sm] + [anywhere] * 8,
+        out_specs=(hbm,) * 8,
         scratch_shapes=[
             pltpu.VMEM((seq, DH), BF16),
             pltpu.VMEM((seq, DH), BF16),
@@ -174,86 +198,119 @@
             pltpu.VMEM((ROWS, DH), jnp.int32),
             pltpu.SMEM((rows // BLK,), jnp.int32),
             pltpu.SMEM((rows // BLK,), jnp.int32),
+            pltpu.VMEM((rows, 2 * DH), BF16),
+        ]
+        + [pltpu.VMEM((rows // 2, 2 * DH), BF16)] * 6
+        + [
+            pltpu.VMEM((rows, 2 * DH), BF16),
+            pltpu.VMEM((8, rows // 2, 2 * DH), BF16),
+            pltpu.VMEM((rows, 2 * DH), BF16),
+            pltpu.SemaphoreType.DMA((8,)),
+            pltpu.SemaphoreType.DMA((9,)),
         ],
-        compiler_params=pltpu.CompilerParams(vmem_limit_bytes=48 * 2**20),
+        compiler_params=pltpu.CompilerParams(vmem_limit_bytes=36 * 2**20),
         name="attention",
-    )(order, me, qg, *parts)
-
-
-def run_copies(copies, sems):
-    started = [pltpu.make_async_copy(src, dst, sems.at[i]) for i, (src, dst) in enumerate(copies)]
-    for copy in started:
-        copy.start()
-    for copy in started:
-        copy.wait()
+    )(order, me, kv, *near, *far, qg)
 
 
 def by_head(a, b, slots):
     rows, width = a.shape
     heads = width // DH
 
-    def kernel(a_ref, b_ref, out, sems):
-        copies = []
+    def kernel(a_ref, b_ref, out):
         for slot in range(slots):
-            cols = slice((slot % heads) * DH, (slot % heads + 1) * DH)
-            copies.append((a_ref.at[:, cols], out.at[slot, :, :DH]))
-            copies.append((b_ref.at[:, cols], out.at[slot, :, DH:]))
-        run_copies(copies, sems)
-
-    anywhere = pl.BlockSpec(memory_space=pl.ANY)
+            head = (slot + 2 * heads - slots) % heads
+            cols = slice(head * DH, (head + 1) * DH)
+            out[slot, :, :DH] = a_ref[:, cols]
+            out[slot, :, DH:] = b_ref[:, cols]
+
+    vm = pl.BlockSpec(memory_space=pltpu.VMEM)
     return pl.pallas_call(
         kernel,
-        out_shape=jax.ShapeDtypeStruct((slots, rows, 2 * DH), BF16),
-        in_specs=[anywhere, anywhere],
-        out_specs=anywhere,
-        scratch_shapes=[pltpu.SemaphoreType.DMA((2 * slots,))],
+        out_shape=pltpu.VMEM((slots, rows, 2 * DH), BF16),
+        in_specs=[vm, vm],
+        out_specs=vm,
         name="by_head",
     )(a, b)
 
 
 def from_heads(stacked, heads):
-    rows = stacked.shape[1]
-
-    def kernel(stack, a_ref, b_ref, sems):
-        copies = []
+    slots, rows = stacked.shape[:2]
+    first = slots - heads
+
+    def kernel(stack, a_ref, b_ref, got, a_own, b_own, sems):
+        fetch = [
+            pltpu.make_async_copy(stack.at[first + head], got.at[head], sems.at[head])
+            for head in range(heads)
+        ]
+        for copy in fetch:
+            copy.start()
         for head in range(heads):
+            fetch[head].wait()
             cols = slice(head * DH, (head + 1) * DH)
-            copies.append((stack.at[head, :, :DH], a_ref.at[:, cols]))
-            copies.append((stack.at[head, :, DH:], b_ref.at[:, cols]))
-        run_copies(copies, sems)
-
-    anywhere = pl.BlockSpec(memory_space=pl.ANY)
-    out = jax.ShapeDtypeStruct((rows, heads * DH), BF16)
+            a_own[:, cols] = got[head, :, :DH]
+            b_own[:, cols] = got[head, :, DH:]
+        sends = [
+            pltpu.make_async_copy(a_own, a_ref, sems.at[heads]),
+            pltpu.make_async_copy(b_own, b_ref, sems.at[heads + 1]),
+        ]
+        for copy in sends:
+            copy.start()
+        for copy in sends:
+            copy.wait()
+
+    hbm = pl.BlockSpec(memory_space=pltpu.HBM)
+    out = pltpu.HBM((rows, heads * DH), BF16)
     return pl.pallas_call(
         kernel,
         out_shape=(out, out),
-        in_specs=[anywhere],
-        out_specs=(anywhere, anywhere),
-        scratch_shapes=[pltpu.SemaphoreType.DMA((2 * heads,))],
+        in_specs=[pl.BlockSpec(memory_space=pl.ANY)],
+        out_specs=(hbm, hbm),
+        scratch_shapes=[
+            pltpu.VMEM((heads, rows, 2 * DH), BF16),
+            pltpu.VMEM((rows, heads * DH), BF16),
+            pltpu.VMEM((rows, heads * DH), BF16),
+            pltpu.SemaphoreType.DMA((heads + 2,)),
+        ],
         name="from_heads",
     )(stacked)
+
+
+def ring_orders(nz):
+    first = list(range(0, nz, 2)) + list(range(nz - 1, 0, -2))
+    turn = nz // 4
+    return first, first[turn:] + first[:turn]
 
 
 def make_shards(nz, nx):
     def to(step):
         return [(i, (i + step) % nx) for i in range(nx)]
 
+    rings = ring_orders(nz)
+    groups = [[z * len(rings) + core for z in ring] for core, ring in enumerate(rings)]
+
     def exchange(v):
-        return lax.all_to_all(v, "z", 0, 0, tiled=True)
+        return lax.all_to_all(v, ("z", "kv"), 0, 0, axis_index_groups=groups, tiled=True)
 
     def shards(queries, keys, values, out_grad, block_order):
         rows, width = queries.shape[1:]
         heads = width // DH
         kv = exchange(by_head(keys[0], values[0], nz)).reshape(nz * rows, 2 * DH)
-        right = lax.ppermute(kv, "x", to(1))
-        left = lax.ppermute(kv, "x", to(-1))
+        cut = nz * rows // 2
+        kva, kvb = kv[:cut], kv[cut:]
+        right_a = lax.ppermute(kva, "x", to(1))
+        left_b = lax.ppermute(kvb, "x", to(-1))
+        right_b = lax.ppermute(kvb, "x", to(1))
+        left_a = lax.ppermute(kva, "x", to(-1))
+        far_a = lax.ppermute(right_a, "x", to(1))
+        far_b = lax.ppermute(left_b, "x", to(-1))
         qg = exchange(by_head(queries[0], out_grad[0], nz)).reshape(nz * rows, 2 * DH)
-        cut = nz * rows // 2
-        far_a = lax.ppermute(right[:cut], "x", to(1))
-        far_b = lax.ppermute(left[cut:], "x", to(-1))
-        me = lax.axis_index("x").astype(jnp.int32).reshape(1)
+        ring = jnp.asarray(rings, jnp.int32)[lax.axis_index("kv")]
+        idle = jnp.any(ring[:nz - heads] == lax.axis_index("z"))
+        place = jnp.stack([lax.axis_index("x").astype(jnp.int32), 1 - idle.astype(jnp.int32)])
+        me = jnp.concatenate([place, ring])
         oq, o0, o1a, o1b, o2a, o2b, o3a, o3b = attention(
-            nz, nx, block_order[0], me, qg, (kv, right, left, far_a, far_b)
+            nz, nx, block_order[0], me, qg, kv, (right_a, right_b, left_a, left_b), (far_a, far_b)
         )
         via_right = lax.ppermute(o2a, "x", to(1))
         via_left = lax.ppermute(o2b, "x", to(-1))

time: 156 us -> 121 us (0.78); the launches traced: 157 us -> 120 us
  Pallas kernels: 75.6 us -> 11.1 us
  waiting for transfers between devices: 30.7 us -> 48.1 us
  starting transfers between devices: 43.1 us -> 53.8 us
  local copies, waits for them, and re-layouts: 5.42 us -> 3.1 us
    pallas_call x4, Pallas kernels: 60.5 us -> 7.46 us  [the longest x2 3.82 us: by_head(): pl.pallas_call(kernel, out_shape=pltpu.VMEM((slots, rows, 2 * DH), BF16),...]
    all_to_all x4, waiting for transfers between devices: 4.22 us -> 25.2 us  [exchange(): lax.all_to_all(v, ('z', 'kv'), 0, 0, axis_index_groups=groups, tiled=True)]
    pallas_call x1, Pallas kernels: 15.1 us -> 3.67 us  [attention(): pl.pallas_call(lambda *refs: attention_kernel(nz, nx, *refs), out_shape=(...]
    all_to_all x4, starting transfers between devices: 27.6 us -> 36.7 us  [exchange(): lax.all_to_all(v, ('z', 'kv'), 0, 0, axis_index_groups=groups, tiled=True)]
    ppermute x4 -> x6, waiting for transfers between devices: 17.9 us -> 11.6 us  [the longest x1 5.01 us: shards(): far_a = lax.ppermute(right_a, 'x', to(1))]
    ppermute x1, waiting for transfers between devices: 1.31 us -> 3.69 us  [shards(): r3b = lax.ppermute(o3b, 'x', to(1))]
    unnamed x18, local copies, waits for them, and re-layouts: 5.39 us -> 3.06 us
    ppermute x4 -> x6, starting transfers between devices: 6.61 us -> 8.58 us  [the longest x1 2.96 us: shards(): far_b = lax.ppermute(left_b, 'x', to(-1))]
  transfers between devices with their start and end apart: 14 -> 16, of which waited for: 9 -> 10; matrix products, arithmetic and copies ran while one was open for 1% -> 2% of each run, Pallas kernels for 19% -> 3%
where the time goes in v3:
time: 121 us; the launch traced here: 120 us
  starting transfers between devices  53.8 us (44%)
  waiting for transfers between devices  48.1 us (40%)
  Pallas kernels  11.1 us (9%)
  local copies, waits for them, and re-layouts  3.1 us (3%)
  other arithmetic  1.89 us (2%)
  between operations  1.52 us (1%)
    all_to_all x4, starting transfers between devices, exchange(): lax.all_to_all(v, ('z', 'kv'), 0, 0, axis_index_groups=groups, tiled=True)  36.7 us
    all_to_all x4, waiting for transfers between devices, exchange(): lax.all_to_all(v, ('z', 'kv'), 0, 0, axis_index_groups=groups, tiled=True)  25.2 us
    ppermute x1, waiting for transfers between devices, shards(): r3a = lax.ppermute(o3a + via_right, 'x', to(1))  5.28 us
    ppermute x1, waiting for transfers between devices, shards(): far_a = lax.ppermute(right_a, 'x', to(1))  5.01 us
    ppermute x1, waiting for transfers between devices, shards(): right_a = lax.ppermute(kva, 'x', to(1))  4.34 us
    pallas_call x2, Pallas kernels, by_head(): pl.pallas_call(kernel, out_shape=pltpu.VMEM((slots, rows, 2 * DH), BF16),...  3.82 us
    ppermute x1, waiting for transfers between devices, shards(): r3b = lax.ppermute(o3b, 'x', to(1))  3.69 us
    pallas_call x1, Pallas kernels, attention(): pl.pallas_call(lambda *refs: attention_kernel(nz, nx, *refs), out_shape=(...  3.67 us
  transfers between devices with their start and end apart: 16, of which 10 were waited for; matrix products, arithmetic and copies ran while one was open for 2% of the time, Pallas kernels for 3%

profile of v3, /device:TPU:8, one launch (start us, length us, event | category | flops | bytes accessed | tf_op | source)
XLA Modules:
  0.0 119.6 jit_solution(5841913822568103953)
XLA Ops:
  0.6 1.9 %by_head.2 = bf16[8,128,256]{2,1,0:T(8,128)(2,1)} custom-call(bf16[128,768]{1,0:T(8,128)(2,1)} %bitcast.27, bf16[128,768]{1,0:T(8,128)(2,1)} %bitcast.28), custom_call_target="tpu_custom_call" | custom-call | tf_op jit(solution)/shard_map/by_head/pallas_call | solution.py:228
  2.5 8.5 %all-to-all-start = ((bf16[8,128,256]{2,1,0:T(8,128)(2,1)}), bf16[8,128,256]{2,1,0:T(8,128)(2,1)S(1)}, u32[]{:S(2)}, u32[]{:S(2)}) async-start(bf16[8,128,256]{2,1,0:T(8,128)(2,1)} %by_head.2), calls=%async_computation | async-start | bytes 1048576 | tf_op jit(solution)/shard_map/all_to_all | solution.py:293
  11.0 1.9 %by_head.3 = bf16[8,128,256]{2,1,0:T(8,128)(2,1)} custom-call(bf16[128,768]{1,0:T(8,128)(2,1)} %bitcast.29, bf16[128,768]{1,0:T(8,128)(2,1)} %bitcast.30), custom_call_target="tpu_custom_call" | custom-call | tf_op jit(solution)/shard_map/by_head/pallas_call | solution.py:228
  12.9 12.1 %all-to-all-done = bf16[8,128,256]{2,1,0:T(8,128)(2,1)S(1)} async-done(((bf16[8,128,256]{2,1,0:T(8,128)(2,1)}), bf16[8,128,256]{2,1,0:T(8,128)(2,1)S(1)}, u32[]{:S(2)}, u32[]{:S(2)}) %all-to-all-start) | async-done | bytes 524320 | tf_op jit(solution)/shard_map/all_to_all | solution.py:293
  25.0 5.4 %all-to-all-start.1 = ((bf16[8,128,256]{2,1,0:T(8,128)(2,1)}), bf16[8,128,256]{2,1,0:T(8,128)(2,1)S(1)}, u32[]{:S(2)}, u32[]{:S(2)}) async-start(bf16[8,128,256]{2,1,0:T(8,128)(2,1)} %by_head.3), calls=%async_computation.1 | async-start | bytes 1048576 | tf_op jit(solution)/shard_map/all_to_all | solution.py:293
  30.5 1.6 %collective-permute-start = (bf16[512,256]{1,0:T(8,128)(2,1)S(1)}, bf16[512,256]{1,0:T(8,128)(2,1)S(1)}, u32[]{:S(2)}, u32[]{:S(2)}) collective-permute-start(bf16[512,256]{1,0:T(8,128)(2,1)S(1)} %bitcast.25), channel_id=1, source_target_pairs={{0,8},{8,16},{16,24},{24,0},{1,9},{9,17},{17,25},{25,1},{2,10},{10... | collective-permute-start | bytes 786440 | tf_op jit(solution)/shard_map/ppermute | solution.py:301
  32.0 1.7 %collective-permute-start.3 = (bf16[512,256]{1,0:T(8,128)(2,1)S(1)}, bf16[512,256]{1,0:T(8,128)(2,1)S(1)}, u32[]{:S(2)}, u32[]{:S(2)}) collective-permute-start(bf16[512,256]{1,0:T(8,128)(2,1)S(1)} %bitcast.23), channel_id=1, source_target_pairs={{0,24},{8,0},{16,8},{24,16},{1,25},{9,1},{17,9},{25,17},{2,26},{10... | collective-permute-start | bytes 786440 | tf_op jit(solution)/shard_map/ppermute | solution.py:302
  33.8 1.5 %collective-permute-start.2 = (bf16[512,256]{1,0:T(8,128)(2,1)S(1)}, bf16[512,256]{1,0:T(8,128)(2,1)S(1)}, u32[]{:S(2)}, u32[]{:S(2)}) collective-permute-start(bf16[512,256]{1,0:T(8,128)(2,1)S(1)} %bitcast.26), channel_id=1, source_target_pairs={{0,24},{8,0},{16,8},{24,16},{1,25},{9,1},{17,9},{25,17},{2,26},{10... | collective-permute-start | bytes 786440 | tf_op jit(solution)/shard_map/ppermute | solution.py:304
  35.8 4.3 %collective-permute-done.refs_3_ = bf16[512,256]{1,0:T(8,128)(2,1)S(1)} collective-permute-done((bf16[512,256]{1,0:T(8,128)(2,1)S(1)}, bf16[512,256]{1,0:T(8,128)(2,1)S(1)}, u32[]{:S(2)}, u32[]{:S(2)}) %collective-permute-start) | collective-permute-done | bytes 262176 | tf_op jit(solution)/shard_map/ppermute | solution.py:301
  40.7 3.0 %collective-permute-start.5 = (bf16[512,256]{1,0:T(8,128)(2,1)S(1)}, bf16[512,256]{1,0:T(8,128)(2,1)S(1)}, u32[]{:S(2)}, u32[]{:S(2)}) collective-permute-start(bf16[512,256]{1,0:T(8,128)(2,1)S(1)} %collective-permute-done.3.refs_6_), channel_id=1, source_target_pairs={{0,24},{8,0},{16,8},{24,16},{1,25},{9,1},{17,9},{25,17},{2,26},{10... | collective-permute-start | bytes 786440 | tf_op jit(solution)/shard_map/ppermute | solution.py:306
  46.4 5.0 %collective-permute-done.4.refs_7_ = bf16[512,256]{1,0:T(8,128)(2,1)S(1)} collective-permute-done((bf16[512,256]{1,0:T(8,128)(2,1)S(1)}, bf16[512,256]{1,0:T(8,128)(2,1)S(1)}, u32[]{:S(2)}, u32[]{:S(2)}) %collective-permute-start.4) | collective-permute-done | bytes 262176 | tf_op jit(solution)/shard_map/ppermute | solution.py:305
  52.6 3.7 %attention.1 = (bf16[1024,256]{1,0:T(8,128)(2,1)}, bf16[1024,256]{1,0:T(8,128)(2,1)}, bf16[512,256]{1,0:T(8,128)(2,1)}, bf16[512,256]{1,0:T(8,128)(2,1)}, bf16[5...) custom-call(s32[64]{0:T(128)S(1)} %bitcast.21, ...), custom_call_target="tpu_custom_call" | custom-call | tf_op jit(solution)/shard_map/attention/pallas_call | solution.py:183
  56.3 1.6 %collective-permute-start.7 = (bf16[512,256]{1,0:T(8,128)(2,1)}, bf16[512,256]{1,0:T(8,128)(2,1)S(1)}, u32[]{:S(2)}, u32[]{:S(2)}) collective-permute-start(bf16[512,256]{1,0:T(8,128)(2,1)} %get-tuple-element.22), channel_id=1, source_target_pairs={{0,8},{8,16},{16,24},{24,0},{1,9},{9,17},{17,25},{25,1},{2,10},{10... | collective-permute-start | bytes 786440 | tf_op jit(solution)/shard_map/ppermute | solution.py:315
  57.9 1.7 %collective-permute-start.9 = (bf16[512,256]{1,0:T(8,128)(2,1)}, bf16[512,256]{1,0:T(8,128)(2,1)S(1)}, u32[]{:S(2)}, u32[]{:S(2)}) collective-permute-start(bf16[512,256]{1,0:T(8,128)(2,1)} %get-tuple-element.24), channel_id=1, source_target_pairs={{0,24},{8,0},{16,8},{24,16},{1,25},{9,1},{17,9},{25,17},{2,26},{10... | collective-permute-start | bytes 786440 | tf_op jit(solution)/shard_map/ppermute | solution.py:316
  59.6 19.3 %all-to-all-start.2 = ((bf16[8,128,256]{2,1,0:T(8,128)(2,1)}), bf16[8,128,256]{2,1,0:T(8,128)(2,1)S(1)}, u32[]{:S(2)}, u32[]{:S(2)}) async-start(bf16[8,128,256]{2,1,0:T(8,128)(2,1)} %bitcast.22), calls=%async_computation.2 | async-start | bytes 1048576 | tf_op jit(solution)/shard_map/all_to_all | solution.py:293
  78.9 1.8 %collective-permute-start.6 = (bf16[512,256]{1,0:T(8,128)(2,1)S(1)}, bf16[512,256]{1,0:T(8,128)(2,1)S(1)}, u32[]{:S(2)}, u32[]{:S(2)}) collective-permute-start(bf16[512,256]{1,0:T(8,128)(2,1)S(1)} %copy-done.8), channel_id=1, source_target_pairs={{0,24},{8,0},{16,8},{24,16},{1,25},{9,1},{17,9},{25,17},{2,26},{10... | collective-permute-start | bytes 786440 | tf_op jit(solution)/shard_map/ppermute | solution.py:318
  82.1 3.0 %collective-permute-start.10 = (bf16[512,256]{1,0:T(8,128)(2,1)S(1)}, bf16[512,256]{1,0:T(8,128)(2,1)S(1)}, u32[]{:S(2)}, u32[]{:S(2)}) collective-permute-start(bf16[512,256]{1,0:T(8,128)(2,1)S(1)} %add.25), channel_id=1, source_target_pairs={{0,24},{8,0},{16,8},{24,16},{1,25},{9,1},{17,9},{25,17},{2,26},{10... | collective-permute-start | bytes 786440 | tf_op jit(solution)/shard_map/ppermute | solution.py:320
  85.1 2.3 %collective-permute-done.6 = bf16[512,256]{1,0:T(8,128)(2,1)S(1)} collective-permute-done((bf16[512,256]{1,0:T(8,128)(2,1)S(1)}, bf16[512,256]{1,0:T(8,128)(2,1)S(1)}, u32[]{:S(2)}, u32[]{:S(2)}) %collective-permute-start.6) | collective-permute-done | bytes 262176 | tf_op jit(solution)/shard_map/ppermute | solution.py:318
  87.5 3.7 %collective-permute-done.11 = bf16[512,256]{1,0:T(8,128)(2,1)S(1)} collective-permute-done((bf16[512,256]{1,0:T(8,128)(2,1)S(1)}, bf16[512,256]{1,0:T(8,128)(2,1)S(1)}, u32[]{:S(2)}, u32[]{:S(2)}) %collective-permute-start.11) | collective-permute-done | bytes 262176 | tf_op jit(solution)/shard_map/ppermute | solution.py:317
  91.2 5.3 %collective-permute-done.8 = bf16[512,256]{1,0:T(8,128)(2,1)S(1)} collective-permute-done((bf16[512,256]{1,0:T(8,128)(2,1)S(1)}, bf16[512,256]{1,0:T(8,128)(2,1)S(1)}, u32[]{:S(2)}, u32[]{:S(2)}) %collective-permute-start.8) | collective-permute-done | bytes 262176 | tf_op jit(solution)/shard_map/ppermute | solution.py:319
  98.3 3.5 %all-to-all-start.3 = ((bf16[8,128,256]{2,1,0:T(8,128)(2,1)}), bf16[8,128,256]{2,1,0:T(8,128)(2,1)S(1)}, u32[]{:S(2)}, u32[]{:S(2)}) async-start(bf16[8,128,256]{2,1,0:T(8,128)(2,1)} %bitcast.15), calls=%async_computation.3 | async-start | bytes 1048576 | tf_op jit(solution)/shard_map/all_to_all | solution.py:293
  101.8 1.8 %from_heads.2 = (bf16[128,768]{1,0:T(8,128)(2,1)}, bf16[128,768]{1,0:T(8,128)(2,1)}) custom-call(bf16[8,128,256]{2,1,0:T(8,128)(2,1)} %copy-done.1), custom_call_target="tpu_custom_call" | custom-call | tf_op jit(solution)/shard_map/from_heads/pallas_call | solution.py:264
  103.6 13.2 %all-to-all-done.3.stack = bf16[8,128,256]{2,1,0:T(8,128)(2,1)S(1)} async-done(((bf16[8,128,256]{2,1,0:T(8,128)(2,1)}), bf16[8,128,256]{2,1,0:T(8,128)(2,1)S(1)}, u32[]{:S(2)}, u32[]{:S(2)}) %all-to-all-start.3) | async-done | bytes 524320 | tf_op jit(solution)/shard_map/all_to_all | solution.py:293
  117.6 1.8 %from_heads.3 = (bf16[128,768]{1,0:T(8,128)(2,1)}, bf16[128,768]{1,0:T(8,128)(2,1)}) custom-call(bf16[8,128,256]{2,1,0:T(8,128)(2,1)} %copy-done.2), custom_call_target="tpu_custom_call" | custom-call | tf_op jit(solution)/shard_map/from_heads/pallas_call | solution.py:264
  (39 shorter events, 8.3 us)
Async XLA Ops:
  2.5 22.4 %all-to-all-start = ((bf16[8,128,256]{2,1,0:T(8,128)(2,1)}), bf16[8,128,256]{2,1,0:T(8,128)(2,1)S(1)}, u32[]{:S(2)}, u32[]{:S(2)}) async-start(bf16[8,128,256]{2,1,0:T(8,128)(2,1)} %by_head.2), calls=%async_computation | async-start | bytes 1048576 | tf_op jit(solution)/shard_map/all_to_all | solution.py:293
  25.0 20.1 %all-to-all-start.1 = ((bf16[8,128,256]{2,1,0:T(8,128)(2,1)}), bf16[8,128,256]{2,1,0:T(8,128)(2,1)S(1)}, u32[]{:S(2)}, u32[]{:S(2)}) async-start(bf16[8,128,256]{2,1,0:T(8,128)(2,1)} %by_head.3), calls=%async_computation.1 | async-start | bytes 1048576 | tf_op jit(solution)/shard_map/all_to_all | solution.py:293
  30.5 9.7 %collective-permute-start = (bf16[512,256]{1,0:T(8,128)(2,1)S(1)}, bf16[512,256]{1,0:T(8,128)(2,1)S(1)}, u32[]{:S(2)}, u32[]{:S(2)}) collective-permute-start(bf16[512,256]{1,0:T(8,128)(2,1)S(1)} %bitcast.25), channel_id=1, source_target_pairs={{0,8},{8,16},{16,24},{24,0},{1,9},{9,17},{17,25},{25,1},{2,10},{10... | collective-permute-start | bytes 786440 | tf_op jit(solution)/shard_map/ppermute | solution.py:301
  32.0 8.7 %collective-permute-start.3 = (bf16[512,256]{1,0:T(8,128)(2,1)S(1)}, bf16[512,256]{1,0:T(8,128)(2,1)S(1)}, u32[]{:S(2)}, u32[]{:S(2)}) collective-permute-start(bf16[512,256]{1,0:T(8,128)(2,1)S(1)} %bitcast.23), channel_id=1, source_target_pairs={{0,24},{8,0},{16,8},{24,16},{1,25},{9,1},{17,9},{25,17},{2,26},{10... | collective-permute-start | bytes 786440 | tf_op jit(solution)/shard_map/ppermute | solution.py:302
  33.8 9.9 %copy-start.6 = (s32[2,8]{1,0:T(2,128)S(1)}, s32[2,8]{1,0:T(2,128)}, u32[]{:S(2)}) copy-start(s32[2,8]{1,0:T(2,128)} %constant.25.clone) | copy-start | bytes 196
  33.8 12.6 %collective-permute-start.2 = (bf16[512,256]{1,0:T(8,128)(2,1)S(1)}, bf16[512,256]{1,0:T(8,128)(2,1)S(1)}, u32[]{:S(2)}, u32[]{:S(2)}) collective-permute-start(bf16[512,256]{1,0:T(8,128)(2,1)S(1)} %bitcast.26), channel_id=1, source_target_pairs={{0,24},{8,0},{16,8},{24,16},{1,25},{9,1},{17,9},{25,17},{2,26},{10... | collective-permute-start | bytes 786440 | tf_op jit(solution)/shard_map/ppermute | solution.py:304
  35.3 11.0 %collective-permute-start.1 = (bf16[512,256]{1,0:T(8,128)(2,1)S(1)}, bf16[512,256]{1,0:T(8,128)(2,1)S(1)}, u32[]{:S(2)}, u32[]{:S(2)}) collective-permute-start(bf16[512,256]{1,0:T(8,128)(2,1)S(1)} %bitcast.24), channel_id=1, source_target_pairs={{0,8},{8,16},{16,24},{24,0},{1,9},{9,17},{17,25},{25,1},{2,10},{10... | collective-permute-start | bytes 786440 | tf_op jit(solution)/shard_map/ppermute | solution.py:303
  40.1 11.2 %collective-permute-start.4 = (bf16[512,256]{1,0:T(8,128)(2,1)S(1)}, bf16[512,256]{1,0:T(8,128)(2,1)S(1)}, u32[]{:S(2)}, u32[]{:S(2)}) collective-permute-start(bf16[512,256]{1,0:T(8,128)(2,1)S(1)} %collective-permute-done.refs_3_), channel_id=1, source_target_pairs={{0,8},{8,16},{16,24},{24,0},{1,9},{9,17},{17,25},{25,1},{2,10},{10... | collective-permute-start | bytes 786440 | tf_op jit(solution)/shard_map/ppermute | solution.py:305
  40.7 11.2 %collective-permute-start.5 = (bf16[512,256]{1,0:T(8,128)(2,1)S(1)}, bf16[512,256]{1,0:T(8,128)(2,1)S(1)}, u32[]{:S(2)}, u32[]{:S(2)}) collective-permute-start(bf16[512,256]{1,0:T(8,128)(2,1)S(1)} %collective-permute-done.3.refs_6_), channel_id=1, source_target_pairs={{0,24},{8,0},{16,8},{24,16},{1,25},{9,1},{17,9},{25,17},{2,26},{10... | collective-permute-start | bytes 786440 | tf_op jit(solution)/shard_map/ppermute | solution.py:306
  56.3 24.7 %collective-permute-start.7 = (bf16[512,256]{1,0:T(8,128)(2,1)}, bf16[512,256]{1,0:T(8,128)(2,1)S(1)}, u32[]{:S(2)}, u32[]{:S(2)}) collective-permute-start(bf16[512,256]{1,0:T(8,128)(2,1)} %get-tuple-element.22), channel_id=1, source_target_pairs={{0,8},{8,16},{16,24},{24,0},{1,9},{9,17},{17,25},{25,1},{2,10},{10... | collective-permute-start | bytes 786440 | tf_op jit(solution)/shard_map/ppermute | solution.py:315
  57.9 23.3 %collective-permute-start.9 = (bf16[512,256]{1,0:T(8,128)(2,1)}, bf16[512,256]{1,0:T(8,128)(2,1)S(1)}, u32[]{:S(2)}, u32[]{:S(2)}) collective-permute-start(bf16[512,256]{1,0:T(8,128)(2,1)} %get-tuple-element.24), channel_id=1, source_target_pairs={{0,24},{8,0},{16,8},{24,16},{1,25},{9,1},{17,9},{25,17},{2,26},{10... | collective-permute-start | bytes 786440 | tf_op jit(solution)/shard_map/ppermute | solution.py:316
  59.6 19.3 %copy-start.8 = (bf16[512,256]{1,0:T(8,128)(2,1)S(1)}, bf16[512,256]{1,0:T(8,128)(2,1)}, u32[]{:S(2)}) copy-start(bf16[512,256]{1,0:T(8,128)(2,1)} %get-tuple-element.20) | copy-start | bytes 786436
  59.6 21.1 %copy-start.7 = (bf16[512,256]{1,0:T(8,128)(2,1)S(1)}, bf16[512,256]{1,0:T(8,128)(2,1)}, u32[]{:S(2)}) copy-start(bf16[512,256]{1,0:T(8,128)(2,1)} %get-tuple-element.25) | copy-start | bytes 786436
  59.6 21.4 %copy-start.5 = (bf16[512,256]{1,0:T(8,128)(2,1)S(1)}, bf16[512,256]{1,0:T(8,128)(2,1)}, u32[]{:S(2)}) copy-start(bf16[512,256]{1,0:T(8,128)(2,1)} %get-tuple-element.21) | copy-start | bytes 786436
  59.6 37.9 %all-to-all-start.2 = ((bf16[8,128,256]{2,1,0:T(8,128)(2,1)}), bf16[8,128,256]{2,1,0:T(8,128)(2,1)S(1)}, u32[]{:S(2)}, u32[]{:S(2)}) async-start(bf16[8,128,256]{2,1,0:T(8,128)(2,1)} %bitcast.22), calls=%async_computation.2 | async-start | bytes 1048576 | tf_op jit(solution)/shard_map/all_to_all | solution.py:293
  78.9 8.5 %collective-permute-start.6 = (bf16[512,256]{1,0:T(8,128)(2,1)S(1)}, bf16[512,256]{1,0:T(8,128)(2,1)S(1)}, u32[]{:S(2)}, u32[]{:S(2)}) collective-permute-start(bf16[512,256]{1,0:T(8,128)(2,1)S(1)} %copy-done.8), channel_id=1, source_target_pairs={{0,24},{8,0},{16,8},{24,16},{1,25},{9,1},{17,9},{25,17},{2,26},{10... | collective-permute-start | bytes 786440 | tf_op jit(solution)/shard_map/ppermute | solution.py:318
  80.8 10.4 %collective-permute-start.11 = (bf16[512,256]{1,0:T(8,128)(2,1)S(1)}, bf16[512,256]{1,0:T(8,128)(2,1)S(1)}, u32[]{:S(2)}, u32[]{:S(2)}) collective-permute-start(bf16[512,256]{1,0:T(8,128)(2,1)S(1)} %copy-done.7), channel_id=1, source_target_pairs={{0,8},{8,16},{16,24},{24,0},{1,9},{9,17},{17,25},{25,1},{2,10},{10... | collective-permute-start | bytes 786440 | tf_op jit(solution)/shard_map/ppermute | solution.py:317
  81.0 1.0 copy-start.4
  81.1 15.3 %copy-start.3 = (bf16[1024,256]{1,0:T(8,128)(2,1)S(1)}, bf16[1024,256]{1,0:T(8,128)(2,1)}, u32[]{:S(2)}) copy-start(bf16[1024,256]{1,0:T(8,128)(2,1)} %get-tuple-element.19) | copy-start | bytes 1572868
  81.1 15.3 %collective-permute-start.8 = (bf16[512,256]{1,0:T(8,128)(2,1)S(1)}, bf16[512,256]{1,0:T(8,128)(2,1)S(1)}, u32[]{:S(2)}, u32[]{:S(2)}) collective-permute-start(bf16[512,256]{1,0:T(8,128)(2,1)S(1)} %add.23), channel_id=1, source_target_pairs={{0,8},{8,16},{16,24},{24,0},{1,9},{9,17},{17,25},{25,1},{2,10},{10... | collective-permute-start | bytes 786440 | tf_op jit(solution)/shard_map/ppermute | solution.py:319
  82.1 14.4 %collective-permute-start.10 = (bf16[512,256]{1,0:T(8,128)(2,1)S(1)}, bf16[512,256]{1,0:T(8,128)(2,1)S(1)}, u32[]{:S(2)}, u32[]{:S(2)}) collective-permute-start(bf16[512,256]{1,0:T(8,128)(2,1)S(1)} %add.25), channel_id=1, source_target_pairs={{0,24},{8,0},{16,8},{24,16},{1,25},{9,1},{17,9},{25,17},{2,26},{10... | collective-permute-start | bytes 786440 | tf_op jit(solution)/shard_map/ppermute | solution.py:320
  97.5 0.8 copy-start.1
  98.3 18.5 %all-to-all-start.3 = ((bf16[8,128,256]{2,1,0:T(8,128)(2,1)}), bf16[8,128,256]{2,1,0:T(8,128)(2,1)S(1)}, u32[]{:S(2)}, u32[]{:S(2)}) async-start(bf16[8,128,256]{2,1,0:T(8,128)(2,1)} %bitcast.15), calls=%async_computation.3 | async-start | bytes 1048576 | tf_op jit(solution)/shard_map/all_to_all | solution.py:293
  116.8 0.8 copy-start.2
  (1 other events, 0.7 us)

commit v4 on v3

--- a/solution.py
+++ b/solution.py
@@ -16,6 +16,7 @@
 GROUP = 8
 ROWS = GROUP * BLK
 WIDE = 2048
+NARROW = 512
 F32 = jnp.float32
 BF16 = jnp.bfloat16
 
@@ -29,7 +30,7 @@
 
 
 def attention_kernel(
-    nz, nx, order, me, in0, in1, in2, in3, in4, in5, in6, in7,
+    nz, nx, me, in0, in1, in2, in3, in4, in5, in6, in7,
     oq, o0, o1a, o1b, o2a, o2b, o3a, o3b,
     ks, vs, qs, gs, scr, dkt, dvt, qacc, oacc, rowpos, sblk, spos,
     kv0, kv1a, kv1b, kv3a, kv3b, kv2a, kv2b, qg, stage, stage_q, in_sems, out_sems,
@@ -44,6 +45,7 @@
         copy.start()
     x = me[0]
     busy = me[1]
+    order = me.at[2 + nz:]
     per_part = 2 * nz
     half = per_part // 2
 
@@ -86,18 +88,17 @@
     dkt[...] = jnp.zeros_like(dkt)
     dvt[...] = jnp.zeros_like(dvt)
 
-    def chunk(c):
-        return pl.ds(pl.multiple_of(c * WIDE, WIDE), WIDE)
-
     def fold(op, s):
         r = s[:, :DH]
-        for i in range(1, WIDE // DH):
+        for i in range(1, s.shape[1] // DH):
             r = op(r, s[:, i * DH:(i + 1) * DH])
         return r
 
     def group_step(g, carry):
         base = g * GROUP
-        count = ((spos[base + GROUP - 1] + 1) * BLK + WIDE - 1) // WIDE
+        tiles = ((spos[base + GROUP - 1] + 1) * BLK + NARROW - 1) // NARROW
+        wide = tiles // (WIDE // NARROW)
+        rest = tiles % (WIDE // NARROW)
         for k in range(GROUP):
             within = lax.broadcasted_iota(jnp.int32, (BLK, DH), 0)
             rowpos[k * BLK:(k + 1) * BLK, :] = within + spos[base + k] * BLK
@@ -107,40 +108,52 @@
         q_t = q.T
         g_t = gr.T
 
-        def score_step(c, m):
-            s = mm_nt(q, ks[chunk(c), :])
-            key = lax.broadcasted_iota(jnp.int32, (ROWS, WIDE), 1) + c * WIDE
+        def sweep(step, value):
+            def over(width, offset):
+                def body(c, v):
+                    start = pl.multiple_of(offset + c * width, NARROW)
+                    return step(start, width, v)
+                return body
+            value = lax.fori_loop(0, wide, over(WIDE, 0), value)
+            return lax.fori_loop(0, rest, over(NARROW, wide * WIDE), value)
+
+        def score_step(start, width, m):
+            at = pl.ds(start, width)
+            s = mm_nt(q, ks[at, :])
+            key = lax.broadcasted_iota(jnp.int32, (ROWS, width), 1) + start
             s = jnp.where(key <= rowpos[:, :1], s, F32(-1e30))
-            scr[:, chunk(c)] = s
+            scr[:, at] = s
             return jnp.maximum(m, fold(jnp.maximum, s))
 
-        m = lax.fori_loop(0, count, score_step, jnp.full((ROWS, DH), -1e30, F32))
+        m = sweep(score_step, jnp.full((ROWS, DH), -1e30, F32))
         top = jnp.max(m, axis=1, keepdims=True)
         oacc[...] = jnp.zeros_like(oacc)
 
-        def expo_step(c, tot):
-            e = jnp.exp2((scr[:, chunk(c)] - top) * F32(SCALE2))
-            scr[:, chunk(c)] = e
-            oacc[...] += mm(e.astype(BF16), vs[chunk(c), :])
+        def expo_step(start, width, tot):
+            at = pl.ds(start, width)
+            e = jnp.exp2((scr[:, at] - top) * F32(SCALE2))
+            scr[:, at] = e
+            oacc[...] += mm(e.astype(BF16), vs[at, :])
             return tot + fold(jnp.add, e)
 
-        tot = lax.fori_loop(0, count, expo_step, jnp.zeros((ROWS, DH), F32))
+        tot = sweep(expo_step, jnp.zeros((ROWS, DH), F32))
         total = jnp.sum(tot, axis=1, keepdims=True)
         inv = 1.0 / total
         att = (oacc[...] / total).astype(BF16)
         dsum = jnp.sum(gr.astype(F32) * att.astype(F32), axis=1, keepdims=True)
         qacc[...] = jnp.zeros_like(qacc)
 
-        def back_step(c, carry):
-            dp = mm_nt(gr, vs[chunk(c), :])
-            p = scr[:, chunk(c)] * inv
+        def back_step(start, width, carry):
+            at = pl.ds(start, width)
+            dp = mm_nt(gr, vs[at, :])
+            p = scr[:, at] * inv
             ds = (p * (dp - dsum)).astype(BF16)
-            qacc[...] += mm(ds, ks[chunk(c), :])
-            dkt[:, chunk(c)] += mm(q_t, ds)
-            dvt[:, chunk(c)] += mm(g_t, p.astype(BF16))
+            qacc[...] += mm(ds, ks[at, :])
+            dkt[:, at] += mm(q_t, ds)
+            dvt[:, at] += mm(g_t, p.astype(BF16))
             return carry
 
-        lax.fori_loop(0, count, back_step, 0)
+        sweep(back_step, 0)
         dq = (qacc[...] * F32(SCALE)).astype(BF16)
         for k in range(GROUP):
             to = block_rows(sblk[base + k])
@@ -172,7 +185,7 @@
         copy.wait()
 
 
-def attention(nz, nx, order, me, qg, kv, near, far):
+def attention(nz, nx, me, qg, kv, near, far):
     rows = qg.shape[0]
     seq = rows * nx
     sm = pl.BlockSpec(memory_space=pltpu.SMEM)
@@ -183,7 +196,7 @@
     return pl.pallas_call(
         lambda *refs: attention_kernel(nz, nx, *refs),
         out_shape=(whole,) * 2 + (half,) * 6,
-        in_specs=[sm, sm] + [anywhere] * 8,
+        in_specs=[sm] + [anywhere] * 8,
         out_specs=(hbm,) * 8,
         scratch_shapes=[
             pltpu.VMEM((seq, DH), BF16),
@@ -210,70 +223,68 @@
         ],
         compiler_params=pltpu.CompilerParams(vmem_limit_bytes=36 * 2**20),
         name="attention",
-    )(order, me, kv, *near, *far, qg)
-
-
-def by_head(a, b, slots):
-    rows, width = a.shape
+    )(me, kv, *near, *far, qg)
+
+
+def by_head(pairs, slots):
+    rows, width = pairs[0][0].shape
     heads = width // DH
-
-    def kernel(a_ref, b_ref, out):
-        for slot in range(slots):
-            head = (slot + 2 * heads - slots) % heads
-            cols = slice(head * DH, (head + 1) * DH)
-            out[slot, :, :DH] = a_ref[:, cols]
-            out[slot, :, DH:] = b_ref[:, cols]
+    count = len(pairs)
+
+    def kernel(*refs):
+        ins, outs = refs[:2 * count], refs[2 * count:]
+        for i, out in enumerate(outs):
+            for slot in range(slots):
+                head = (slot + 2 * heads - slots) % heads
+                cols = slice(head * DH, (head + 1) * DH)
+                out[slot, :, :DH] = ins[2 * i][:, cols]
+                out[slot, :, DH:] = ins[2 * i + 1][:, cols]
 
     vm = pl.BlockSpec(memory_space=pltpu.VMEM)
     return pl.pallas_call(
         kernel,
-        out_shape=pltpu.VMEM((slots, rows, 2 * DH), BF16),
-        in_specs=[vm, vm],
-        out_specs=vm,
+        out_shape=(jax.ShapeDtypeStruct((slots, rows, 2 * DH), BF16),) * count,
+        in_specs=[vm] * (2 * count),
+        out_specs=(vm,) * count,
         name="by_head",
-    )(a, b)
-
-
-def from_heads(stacked, heads):
-    slots, rows = stacked.shape[:2]
+    )(*[array for pair in pairs for array in pair])
+
+
+def from_heads(early, late, heads):
+    slots, rows = late.shape[:2]
     first = slots - heads
 
-    def kernel(stack, a_ref, b_ref, got, a_own, b_own, sems):
-        fetch = [
-            pltpu.make_async_copy(stack.at[first + head], got.at[head], sems.at[head])
-            for head in range(heads)
-        ]
-        for copy in fetch:
-            copy.start()
-        for head in range(heads):
-            fetch[head].wait()
-            cols = slice(head * DH, (head + 1) * DH)
-            a_own[:, cols] = got[head, :, :DH]
-            b_own[:, cols] = got[head, :, DH:]
-        sends = [
-            pltpu.make_async_copy(a_own, a_ref, sems.at[heads]),
-            pltpu.make_async_copy(b_own, b_ref, sems.at[heads + 1]),
-        ]
-        for copy in sends:
-            copy.start()
+    def kernel(early_ref, late_ref, a_ref, b_ref, c_ref, d_ref, got, a_own, b_own, c_own, d_own, sems):
+        fetch = pltpu.make_async_copy(early_ref.at[first:], got, sems.at[0])
+        fetch.start()
+        sends = []
+
+        def split(stack, skip, left, right, left_out, right_out):
+            for head in range(heads):
+                cols = slice(head * DH, (head + 1) * DH)
+                left[:, cols] = stack[skip + head, :, :DH]
+                right[:, cols] = stack[skip + head, :, DH:]
+            for own, out in ((left, left_out), (right, right_out)):
+                sends.append(pltpu.make_async_copy(own, out, sems.at[len(sends) + 1]))
+                sends[-1].start()
+
+        split(late_ref, first, c_own, d_own, c_ref, d_ref)
+        fetch.wait()
+        split(got, 0, a_own, b_own, a_ref, b_ref)
         for copy in sends:
             copy.wait()
 
     hbm = pl.BlockSpec(memory_space=pltpu.HBM)
-    out = pltpu.HBM((rows, heads * DH), BF16)
     return pl.pallas_call(
         kernel,
-        out_shape=(out, out),
-        in_specs=[pl.BlockSpec(memory_space=pl.ANY)],
-        out_specs=(hbm, hbm),
-        scratch_shapes=[
-            pltpu.VMEM((heads, rows, 2 * DH), BF16),
-            pltpu.VMEM((rows, heads * DH), BF16),
-            pltpu.VMEM((rows, heads * DH), BF16),
-            pltpu.SemaphoreType.DMA((heads + 2,)),
-        ],
+        out_shape=(pltpu.HBM((rows, heads * DH), BF16),) * 4,
+        in_specs=[pl.BlockSpec(memory_space=pl.ANY), pl.BlockSpec(memory_space=pltpu.VMEM)],
+        out_specs=(hbm,) * 4,
+        scratch_shapes=[pltpu.VMEM((heads, rows, 2 * DH), BF16)]
+        + [pltpu.VMEM((rows, heads * DH), BF16)] * 4
+        + [pltpu.SemaphoreType.DMA((5,))],
         name="from_heads",
-    )(stacked)
+    )(early, pltpu.with_memory_space_constraint(late, pltpu.VMEM))
 
 
 def ring_orders(nz):
@@ -295,7 +306,8 @@
     def shards(queries, keys, values, out_grad, block_order):
         rows, width = queries.shape[1:]
         heads = width // DH
-        kv = exchange(by_head(keys[0], values[0], nz)).reshape(nz * rows, 2 * DH)
+        kv, qg = by_head(((keys[0], values[0]), (queries[0], out_grad[0])), nz)
+        kv = exchange(kv).reshape(nz * rows, 2 * DH)
         cut = nz * rows // 2
         kva, kvb = kv[:cut], kv[cut:]
         right_a = lax.ppermute(kva, "x", to(1))
@@ -304,13 +316,13 @@
         left_a = lax.ppermute(kva, "x", to(-1))
         far_a = lax.ppermute(right_a, "x", to(1))
         far_b = lax.ppermute(left_b, "x", to(-1))
-        qg = exchange(by_head(queries[0], out_grad[0], nz)).reshape(nz * rows, 2 * DH)
+        qg = exchange(qg).reshape(nz * rows, 2 * DH)
         ring = jnp.asarray(rings, jnp.int32)[lax.axis_index("kv")]
         idle = jnp.any(ring[:nz - heads] == lax.axis_index("z"))
         place = jnp.stack([lax.axis_index("x").astype(jnp.int32), 1 - idle.astype(jnp.int32)])
-        me = jnp.concatenate([place, ring])
+        me = jnp.concatenate([place, ring, block_order[0]])
         oq, o0, o1a, o1b, o2a, o2b, o3a, o3b = attention(
-            nz, nx, block_order[0], me, qg, kv, (right_a, right_b, left_a, left_b), (far_a, far_b)
+            nz, nx, me, qg, kv, (right_a, right_b, left_a, left_b), (far_a, far_b)
         )
         via_right = lax.ppermute(o2a, "x", to(1))
         via_left = lax.ppermute(o2b, "x", to(-1))
@@ -318,11 +330,12 @@
         r1a = lax.ppermute(o1a, "x", to(-1))
         r3a = lax.ppermute(o3a + via_right, "x", to(1))
         r1b = lax.ppermute(o1b + via_left, "x", to(-1))
-        att, q_grad = from_heads(exchange(oq.reshape(nz, rows, 2 * DH)), heads)
+        early = exchange(oq.reshape(nz, rows, 2 * DH))
         total_a = (o0[:cut].astype(F32) + r1a.astype(F32) + r3a.astype(F32)).astype(BF16)
         total_b = (o0[cut:].astype(F32) + r1b.astype(F32) + r3b.astype(F32)).astype(BF16)
         total = jnp.concatenate([total_a, total_b], axis=0)
-        k_grad, v_grad = from_heads(exchange(total.reshape(nz, rows, 2 * DH)), heads)
+        late = exchange(total.reshape(nz, rows, 2 * DH))
+        att, q_grad, k_grad, v_grad = from_heads(early, late, heads)
         return att[None], q_grad[None], k_grad[None], v_grad[None]
 
     return shards

time: 121 us -> 116 us (0.959)
  blocking collectives: 0 us -> 41.3 us
  waiting for transfers between devices: 48.1 us -> 22.8 us
  starting transfers between devices: 53.8 us -> 39.4 us
  Pallas kernels: 11.1 us -> 8.17 us
  local copies, waits for them, and re-layouts: 3.1 us -> 1.48 us
    all_to_all x0 -> x2, blocking collectives: none -> 41.3 us  [exchange(): lax.all_to_all(v, ('z', 'kv'), 0, 0, axis_index_groups=groups, tiled=True)]
    all_to_all x4 -> x2, waiting for transfers between devices: 25.2 us -> 0.01 us  [exchange(): lax.all_to_all(v, ('z', 'kv'), 0, 0, axis_index_groups=groups, tiled=True)]
    all_to_all x4 -> x2, starting transfers between devices: 36.7 us -> 22 us  [exchange(): lax.all_to_all(v, ('z', 'kv'), 0, 0, axis_index_groups=groups, tiled=True)]
    pallas_call x4 -> x2, Pallas kernels: 7.46 us -> 4.33 us  [the longest x1 2.39 us: by_head(): pl.pallas_call(kernel, out_shape=(jax.ShapeDtypeStruct((slots, rows, 2 *...]
    unnamed x18 -> x16, local copies, waits for them, and re-layouts: 3.06 us -> 1.44 us
  transfers between devices with their start and end apart: 16 -> 14, of which waited for: 10 -> 8; matrix products, arithmetic and copies ran while one was open for 2% -> 1% of each run, Pallas kernels for 3% -> 0%
where the time goes in v4:
time: 116 us
  blocking collectives  41.3 us (36%)
  starting transfers between devices  39.4 us (34%)
  waiting for transfers between devices  22.8 us (20%)
  Pallas kernels  8.17 us (7%)
  between operations  1.54 us (1%)
  local copies, waits for them, and re-layouts  1.48 us (1%)
    all_to_all x2, blocking collectives, exchange(): lax.all_to_all(v, ('z', 'kv'), 0, 0, axis_index_groups=groups, tiled=True)  41.3 us
    all_to_all x2, starting transfers between devices, exchange(): lax.all_to_all(v, ('z', 'kv'), 0, 0, axis_index_groups=groups, tiled=True)  22 us
    ppermute x1, waiting for transfers between devices, shards(): r3a = lax.ppermute(o3a + via_right, 'x', to(1))  5.48 us
    ppermute x1, waiting for transfers between devices, shards(): far_a = lax.ppermute(right_a, 'x', to(1))  5.14 us
    ppermute x1, waiting for transfers between devices, shards(): right_a = lax.ppermute(kva, 'x', to(1))  4.79 us
    pallas_call x1, Pallas kernels, attention(): pl.pallas_call(lambda *refs: attention_kernel(nz, nx, *refs), out_shape=(...  3.84 us
    ppermute x1, waiting for transfers between devices, shards(): r3b = lax.ppermute(o3b, 'x', to(1))  3.49 us
    ppermute x1, starting transfers between devices, shards(): r1b = lax.ppermute(o1b + via_left, 'x', to(-1))  3.22 us
  transfers between devices with their start and end apart: 14, of which 8 were waited for; matrix products, arithmetic and copies ran while one was open for 1% of the time, Pallas kernels for 0%

profile of v4, /device:TPU:8, one launch (start us, length us, event | category | flops | bytes accessed | tf_op | source)
XLA Modules:
  0.0 115.7 jit_solution(10703231465149820065)
XLA Ops:
  0.6 2.4 %by_head.1 = (bf16[8,128,256]{2,1,0:T(8,128)(2,1)}, bf16[8,128,256]{2,1,0:T(8,128)(2,1)}) custom-call(bf16[128,768]{1,0:T(8,128)(2,1)} %bitcast.27, bf16[128,768]{1,0:T(8,128)(2,1)} %bitcast.28, bf16[128,768]{1,0:T(8,128)(2,1)} %bitcast.29, bf16[128,768]{1,0:T(8,128)(2,1)} %bitcast.30), custom_call_target="tpu_custom_call" | custom-call | tf_op jit(solution)/shard_map/by_head/pallas_call | solution.py:244
  3.0 22.6 %all_to_all.20 = bf16[8,128,256]{2,1,0:T(8,128)(2,1)S(1)} all-to-all(bf16[8,128,256]{2,1,0:T(8,128)(2,1)} %get-tuple-element.18), channel_id=1, replica_groups={{0,64,128,192,224,160,96,32},{132,196,228,164,100,36,4,68},{1,65,129,19..., dimensions={0} | all-to-all | bytes 1048576 | tf_op jit(solution)/shard_map/all_to_all | solution.py:304
  25.6 5.5 %all-to-all-start.1 = ((bf16[8,128,256]{2,1,0:T(8,128)(2,1)}), bf16[8,128,256]{2,1,0:T(8,128)(2,1)S(1)}, u32[]{:S(2)}, u32[]{:S(2)}) async-start(bf16[8,128,256]{2,1,0:T(8,128)(2,1)} %get-tuple-element.19), calls=%async_computation.1 | async-start | bytes 1048576 | tf_op jit(solution)/shard_map/all_to_all | solution.py:304
  31.1 1.6 %collective-permute-start = (bf16[512,256]{1,0:T(8,128)(2,1)S(1)}, bf16[512,256]{1,0:T(8,128)(2,1)S(1)}, u32[]{:S(2)}, u32[]{:S(2)}) collective-permute-start(bf16[512,256]{1,0:T(8,128)(2,1)S(1)} %bitcast.25), channel_id=1, source_target_pairs={{0,8},{8,16},{16,24},{24,0},{1,9},{9,17},{17,25},{25,1},{2,10},{10... | collective-permute-start | bytes 786440 | tf_op jit(solution)/shard_map/ppermute | solution.py:313
  32.7 1.7 %collective-permute-start.3 = (bf16[512,256]{1,0:T(8,128)(2,1)S(1)}, bf16[512,256]{1,0:T(8,128)(2,1)S(1)}, u32[]{:S(2)}, u32[]{:S(2)}) collective-permute-start(bf16[512,256]{1,0:T(8,128)(2,1)S(1)} %bitcast.23), channel_id=1, source_target_pairs={{0,24},{8,0},{16,8},{24,16},{1,25},{9,1},{17,9},{25,17},{2,26},{10... | collective-permute-start | bytes 786440 | tf_op jit(solution)/shard_map/ppermute | solution.py:314
  34.5 1.5 %collective-permute-start.2 = (bf16[512,256]{1,0:T(8,128)(2,1)S(1)}, bf16[512,256]{1,0:T(8,128)(2,1)S(1)}, u32[]{:S(2)}, u32[]{:S(2)}) collective-permute-start(bf16[512,256]{1,0:T(8,128)(2,1)S(1)} %bitcast.26), channel_id=1, source_target_pairs={{0,24},{8,0},{16,8},{24,16},{1,25},{9,1},{17,9},{25,17},{2,26},{10... | collective-permute-start | bytes 786440 | tf_op jit(solution)/shard_map/ppermute | solution.py:316
  36.5 4.8 %collective-permute-done.refs_2_ = bf16[512,256]{1,0:T(8,128)(2,1)S(1)} collective-permute-done((bf16[512,256]{1,0:T(8,128)(2,1)S(1)}, bf16[512,256]{1,0:T(8,128)(2,1)S(1)}, u32[]{:S(2)}, u32[]{:S(2)}) %collective-permute-start) | collective-permute-done | bytes 262176 | tf_op jit(solution)/shard_map/ppermute | solution.py:313
  41.8 3.0 %collective-permute-start.5 = (bf16[512,256]{1,0:T(8,128)(2,1)S(1)}, bf16[512,256]{1,0:T(8,128)(2,1)S(1)}, u32[]{:S(2)}, u32[]{:S(2)}) collective-permute-start(bf16[512,256]{1,0:T(8,128)(2,1)S(1)} %collective-permute-done.3.refs_5_), channel_id=1, source_target_pairs={{0,24},{8,0},{16,8},{24,16},{1,25},{9,1},{17,9},{25,17},{2,26},{10... | collective-permute-start | bytes 786440 | tf_op jit(solution)/shard_map/ppermute | solution.py:318
  44.7 0.6 compare_reduce_fusion
  46.0 0.6 copy-done.4
  46.7 0.6 collective-permute-done.2.refs_4_
  47.4 5.1 %collective-permute-done.4.refs_6_ = bf16[512,256]{1,0:T(8,128)(2,1)S(1)} collective-permute-done((bf16[512,256]{1,0:T(8,128)(2,1)S(1)}, bf16[512,256]{1,0:T(8,128)(2,1)S(1)}, u32[]{:S(2)}, u32[]{:S(2)}) %collective-permute-start.4) | collective-permute-done | bytes 262176 | tf_op jit(solution)/shard_map/ppermute | solution.py:317
  53.0 3.8 %attention.1 = (bf16[1024,256]{1,0:T(8,128)(2,1)}, bf16[1024,256]{1,0:T(8,128)(2,1)}, bf16[512,256]{1,0:T(8,128)(2,1)}, bf16[512,256]{1,0:T(8,128)(2,1)}, bf16[5...) custom-call(s32[74]{0:T(128)S(1)} %pad_add_fusion.refs_0_, ...), custom_call_target="tpu_custom_call" | custom-call | tf_op jit(solution)/shard_map/attention/pallas_call | solution.py:196
  56.8 1.6 %collective-permute-start.7 = (bf16[512,256]{1,0:T(8,128)(2,1)}, bf16[512,256]{1,0:T(8,128)(2,1)S(1)}, u32[]{:S(2)}, u32[]{:S(2)}) collective-permute-start(bf16[512,256]{1,0:T(8,128)(2,1)} %get-tuple-element.24), channel_id=1, source_target_pairs={{0,8},{8,16},{16,24},{24,0},{1,9},{9,17},{17,25},{25,1},{2,10},{10... | collective-permute-start | bytes 786440 | tf_op jit(solution)/shard_map/ppermute | solution.py:327
  58.4 1.7 %collective-permute-start.9 = (bf16[512,256]{1,0:T(8,128)(2,1)}, bf16[512,256]{1,0:T(8,128)(2,1)S(1)}, u32[]{:S(2)}, u32[]{:S(2)}) collective-permute-start(bf16[512,256]{1,0:T(8,128)(2,1)} %get-tuple-element.26), channel_id=1, source_target_pairs={{0,24},{8,0},{16,8},{24,16},{1,25},{9,1},{17,9},{25,17},{2,26},{10... | collective-permute-start | bytes 786440 | tf_op jit(solution)/shard_map/ppermute | solution.py:328
  60.2 16.6 %all-to-all-start.2 = ((bf16[8,128,256]{2,1,0:T(8,128)(2,1)}), bf16[8,128,256]{2,1,0:T(8,128)(2,1)S(1)}, u32[]{:S(2)}, u32[]{:S(2)}) async-start(bf16[8,128,256]{2,1,0:T(8,128)(2,1)} %bitcast.22), calls=%async_computation.2 | async-start | bytes 1048576 | tf_op jit(solution)/shard_map/all_to_all | solution.py:304
  76.8 2.0 %collective-permute-start.6 = (bf16[512,256]{1,0:T(8,128)(2,1)S(1)}, bf16[512,256]{1,0:T(8,128)(2,1)S(1)}, u32[]{:S(2)}, u32[]{:S(2)}) collective-permute-start(bf16[512,256]{1,0:T(8,128)(2,1)S(1)} %copy-done.7), channel_id=1, source_target_pairs={{0,24},{8,0},{16,8},{24,16},{1,25},{9,1},{17,9},{25,17},{2,26},{10... | collective-permute-start | bytes 786440 | tf_op jit(solution)/shard_map/ppermute | solution.py:330
  79.1 0.8 copy-done.2
  79.9 3.2 %collective-permute-start.10 = (bf16[512,256]{1,0:T(8,128)(2,1)S(1)}, bf16[512,256]{1,0:T(8,128)(2,1)S(1)}, u32[]{:S(2)}, u32[]{:S(2)}) collective-permute-start(bf16[512,256]{1,0:T(8,128)(2,1)S(1)} %add.25), channel_id=1, source_target_pairs={{0,24},{8,0},{16,8},{24,16},{1,25},{9,1},{17,9},{25,17},{2,26},{10... | collective-permute-start | bytes 786440 | tf_op jit(solution)/shard_map/ppermute | solution.py:332
  83.1 2.6 %collective-permute-done.6 = bf16[512,256]{1,0:T(8,128)(2,1)S(1)} collective-permute-done((bf16[512,256]{1,0:T(8,128)(2,1)S(1)}, bf16[512,256]{1,0:T(8,128)(2,1)S(1)}, u32[]{:S(2)}, u32[]{:S(2)}) %collective-permute-start.6) | collective-permute-done | bytes 262176 | tf_op jit(solution)/shard_map/ppermute | solution.py:330
  85.7 3.5 %collective-permute-done.11 = bf16[512,256]{1,0:T(8,128)(2,1)S(1)} collective-permute-done((bf16[512,256]{1,0:T(8,128)(2,1)S(1)}, bf16[512,256]{1,0:T(8,128)(2,1)S(1)}, u32[]{:S(2)}, u32[]{:S(2)}) %collective-permute-start.11) | collective-permute-done | bytes 262176 | tf_op jit(solution)/shard_map/ppermute | solution.py:329
  89.2 5.5 %collective-permute-done.8 = bf16[512,256]{1,0:T(8,128)(2,1)S(1)} collective-permute-done((bf16[512,256]{1,0:T(8,128)(2,1)S(1)}, bf16[512,256]{1,0:T(8,128)(2,1)S(1)}, u32[]{:S(2)}, u32[]{:S(2)}) %collective-permute-start.8) | collective-permute-done | bytes 262176 | tf_op jit(solution)/shard_map/ppermute | solution.py:331
  94.9 18.7 %all_to_all.21.late_ref = bf16[8,128,256]{2,1,0:T(8,128)(2,1)S(1)} all-to-all(bf16[8,128,256]{2,1,0:T(8,128)(2,1)S(1)} %bitcast.21), channel_id=1, replica_groups={{0,64,128,192,224,160,96,32},{132,196,228,164,100,36,4,68},{1,65,129,19..., dimensions={0} | all-to-all | bytes 1048576 | tf_op jit(solution)/shard_map/all_to_all | solution.py:304
  113.6 1.9 %from_heads.1 = (bf16[128,768]{1,0:T(8,128)(2,1)}, bf16[128,768]{1,0:T(8,128)(2,1)}, bf16[128,768]{1,0:T(8,128)(2,1)}, bf16[128,768]{1,0:T(8,128)(2,1)}) custom-call(bf16[8,128,256]{2,1,0:T(8,128)(2,1)} %copy-done, bf16[8,128,256]{2,1,0:T(8,128)(2,1)S(1)} %all_to_all.21.late_ref), custom_call_target="tpu_custom_call" | custom-call | tf_op jit(solution)/shard_map/from_heads/pallas_call | solution.py:278
  (33 shorter events, 2.1 us)
Async XLA Ops:
  25.6 21.1 %all-to-all-start.1 = ((bf16[8,128,256]{2,1,0:T(8,128)(2,1)}), bf16[8,128,256]{2,1,0:T(8,128)(2,1)S(1)}, u32[]{:S(2)}, u32[]{:S(2)}) async-start(bf16[8,128,256]{2,1,0:T(8,128)(2,1)} %get-tuple-element.19), calls=%async_computation.1 | async-start | bytes 1048576 | tf_op jit(solution)/shard_map/all_to_all | solution.py:304
  31.1 10.1 %collective-permute-start = (bf16[512,256]{1,0:T(8,128)(2,1)S(1)}, bf16[512,256]{1,0:T(8,128)(2,1)S(1)}, u32[]{:S(2)}, u32[]{:S(2)}) collective-permute-start(bf16[512,256]{1,0:T(8,128)(2,1)S(1)} %bitcast.25), channel_id=1, source_target_pairs={{0,8},{8,16},{16,24},{24,0},{1,9},{9,17},{17,25},{25,1},{2,10},{10... | collective-permute-start | bytes 786440 | tf_op jit(solution)/shard_map/ppermute | solution.py:313
  32.7 9.0 %collective-permute-start.3 = (bf16[512,256]{1,0:T(8,128)(2,1)S(1)}, bf16[512,256]{1,0:T(8,128)(2,1)S(1)}, u32[]{:S(2)}, u32[]{:S(2)}) collective-permute-start(bf16[512,256]{1,0:T(8,128)(2,1)S(1)} %bitcast.23), channel_id=1, source_target_pairs={{0,24},{8,0},{16,8},{24,16},{1,25},{9,1},{17,9},{25,17},{2,26},{10... | collective-permute-start | bytes 786440 | tf_op jit(solution)/shard_map/ppermute | solution.py:314
  34.5 10.3 %copy-start.5 = (s32[2,8]{1,0:T(2,128)S(1)}, s32[2,8]{1,0:T(2,128)}, u32[]{:S(2)}) copy-start(s32[2,8]{1,0:T(2,128)} %constant.25.clone) | copy-start | bytes 196
  34.5 12.9 %collective-permute-start.2 = (bf16[512,256]{1,0:T(8,128)(2,1)S(1)}, bf16[512,256]{1,0:T(8,128)(2,1)S(1)}, u32[]{:S(2)}, u32[]{:S(2)}) collective-permute-start(bf16[512,256]{1,0:T(8,128)(2,1)S(1)} %bitcast.26), channel_id=1, source_target_pairs={{0,24},{8,0},{16,8},{24,16},{1,25},{9,1},{17,9},{25,17},{2,26},{10... | collective-permute-start | bytes 786440 | tf_op jit(solution)/shard_map/ppermute | solution.py:316
  36.0 11.4 %collective-permute-start.1 = (bf16[512,256]{1,0:T(8,128)(2,1)S(1)}, bf16[512,256]{1,0:T(8,128)(2,1)S(1)}, u32[]{:S(2)}, u32[]{:S(2)}) collective-permute-start(bf16[512,256]{1,0:T(8,128)(2,1)S(1)} %bitcast.24), channel_id=1, source_target_pairs={{0,8},{8,16},{16,24},{24,0},{1,9},{9,17},{17,25},{25,1},{2,10},{10... | collective-permute-start | bytes 786440 | tf_op jit(solution)/shard_map/ppermute | solution.py:315
  41.3 11.2 %collective-permute-start.4 = (bf16[512,256]{1,0:T(8,128)(2,1)S(1)}, bf16[512,256]{1,0:T(8,128)(2,1)S(1)}, u32[]{:S(2)}, u32[]{:S(2)}) collective-permute-start(bf16[512,256]{1,0:T(8,128)(2,1)S(1)} %collective-permute-done.refs_2_), channel_id=1, source_target_pairs={{0,8},{8,16},{16,24},{24,0},{1,9},{9,17},{17,25},{25,1},{2,10},{10... | collective-permute-start | bytes 786440 | tf_op jit(solution)/shard_map/ppermute | solution.py:317
  41.8 11.2 %collective-permute-start.5 = (bf16[512,256]{1,0:T(8,128)(2,1)S(1)}, bf16[512,256]{1,0:T(8,128)(2,1)S(1)}, u32[]{:S(2)}, u32[]{:S(2)}) collective-permute-start(bf16[512,256]{1,0:T(8,128)(2,1)S(1)} %collective-permute-done.3.refs_5_), channel_id=1, source_target_pairs={{0,24},{8,0},{16,8},{24,16},{1,25},{9,1},{17,9},{25,17},{2,26},{10... | collective-permute-start | bytes 786440 | tf_op jit(solution)/shard_map/ppermute | solution.py:318
  46.0 0.7 copy-start.4
  56.8 22.0 %collective-permute-start.7 = (bf16[512,256]{1,0:T(8,128)(2,1)}, bf16[512,256]{1,0:T(8,128)(2,1)S(1)}, u32[]{:S(2)}, u32[]{:S(2)}) collective-permute-start(bf16[512,256]{1,0:T(8,128)(2,1)} %get-tuple-element.24), channel_id=1, source_target_pairs={{0,8},{8,16},{16,24},{24,0},{1,9},{9,17},{17,25},{25,1},{2,10},{10... | collective-permute-start | bytes 786440 | tf_op jit(solution)/shard_map/ppermute | solution.py:327
  58.4 20.6 %collective-permute-start.9 = (bf16[512,256]{1,0:T(8,128)(2,1)}, bf16[512,256]{1,0:T(8,128)(2,1)S(1)}, u32[]{:S(2)}, u32[]{:S(2)}) collective-permute-start(bf16[512,256]{1,0:T(8,128)(2,1)} %get-tuple-element.26), channel_id=1, source_target_pairs={{0,24},{8,0},{16,8},{24,16},{1,25},{9,1},{17,9},{25,17},{2,26},{10... | collective-permute-start | bytes 786440 | tf_op jit(solution)/shard_map/ppermute | solution.py:328
  60.1 16.6 %copy-start.7 = (bf16[512,256]{1,0:T(8,128)(2,1)S(1)}, bf16[512,256]{1,0:T(8,128)(2,1)}, u32[]{:S(2)}) copy-start(bf16[512,256]{1,0:T(8,128)(2,1)} %get-tuple-element.22) | copy-start | bytes 786436
  60.1 18.6 %copy-start.6 = (bf16[512,256]{1,0:T(8,128)(2,1)S(1)}, bf16[512,256]{1,0:T(8,128)(2,1)}, u32[]{:S(2)}) copy-start(bf16[512,256]{1,0:T(8,128)(2,1)} %get-tuple-element.27) | copy-start | bytes 786436
  60.2 18.7 %copy-start.3 = (bf16[512,256]{1,0:T(8,128)(2,1)S(1)}, bf16[512,256]{1,0:T(8,128)(2,1)}, u32[]{:S(2)}) copy-start(bf16[512,256]{1,0:T(8,128)(2,1)} %get-tuple-element.23) | copy-start | bytes 786436
  60.2 34.7 %all-to-all-start.2 = ((bf16[8,128,256]{2,1,0:T(8,128)(2,1)}), bf16[8,128,256]{2,1,0:T(8,128)(2,1)S(1)}, u32[]{:S(2)}, u32[]{:S(2)}) async-start(bf16[8,128,256]{2,1,0:T(8,128)(2,1)} %bitcast.22), calls=%async_computation.2 | async-start | bytes 1048576 | tf_op jit(solution)/shard_map/all_to_all | solution.py:304
  76.8 8.9 %collective-permute-start.6 = (bf16[512,256]{1,0:T(8,128)(2,1)S(1)}, bf16[512,256]{1,0:T(8,128)(2,1)S(1)}, u32[]{:S(2)}, u32[]{:S(2)}) collective-permute-start(bf16[512,256]{1,0:T(8,128)(2,1)S(1)} %copy-done.7), channel_id=1, source_target_pairs={{0,24},{8,0},{16,8},{24,16},{1,25},{9,1},{17,9},{25,17},{2,26},{10... | collective-permute-start | bytes 786440 | tf_op jit(solution)/shard_map/ppermute | solution.py:330
  78.8 10.4 %collective-permute-start.11 = (bf16[512,256]{1,0:T(8,128)(2,1)S(1)}, bf16[512,256]{1,0:T(8,128)(2,1)S(1)}, u32[]{:S(2)}, u32[]{:S(2)}) collective-permute-start(bf16[512,256]{1,0:T(8,128)(2,1)S(1)} %copy-done.6), channel_id=1, source_target_pairs={{0,8},{8,16},{16,24},{24,0},{1,9},{9,17},{17,25},{25,1},{2,10},{10... | collective-permute-start | bytes 786440 | tf_op jit(solution)/shard_map/ppermute | solution.py:329
  78.9 1.0 copy-start.2
  78.9 15.7 %copy-start.1 = (bf16[1024,256]{1,0:T(8,128)(2,1)S(1)}, bf16[1024,256]{1,0:T(8,128)(2,1)}, u32[]{:S(2)}) copy-start(bf16[1024,256]{1,0:T(8,128)(2,1)} %get-tuple-element.21) | copy-start | bytes 1572868
  78.9 15.7 %collective-permute-start.8 = (bf16[512,256]{1,0:T(8,128)(2,1)S(1)}, bf16[512,256]{1,0:T(8,128)(2,1)S(1)}, u32[]{:S(2)}, u32[]{:S(2)}) collective-permute-start(bf16[512,256]{1,0:T(8,128)(2,1)S(1)} %add.23), channel_id=1, source_target_pairs={{0,8},{8,16},{16,24},{24,0},{1,9},{9,17},{17,25},{25,1},{2,10},{10... | collective-permute-start | bytes 786440 | tf_op jit(solution)/shard_map/ppermute | solution.py:331
  79.9 14.8 %collective-permute-start.10 = (bf16[512,256]{1,0:T(8,128)(2,1)S(1)}, bf16[512,256]{1,0:T(8,128)(2,1)S(1)}, u32[]{:S(2)}, u32[]{:S(2)}) collective-permute-start(bf16[512,256]{1,0:T(8,128)(2,1)S(1)} %add.25), channel_id=1, source_target_pairs={{0,24},{8,0},{16,8},{24,16},{1,25},{9,1},{17,9},{25,17},{2,26},{10... | collective-permute-start | bytes 786440 | tf_op jit(solution)/shard_map/ppermute | solution.py:332
  94.9 18.7 %copy-start = (bf16[8,128,256]{2,1,0:T(8,128)(2,1)}, bf16[8,128,256]{2,1,0:T(8,128)(2,1)S(1)}, u32[]{:S(2)}) copy-start(bf16[8,128,256]{2,1,0:T(8,128)(2,1)S(1)} %all-to-all-done.2.early_ref) | copy-start | bytes 1572868

commit v5 on v4

--- a/solution.py
+++ b/solution.py
@@ -232,20 +232,39 @@
     count = len(pairs)
 
     def kernel(*refs):
-        ins, outs = refs[:2 * count], refs[2 * count:]
+        ins, outs = refs[:2 * count], refs[2 * count:3 * count]
+        got, packed, sems = refs[3 * count:]
+        fetch = [
+            pltpu.make_async_copy(src, got.at[i], sems.at[i]) for i, src in enumerate(ins)
+        ]
+        for copy in fetch:
+            copy.start()
+        sends = []
         for i, out in enumerate(outs):
+            fetch[2 * i].wait()
+            fetch[2 * i + 1].wait()
             for slot in range(slots):
                 head = (slot + 2 * heads - slots) % heads
                 cols = slice(head * DH, (head + 1) * DH)
-                out[slot, :, :DH] = ins[2 * i][:, cols]
-                out[slot, :, DH:] = ins[2 * i + 1][:, cols]
-
-    vm = pl.BlockSpec(memory_space=pltpu.VMEM)
+                packed[i, slot, :, :DH] = got[2 * i, :, cols]
+                packed[i, slot, :, DH:] = got[2 * i + 1, :, cols]
+            sends.append(pltpu.make_async_copy(packed.at[i], out, sems.at[2 * count + i]))
+            sends[-1].start()
+        for copy in sends:
+            copy.wait()
+
+    anywhere = pl.BlockSpec(memory_space=pl.ANY)
+    hbm = pl.BlockSpec(memory_space=pltpu.HBM)
     return pl.pallas_call(
         kernel,
-        out_shape=(jax.ShapeDtypeStruct((slots, rows, 2 * DH), BF16),) * count,
-        in_specs=[vm] * (2 * count),
-        out_specs=(vm,) * count,
+        out_shape=(pltpu.HBM((slots, rows, 2 * DH), BF16),) * count,
+        in_specs=[anywhere] * (2 * count),
+        out_specs=(hbm,) * count,
+        scratch_shapes=[
+            pltpu.VMEM((2 * count, rows, width), BF16),
+            pltpu.VMEM((count, slots, rows, 2 * DH), BF16),
+            pltpu.SemaphoreType.DMA((3 * count,)),
+        ],
         name="by_head",
     )(*[array for pair in pairs for array in pair])
 
@@ -254,23 +273,25 @@
     slots, rows = late.shape[:2]
     first = slots - heads
 
-    def kernel(early_ref, late_ref, a_ref, b_ref, c_ref, d_ref, got, a_own, b_own, c_own, d_own, sems):
+    def kernel(early_ref, late_ref, a_ref, b_ref, c_ref, d_ref, got, sems):
         fetch = pltpu.make_async_copy(early_ref.at[first:], got, sems.at[0])
         fetch.start()
         sends = []
 
-        def split(stack, skip, left, right, left_out, right_out):
+        def split(stack, skip, left_out, right_out):
             for head in range(heads):
                 cols = slice(head * DH, (head + 1) * DH)
-                left[:, cols] = stack[skip + head, :, :DH]
-                right[:, cols] = stack[skip + head, :, DH:]
-            for own, out in ((left, left_out), (right, right_out)):
-                sends.append(pltpu.make_async_copy(own, out, sems.at[len(sends) + 1]))
-                sends[-1].start()
-
-        split(late_ref, first, c_own, d_own, c_ref, d_ref)
+                for out, at in ((left_out, slice(0, DH)), (right_out, slice(DH, 2 * DH))):
+                    sends.append(
+                        pltpu.make_async_copy(
+                            stack.at[skip + head, :, at], out.at[:, cols], sems.at[len(sends) + 1]
+                        )
+                    )
+                    sends[-1].start()
+
+        split(late_ref, first, c_ref, d_ref)
         fetch.wait()
-        split(got, 0, a_own, b_own, a_ref, b_ref)
+        split(got, 0, a_ref, b_ref)
         for copy in sends:
             copy.wait()
 
@@ -280,9 +301,10 @@
         out_shape=(pltpu.HBM((rows, heads * DH), BF16),) * 4,
         in_specs=[pl.BlockSpec(memory_space=pl.ANY), pl.BlockSpec(memory_space=pltpu.VMEM)],
         out_specs=(hbm,) * 4,
-        scratch_shapes=[pltpu.VMEM((heads, rows, 2 * DH), BF16)]
-        + [pltpu.VMEM((rows, heads * DH), BF16)] * 4
-        + [pltpu.SemaphoreType.DMA((5,))],
+        scratch_shapes=[
+            pltpu.VMEM((heads, rows, 2 * DH), BF16),
+            pltpu.SemaphoreType.DMA((4 * heads + 1,)),
+        ],
         name="from_heads",
     )(early, pltpu.with_memory_space_constraint(late, pltpu.VMEM))
 
@@ -306,7 +328,8 @@
     def shards(queries, keys, values, out_grad, block_order):
         rows, width = queries.shape[1:]
         heads = width // DH
-        kv, qg = by_head(((keys[0], values[0]), (queries[0], out_grad[0])), nz)
+        (kv,) = by_head(((keys[0], values[0]),), nz)
+        (qg,) = by_head(((queries[0], out_grad[0]),), nz)
         kv = exchange(kv).reshape(nz * rows, 2 * DH)
         cut = nz * rows // 2
         kva, kvb = kv[:cut], kv[cut:]

time: 116 us -> 116 us (level)
  blocking collectives: 41.3 us -> 18.7 us
  waiting for transfers between devices: 22.8 us -> 33.9 us
  starting transfers between devices: 39.4 us -> 48.5 us
  Pallas kernels: 8.17 us -> 9.79 us
    all_to_all x2 -> x1, blocking collectives: 41.3 us -> 18.7 us  [exchange(): lax.all_to_all(v, ('z', 'kv'), 0, 0, axis_index_groups=groups, tiled=True)]
    all_to_all x2 -> x3, waiting for transfers between devices: 0.01 us -> 12 us  [exchange(): lax.all_to_all(v, ('z', 'kv'), 0, 0, axis_index_groups=groups, tiled=True)]
    all_to_all x2 -> x3, starting transfers between devices: 22 us -> 31.9 us  [exchange(): lax.all_to_all(v, ('z', 'kv'), 0, 0, axis_index_groups=groups, tiled=True)]
    pallas_call x1 -> x2, Pallas kernels: 2.39 us -> 3.87 us  [by_head(): pl.pallas_call(kernel, out_shape=(pltpu.HBM((slots, rows, 2 * DH), BF16),...]
    ppermute x1, waiting for transfers between devices: 3.49 us -> 2.04 us  [shards(): r3b = lax.ppermute(o3b, 'x', to(1))]
  transfers between devices with their start and end apart: 14 -> 15, of which waited for: 8 -> 9; matrix products, arithmetic and copies ran while one was open for 1% -> 1% of each run, Pallas kernels for 0% -> 2%
where the time goes in v5:
time: 116 us; the launch traced here: 115 us
  starting transfers between devices  48.5 us (42%)
  waiting for transfers between devices  33.9 us (29%)
  blocking collectives  18.7 us (16%)
  Pallas kernels  9.79 us (8%)
  between operations  1.55 us (1%)
  local copies, waits for them, and re-layouts  1.48 us (1%)
    all_to_all x3, starting transfers between devices, exchange(): lax.all_to_all(v, ('z', 'kv'), 0, 0, axis_index_groups=groups, tiled=True)  31.9 us
    all_to_all x1, blocking collectives, exchange(): lax.all_to_all(v, ('z', 'kv'), 0, 0, axis_index_groups=groups, tiled=True)  18.7 us
    all_to_all x3, waiting for transfers between devices, exchange(): lax.all_to_all(v, ('z', 'kv'), 0, 0, axis_index_groups=groups, tiled=True)  12 us
    ppermute x1, waiting for transfers between devices, shards(): r3a = lax.ppermute(o3a + via_right, 'x', to(1))  5.38 us
    ppermute x1, waiting for transfers between devices, shards(): far_a = lax.ppermute(right_a, 'x', to(1))  5.01 us
    ppermute x1, waiting for transfers between devices, shards(): right_a = lax.ppermute(kva, 'x', to(1))  4.34 us
    pallas_call x2, Pallas kernels, by_head(): pl.pallas_call(kernel, out_shape=(pltpu.HBM((slots, rows, 2 * DH), BF16),...  3.87 us
    pallas_call x1, Pallas kernels, attention(): pl.pallas_call(lambda *refs: attention_kernel(nz, nx, *refs), out_shape=(...  3.82 us
  transfers between devices with their start and end apart: 15, of which 9 were waited for; matrix products, arithmetic and copies ran while one was open for 1% of the time, Pallas kernels for 2%

profile of v5, /device:TPU:8, one launch (start us, length us, event | category | flops | bytes accessed | tf_op | source)
XLA Modules:
  0.0 115.0 jit_solution(6723063618418800530)
XLA Ops:
  0.6 1.9 %by_head.2 = bf16[8,128,256]{2,1,0:T(8,128)(2,1)} custom-call(bf16[128,768]{1,0:T(8,128)(2,1)} %bitcast.27, bf16[128,768]{1,0:T(8,128)(2,1)} %bitcast.28), custom_call_target="tpu_custom_call" | custom-call | tf_op jit(solution)/shard_map/by_head/pallas_call | solution.py:258
  2.6 8.5 %all-to-all-start = ((bf16[8,128,256]{2,1,0:T(8,128)(2,1)}), bf16[8,128,256]{2,1,0:T(8,128)(2,1)S(1)}, u32[]{:S(2)}, u32[]{:S(2)}) async-start(bf16[8,128,256]{2,1,0:T(8,128)(2,1)} %by_head.2), calls=%async_computation | async-start | bytes 1048576 | tf_op jit(solution)/shard_map/all_to_all | solution.py:326
  11.1 1.9 %by_head.3 = bf16[8,128,256]{2,1,0:T(8,128)(2,1)} custom-call(bf16[128,768]{1,0:T(8,128)(2,1)} %bitcast.29, bf16[128,768]{1,0:T(8,128)(2,1)} %bitcast.30), custom_call_target="tpu_custom_call" | custom-call | tf_op jit(solution)/shard_map/by_head/pallas_call | solution.py:258
  13.0 12.0 %all-to-all-done = bf16[8,128,256]{2,1,0:T(8,128)(2,1)S(1)} async-done(((bf16[8,128,256]{2,1,0:T(8,128)(2,1)}), bf16[8,128,256]{2,1,0:T(8,128)(2,1)S(1)}, u32[]{:S(2)}, u32[]{:S(2)}) %all-to-all-start) | async-done | bytes 524320 | tf_op jit(solution)/shard_map/all_to_all | solution.py:326
  25.0 5.4 %all-to-all-start.1 = ((bf16[8,128,256]{2,1,0:T(8,128)(2,1)}), bf16[8,128,256]{2,1,0:T(8,128)(2,1)S(1)}, u32[]{:S(2)}, u32[]{:S(2)}) async-start(bf16[8,128,256]{2,1,0:T(8,128)(2,1)} %by_head.3), calls=%async_computation.1 | async-start | bytes 1048576 | tf_op jit(solution)/shard_map/all_to_all | solution.py:326
  30.5 1.6 %collective-permute-start = (bf16[512,256]{1,0:T(8,128)(2,1)S(1)}, bf16[512,256]{1,0:T(8,128)(2,1)S(1)}, u32[]{:S(2)}, u32[]{:S(2)}) collective-permute-start(bf16[512,256]{1,0:T(8,128)(2,1)S(1)} %bitcast.25), channel_id=1, source_target_pairs={{0,8},{8,16},{16,24},{24,0},{1,9},{9,17},{17,25},{25,1},{2,10},{10... | collective-permute-start | bytes 786440 | tf_op jit(solution)/shard_map/ppermute | solution.py:336
  32.1 1.7 %collective-permute-start.3 = (bf16[512,256]{1,0:T(8,128)(2,1)S(1)}, bf16[512,256]{1,0:T(8,128)(2,1)S(1)}, u32[]{:S(2)}, u32[]{:S(2)}) collective-permute-start(bf16[512,256]{1,0:T(8,128)(2,1)S(1)} %bitcast.23), channel_id=1, source_target_pairs={{0,24},{8,0},{16,8},{24,16},{1,25},{9,1},{17,9},{25,17},{2,26},{10... | collective-permute-start | bytes 786440 | tf_op jit(solution)/shard_map/ppermute | solution.py:337
  33.8 1.5 %collective-permute-start.2 = (bf16[512,256]{1,0:T(8,128)(2,1)S(1)}, bf16[512,256]{1,0:T(8,128)(2,1)S(1)}, u32[]{:S(2)}, u32[]{:S(2)}) collective-permute-start(bf16[512,256]{1,0:T(8,128)(2,1)S(1)} %bitcast.26), channel_id=1, source_target_pairs={{0,24},{8,0},{16,8},{24,16},{1,25},{9,1},{17,9},{25,17},{2,26},{10... | collective-permute-start | bytes 786440 | tf_op jit(solution)/shard_map/ppermute | solution.py:339
  35.9 4.3 %collective-permute-done.refs_2_ = bf16[512,256]{1,0:T(8,128)(2,1)S(1)} collective-permute-done((bf16[512,256]{1,0:T(8,128)(2,1)S(1)}, bf16[512,256]{1,0:T(8,128)(2,1)S(1)}, u32[]{:S(2)}, u32[]{:S(2)}) %collective-permute-start) | collective-permute-done | bytes 262176 | tf_op jit(solution)/shard_map/ppermute | solution.py:336
  40.8 3.0 %collective-permute-start.5 = (bf16[512,256]{1,0:T(8,128)(2,1)S(1)}, bf16[512,256]{1,0:T(8,128)(2,1)S(1)}, u32[]{:S(2)}, u32[]{:S(2)}) collective-permute-start(bf16[512,256]{1,0:T(8,128)(2,1)S(1)} %collective-permute-done.3.refs_5_), channel_id=1, source_target_pairs={{0,24},{8,0},{16,8},{24,16},{1,25},{9,1},{17,9},{25,17},{2,26},{10... | collective-permute-start | bytes 786440 | tf_op jit(solution)/shard_map/ppermute | solution.py:341
  46.4 5.0 %collective-permute-done.4.refs_6_ = bf16[512,256]{1,0:T(8,128)(2,1)S(1)} collective-permute-done((bf16[512,256]{1,0:T(8,128)(2,1)S(1)}, bf16[512,256]{1,0:T(8,128)(2,1)S(1)}, u32[]{:S(2)}, u32[]{:S(2)}) %collective-permute-start.4) | collective-permute-done | bytes 262176 | tf_op jit(solution)/shard_map/ppermute | solution.py:340
  52.0 3.8 %attention.1 = (bf16[1024,256]{1,0:T(8,128)(2,1)}, bf16[1024,256]{1,0:T(8,128)(2,1)}, bf16[512,256]{1,0:T(8,128)(2,1)}, bf16[512,256]{1,0:T(8,128)(2,1)}, bf16[5...) custom-call(s32[74]{0:T(128)S(1)} %pad_add_fusion.refs_0_, ...), custom_call_target="tpu_custom_call" | custom-call | tf_op jit(solution)/shard_map/attention/pallas_call | solution.py:196
  55.9 1.6 %collective-permute-start.7 = (bf16[512,256]{1,0:T(8,128)(2,1)}, bf16[512,256]{1,0:T(8,128)(2,1)S(1)}, u32[]{:S(2)}, u32[]{:S(2)}) collective-permute-start(bf16[512,256]{1,0:T(8,128)(2,1)} %get-tuple-element.20), channel_id=1, source_target_pairs={{0,8},{8,16},{16,24},{24,0},{1,9},{9,17},{17,25},{25,1},{2,10},{10... | collective-permute-start | bytes 786440 | tf_op jit(solution)/shard_map/ppermute | solution.py:350
  57.4 1.7 %collective-permute-start.9 = (bf16[512,256]{1,0:T(8,128)(2,1)}, bf16[512,256]{1,0:T(8,128)(2,1)S(1)}, u32[]{:S(2)}, u32[]{:S(2)}) collective-permute-start(bf16[512,256]{1,0:T(8,128)(2,1)} %get-tuple-element.22), channel_id=1, source_target_pairs={{0,24},{8,0},{16,8},{24,16},{1,25},{9,1},{17,9},{25,17},{2,26},{10... | collective-permute-start | bytes 786440 | tf_op jit(solution)/shard_map/ppermute | solution.py:351
  59.2 18.0 %all-to-all-start.2 = ((bf16[8,128,256]{2,1,0:T(8,128)(2,1)}), bf16[8,128,256]{2,1,0:T(8,128)(2,1)S(1)}, u32[]{:S(2)}, u32[]{:S(2)}) async-start(bf16[8,128,256]{2,1,0:T(8,128)(2,1)} %bitcast.22), calls=%async_computation.2 | async-start | bytes 1048576 | tf_op jit(solution)/shard_map/all_to_all | solution.py:326
  77.2 0.9 collective-permute-start.6
  78.1 1.2 %collective-permute-start.11 = (bf16[512,256]{1,0:T(8,128)(2,1)S(1)}, bf16[512,256]{1,0:T(8,128)(2,1)S(1)}, u32[]{:S(2)}, u32[]{:S(2)}) collective-permute-start(bf16[512,256]{1,0:T(8,128)(2,1)S(1)} %copy-done.6), channel_id=1, source_target_pairs={{0,8},{8,16},{16,24},{24,0},{1,9},{9,17},{17,25},{25,1},{2,10},{10... | collective-permute-start | bytes 786440 | tf_op jit(solution)/shard_map/ppermute | solution.py:352
  79.5 0.8 copy-done.2
  80.3 2.5 %collective-permute-start.10 = (bf16[512,256]{1,0:T(8,128)(2,1)S(1)}, bf16[512,256]{1,0:T(8,128)(2,1)S(1)}, u32[]{:S(2)}, u32[]{:S(2)}) collective-permute-start(bf16[512,256]{1,0:T(8,128)(2,1)S(1)} %add.25), channel_id=1, source_target_pairs={{0,24},{8,0},{16,8},{24,16},{1,25},{9,1},{17,9},{25,17},{2,26},{10... | collective-permute-start | bytes 786440 | tf_op jit(solution)/shard_map/ppermute | solution.py:355
  82.9 3.5 %collective-permute-done.6 = bf16[512,256]{1,0:T(8,128)(2,1)S(1)} collective-permute-done((bf16[512,256]{1,0:T(8,128)(2,1)S(1)}, bf16[512,256]{1,0:T(8,128)(2,1)S(1)}, u32[]{:S(2)}, u32[]{:S(2)}) %collective-permute-start.6) | collective-permute-done | bytes 262176 | tf_op jit(solution)/shard_map/ppermute | solution.py:353
  86.4 2.0 %collective-permute-done.11 = bf16[512,256]{1,0:T(8,128)(2,1)S(1)} collective-permute-done((bf16[512,256]{1,0:T(8,128)(2,1)S(1)}, bf16[512,256]{1,0:T(8,128)(2,1)S(1)}, u32[]{:S(2)}, u32[]{:S(2)}) %collective-permute-start.11) | collective-permute-done | bytes 262176 | tf_op jit(solution)/shard_map/ppermute | solution.py:352
  88.4 5.4 %collective-permute-done.8 = bf16[512,256]{1,0:T(8,128)(2,1)S(1)} collective-permute-done((bf16[512,256]{1,0:T(8,128)(2,1)S(1)}, bf16[512,256]{1,0:T(8,128)(2,1)S(1)}, u32[]{:S(2)}, u32[]{:S(2)}) %collective-permute-start.8) | collective-permute-done | bytes 262176 | tf_op jit(solution)/shard_map/ppermute | solution.py:354
  94.1 18.7 %all_to_all.20.late_ref = bf16[8,128,256]{2,1,0:T(8,128)(2,1)S(1)} all-to-all(bf16[8,128,256]{2,1,0:T(8,128)(2,1)S(1)} %bitcast.21), channel_id=1, replica_groups={{0,64,128,192,224,160,96,32},{132,196,228,164,100,36,4,68},{1,65,129,19..., dimensions={0} | all-to-all | bytes 1048576 | tf_op jit(solution)/shard_map/all_to_all | solution.py:326
  112.8 2.1 %from_heads.1 = (bf16[128,768]{1,0:T(8,128)(2,1)}, bf16[128,768]{1,0:T(8,128)(2,1)}, bf16[128,768]{1,0:T(8,128)(2,1)}, bf16[128,768]{1,0:T(8,128)(2,1)}) custom-call(bf16[8,128,256]{2,1,0:T(8,128)(2,1)} %copy-done, bf16[8,128,256]{2,1,0:T(8,128)(2,1)S(1)} %all_to_all.20.late_ref), custom_call_target="tpu_custom_call" | custom-call | tf_op jit(solution)/shard_map/from_heads/pallas_call | solution.py:299
  (35 shorter events, 4.2 us)
Async XLA Ops:
  2.6 22.5 %all-to-all-start = ((bf16[8,128,256]{2,1,0:T(8,128)(2,1)}), bf16[8,128,256]{2,1,0:T(8,128)(2,1)S(1)}, u32[]{:S(2)}, u32[]{:S(2)}) async-start(bf16[8,128,256]{2,1,0:T(8,128)(2,1)} %by_head.2), calls=%async_computation | async-start | bytes 1048576 | tf_op jit(solution)/shard_map/all_to_all | solution.py:326
  25.0 20.7 %all-to-all-start.1 = ((bf16[8,128,256]{2,1,0:T(8,128)(2,1)}), bf16[8,128,256]{2,1,0:T(8,128)(2,1)S(1)}, u32[]{:S(2)}, u32[]{:S(2)}) async-start(bf16[8,128,256]{2,1,0:T(8,128)(2,1)} %by_head.3), calls=%async_computation.1 | async-start | bytes 1048576 | tf_op jit(solution)/shard_map/all_to_all | solution.py:326
  30.5 9.7 %collective-permute-start = (bf16[512,256]{1,0:T(8,128)(2,1)S(1)}, bf16[512,256]{1,0:T(8,128)(2,1)S(1)}, u32[]{:S(2)}, u32[]{:S(2)}) collective-permute-start(bf16[512,256]{1,0:T(8,128)(2,1)S(1)} %bitcast.25), channel_id=1, source_target_pairs={{0,8},{8,16},{16,24},{24,0},{1,9},{9,17},{17,25},{25,1},{2,10},{10... | collective-permute-start | bytes 786440 | tf_op jit(solution)/shard_map/ppermute | solution.py:336
  32.1 8.7 %collective-permute-start.3 = (bf16[512,256]{1,0:T(8,128)(2,1)S(1)}, bf16[512,256]{1,0:T(8,128)(2,1)S(1)}, u32[]{:S(2)}, u32[]{:S(2)}) collective-permute-start(bf16[512,256]{1,0:T(8,128)(2,1)S(1)} %bitcast.23), channel_id=1, source_target_pairs={{0,24},{8,0},{16,8},{24,16},{1,25},{9,1},{17,9},{25,17},{2,26},{10... | collective-permute-start | bytes 786440 | tf_op jit(solution)/shard_map/ppermute | solution.py:337
  33.8 9.9 %copy-start.5 = (s32[2,8]{1,0:T(2,128)S(1)}, s32[2,8]{1,0:T(2,128)}, u32[]{:S(2)}) copy-start(s32[2,8]{1,0:T(2,128)} %constant.25.clone) | copy-start | bytes 196
  33.8 12.6 %collective-permute-start.2 = (bf16[512,256]{1,0:T(8,128)(2,1)S(1)}, bf16[512,256]{1,0:T(8,128)(2,1)S(1)}, u32[]{:S(2)}, u32[]{:S(2)}) collective-permute-start(bf16[512,256]{1,0:T(8,128)(2,1)S(1)} %bitcast.26), channel_id=1, source_target_pairs={{0,24},{8,0},{16,8},{24,16},{1,25},{9,1},{17,9},{25,17},{2,26},{10... | collective-permute-start | bytes 786440 | tf_op jit(solution)/shard_map/ppermute | solution.py:339
  35.4 11.0 %collective-permute-start.1 = (bf16[512,256]{1,0:T(8,128)(2,1)S(1)}, bf16[512,256]{1,0:T(8,128)(2,1)S(1)}, u32[]{:S(2)}, u32[]{:S(2)}) collective-permute-start(bf16[512,256]{1,0:T(8,128)(2,1)S(1)} %bitcast.24), channel_id=1, source_target_pairs={{0,8},{8,16},{16,24},{24,0},{1,9},{9,17},{17,25},{25,1},{2,10},{10... | collective-permute-start | bytes 786440 | tf_op jit(solution)/shard_map/ppermute | solution.py:338
  40.2 11.2 %collective-permute-start.4 = (bf16[512,256]{1,0:T(8,128)(2,1)S(1)}, bf16[512,256]{1,0:T(8,128)(2,1)S(1)}, u32[]{:S(2)}, u32[]{:S(2)}) collective-permute-start(bf16[512,256]{1,0:T(8,128)(2,1)S(1)} %collective-permute-done.refs_2_), channel_id=1, source_target_pairs={{0,8},{8,16},{16,24},{24,0},{1,9},{9,17},{17,25},{25,1},{2,10},{10... | collective-permute-start | bytes 786440 | tf_op jit(solution)/shard_map/ppermute | solution.py:340
  40.8 11.2 %collective-permute-start.5 = (bf16[512,256]{1,0:T(8,128)(2,1)S(1)}, bf16[512,256]{1,0:T(8,128)(2,1)S(1)}, u32[]{:S(2)}, u32[]{:S(2)}) collective-permute-start(bf16[512,256]{1,0:T(8,128)(2,1)S(1)} %collective-permute-done.3.refs_5_), channel_id=1, source_target_pairs={{0,24},{8,0},{16,8},{24,16},{1,25},{9,1},{17,9},{25,17},{2,26},{10... | collective-permute-start | bytes 786440 | tf_op jit(solution)/shard_map/ppermute | solution.py:341
  45.0 0.7 copy-start.4
  55.9 23.4 %collective-permute-start.7 = (bf16[512,256]{1,0:T(8,128)(2,1)}, bf16[512,256]{1,0:T(8,128)(2,1)S(1)}, u32[]{:S(2)}, u32[]{:S(2)}) collective-permute-start(bf16[512,256]{1,0:T(8,128)(2,1)} %get-tuple-element.20), channel_id=1, source_target_pairs={{0,8},{8,16},{16,24},{24,0},{1,9},{9,17},{17,25},{25,1},{2,10},{10... | collective-permute-start | bytes 786440 | tf_op jit(solution)/shard_map/ppermute | solution.py:350
  57.4 22.1 %collective-permute-start.9 = (bf16[512,256]{1,0:T(8,128)(2,1)}, bf16[512,256]{1,0:T(8,128)(2,1)S(1)}, u32[]{:S(2)}, u32[]{:S(2)}) collective-permute-start(bf16[512,256]{1,0:T(8,128)(2,1)} %get-tuple-element.22), channel_id=1, source_target_pairs={{0,24},{8,0},{16,8},{24,16},{1,25},{9,1},{17,9},{25,17},{2,26},{10... | collective-permute-start | bytes 786440 | tf_op jit(solution)/shard_map/ppermute | solution.py:351
  59.2 18.0 %copy-start.7 = (bf16[512,256]{1,0:T(8,128)(2,1)S(1)}, bf16[512,256]{1,0:T(8,128)(2,1)}, u32[]{:S(2)}) copy-start(bf16[512,256]{1,0:T(8,128)(2,1)} %get-tuple-element.18) | copy-start | bytes 786436
  59.2 18.9 %copy-start.6 = (bf16[512,256]{1,0:T(8,128)(2,1)S(1)}, bf16[512,256]{1,0:T(8,128)(2,1)}, u32[]{:S(2)}) copy-start(bf16[512,256]{1,0:T(8,128)(2,1)} %get-tuple-element.23) | copy-start | bytes 786436
  59.2 20.1 %copy-start.3 = (bf16[512,256]{1,0:T(8,128)(2,1)S(1)}, bf16[512,256]{1,0:T(8,128)(2,1)}, u32[]{:S(2)}) copy-start(bf16[512,256]{1,0:T(8,128)(2,1)} %get-tuple-element.19) | copy-start | bytes 786436
  59.2 34.9 %all-to-all-start.2 = ((bf16[8,128,256]{2,1,0:T(8,128)(2,1)}), bf16[8,128,256]{2,1,0:T(8,128)(2,1)S(1)}, u32[]{:S(2)}, u32[]{:S(2)}) async-start(bf16[8,128,256]{2,1,0:T(8,128)(2,1)} %bitcast.22), calls=%async_computation.2 | async-start | bytes 1048576 | tf_op jit(solution)/shard_map/all_to_all | solution.py:326
  77.2 9.2 %collective-permute-start.6 = (bf16[512,256]{1,0:T(8,128)(2,1)S(1)}, bf16[512,256]{1,0:T(8,128)(2,1)S(1)}, u32[]{:S(2)}, u32[]{:S(2)}) collective-permute-start(bf16[512,256]{1,0:T(8,128)(2,1)S(1)} %copy-done.7), channel_id=1, source_target_pairs={{0,24},{8,0},{16,8},{24,16},{1,25},{9,1},{17,9},{25,17},{2,26},{10... | collective-permute-start | bytes 786440 | tf_op jit(solution)/shard_map/ppermute | solution.py:353
  78.1 10.4 %collective-permute-start.11 = (bf16[512,256]{1,0:T(8,128)(2,1)S(1)}, bf16[512,256]{1,0:T(8,128)(2,1)S(1)}, u32[]{:S(2)}, u32[]{:S(2)}) collective-permute-start(bf16[512,256]{1,0:T(8,128)(2,1)S(1)} %copy-done.6), channel_id=1, source_target_pairs={{0,8},{8,16},{16,24},{24,0},{1,9},{9,17},{17,25},{25,1},{2,10},{10... | collective-permute-start | bytes 786440 | tf_op jit(solution)/shard_map/ppermute | solution.py:352
  79.3 1.0 copy-start.2
  79.4 14.5 %copy-start.1 = (bf16[1024,256]{1,0:T(8,128)(2,1)S(1)}, bf16[1024,256]{1,0:T(8,128)(2,1)}, u32[]{:S(2)}) copy-start(bf16[1024,256]{1,0:T(8,128)(2,1)} %get-tuple-element.17) | copy-start | bytes 1572868
  79.4 14.4 %collective-permute-start.8 = (bf16[512,256]{1,0:T(8,128)(2,1)S(1)}, bf16[512,256]{1,0:T(8,128)(2,1)S(1)}, u32[]{:S(2)}, u32[]{:S(2)}) collective-permute-start(bf16[512,256]{1,0:T(8,128)(2,1)S(1)} %add.23), channel_id=1, source_target_pairs={{0,8},{8,16},{16,24},{24,0},{1,9},{9,17},{17,25},{25,1},{2,10},{10... | collective-permute-start | bytes 786440 | tf_op jit(solution)/shard_map/ppermute | solution.py:354
  80.3 13.5 %collective-permute-start.10 = (bf16[512,256]{1,0:T(8,128)(2,1)S(1)}, bf16[512,256]{1,0:T(8,128)(2,1)S(1)}, u32[]{:S(2)}, u32[]{:S(2)}) collective-permute-start(bf16[512,256]{1,0:T(8,128)(2,1)S(1)} %add.25), channel_id=1, source_target_pairs={{0,24},{8,0},{16,8},{24,16},{1,25},{9,1},{17,9},{25,17},{2,26},{10... | collective-permute-start | bytes 786440 | tf_op jit(solution)/shard_map/ppermute | solution.py:355
  94.1 18.7 %copy-start = (bf16[8,128,256]{2,1,0:T(8,128)(2,1)}, bf16[8,128,256]{2,1,0:T(8,128)(2,1)S(1)}, u32[]{:S(2)}) copy-start(bf16[8,128,256]{2,1,0:T(8,128)(2,1)S(1)} %all-to-all-done.2.early_ref) | copy-start | bytes 1572868

commit v6 on v5

--- a/solution.py
+++ b/solution.py
@@ -13,10 +13,9 @@
 BLK = 64
 SCALE = 1.0 / math.sqrt(DH)
 SCALE2 = SCALE * math.log2(math.e)
-GROUP = 8
+GROUP = 4
 ROWS = GROUP * BLK
 WIDE = 2048
-NARROW = 512
 F32 = jnp.float32
 BF16 = jnp.bfloat16
 
@@ -32,7 +31,7 @@
 def attention_kernel(
     nz, nx, me, in0, in1, in2, in3, in4, in5, in6, in7,
     oq, o0, o1a, o1b, o2a, o2b, o3a, o3b,
-    ks, vs, qs, gs, scr, dkt, dvt, qacc, oacc, rowpos, sblk, spos,
+    ks, vs, qs, gs, scr, dkt, dvt, qacc, oacc, acc_m, acc_l, q_t, g_t, rowpos, sblk, spos,
     kv0, kv1a, kv1b, kv3a, kv3b, kv2a, kv2b, qg, stage, stage_q, in_sems, out_sems,
 ):
     arrays = (in0, in1, in2, in3, in4, in5, in6, in7)
@@ -85,8 +84,16 @@
         qs[at, :] = qg[j * BLK:(j + 1) * BLK, :DH]
         gs[at, :] = qg[j * BLK:(j + 1) * BLK, DH:]
 
-    dkt[...] = jnp.zeros_like(dkt)
-    dvt[...] = jnp.zeros_like(dvt)
+    rows = per_part * BLK
+    for k in range(per_part):
+        within = lax.broadcasted_iota(jnp.int32, (BLK, DH), 0)
+        rowpos[k * BLK:(k + 1) * BLK, :] = within + spos[k] * BLK
+    q_t[...] = qs[...].T
+    g_t[...] = gs[...].T
+    acc_m[...] = jnp.full_like(acc_m, -1e30)
+    acc_l[...] = jnp.zeros_like(acc_l)
+    oacc[...] = jnp.zeros_like(oacc)
+    qacc[...] = jnp.zeros_like(qacc)
 
     def fold(op, s):
         r = s[:, :DH]
@@ -94,74 +101,66 @@
             r = op(r, s[:, i * DH:(i + 1) * DH])
         return r
 
-    def group_step(g, carry):
-        base = g * GROUP
-        tiles = ((spos[base + GROUP - 1] + 1) * BLK + NARROW - 1) // NARROW
-        wide = tiles // (WIDE // NARROW)
-        rest = tiles % (WIDE // NARROW)
-        for k in range(GROUP):
-            within = lax.broadcasted_iota(jnp.int32, (BLK, DH), 0)
-            rowpos[k * BLK:(k + 1) * BLK, :] = within + spos[base + k] * BLK
-        at = pl.ds(pl.multiple_of(base * BLK, ROWS), ROWS)
-        q = qs[at, :]
-        gr = gs[at, :]
-        q_t = q.T
-        g_t = gr.T
-
-        def sweep(step, value):
-            def over(width, offset):
-                def body(c, v):
-                    start = pl.multiple_of(offset + c * width, NARROW)
-                    return step(start, width, v)
-                return body
-            value = lax.fori_loop(0, wide, over(WIDE, 0), value)
-            return lax.fori_loop(0, rest, over(NARROW, wide * WIDE), value)
-
-        def score_step(start, width, m):
-            at = pl.ds(start, width)
-            s = mm_nt(q, ks[at, :])
-            key = lax.broadcasted_iota(jnp.int32, (ROWS, width), 1) + start
-            s = jnp.where(key <= rowpos[:, :1], s, F32(-1e30))
-            scr[:, at] = s
-            return jnp.maximum(m, fold(jnp.maximum, s))
-
-        m = sweep(score_step, jnp.full((ROWS, DH), -1e30, F32))
-        top = jnp.max(m, axis=1, keepdims=True)
-        oacc[...] = jnp.zeros_like(oacc)
-
-        def expo_step(start, width, tot):
-            at = pl.ds(start, width)
-            e = jnp.exp2((scr[:, at] - top) * F32(SCALE2))
-            scr[:, at] = e
-            oacc[...] += mm(e.astype(BF16), vs[at, :])
-            return tot + fold(jnp.add, e)
-
-        tot = sweep(expo_step, jnp.zeros((ROWS, DH), F32))
-        total = jnp.sum(tot, axis=1, keepdims=True)
-        inv = 1.0 / total
-        att = (oacc[...] / total).astype(BF16)
-        dsum = jnp.sum(gr.astype(F32) * att.astype(F32), axis=1, keepdims=True)
-        qacc[...] = jnp.zeros_like(qacc)
-
-        def back_step(start, width, carry):
-            at = pl.ds(start, width)
-            dp = mm_nt(gr, vs[at, :])
-            p = scr[:, at] * inv
-            ds = (p * (dp - dsum)).astype(BF16)
-            qacc[...] += mm(ds, ks[at, :])
-            dkt[:, at] += mm(q_t, ds)
-            dvt[:, at] += mm(g_t, p.astype(BF16))
+    def sweep(step, empty=None):
+        def chunk(c, carry):
+            start = pl.multiple_of(c * WIDE, WIDE)
+            late = jnp.int32(0)
+            for k in range(per_part):
+                late = late + (spos[k] * BLK + (BLK - 1) >= start).astype(jnp.int32)
+            steps = (late + GROUP - 1) // GROUP
+            for v in range(1, per_part // GROUP + 1):
+                @pl.when(steps == v)
+                def _(v=v):
+                    step(pl.ds(start, WIDE), start, slice(rows - v * ROWS, rows))
+            if empty is not None:
+                @pl.when(steps == 0)
+                def _():
+                    empty(pl.ds(start, WIDE))
             return carry
 
-        sweep(back_step, 0)
-        dq = (qacc[...] * F32(SCALE)).astype(BF16)
-        for k in range(GROUP):
-            to = block_rows(sblk[base + k])
-            stage_q[to, :DH] = att[k * BLK:(k + 1) * BLK, :]
-            stage_q[to, DH:] = dq[k * BLK:(k + 1) * BLK, :]
-        return carry
-
-    lax.fori_loop(0, (per_part // GROUP) * busy, group_step, 0)
+        lax.fori_loop(0, (ks.shape[0] // WIDE) * busy, chunk, 0)
+
+    def score_step(at, start, low):
+        s = mm_nt(qs[low, :], ks[at, :])
+        key = lax.broadcasted_iota(jnp.int32, s.shape, 1) + start
+        s = jnp.where(key <= rowpos[low, :1], s, F32(-1e30))
+        scr[low, at] = s
+        acc_m[low, :] = jnp.maximum(acc_m[low, :], fold(jnp.maximum, s))
+
+    sweep(score_step)
+    acc_m[...] = jnp.broadcast_to(jnp.max(acc_m[...], axis=1, keepdims=True), acc_m.shape)
+
+    def expo_step(at, start, low):
+        e = jnp.exp2((scr[low, at] - acc_m[low, :1]) * F32(SCALE2))
+        scr[low, at] = e
+        oacc[low, :] += mm(e.astype(BF16), vs[at, :])
+        acc_l[low, :] += fold(jnp.add, e)
+
+    sweep(expo_step)
+    total = jnp.sum(acc_l[...], axis=1, keepdims=True)
+    att = (oacc[...] / total).astype(BF16)
+    dsum = jnp.sum(gs[...].astype(F32) * att.astype(F32), axis=1, keepdims=True)
+    acc_m[...] = jnp.broadcast_to(1.0 / total, acc_m.shape)
+    acc_l[...] = jnp.broadcast_to(dsum, acc_l.shape)
+
+    def back_step(at, start, low):
+        dp = mm_nt(gs[low, :], vs[at, :])
+        p = scr[low, at] * acc_m[low, :1]
+        ds = (p * (dp - acc_l[low, :1])).astype(BF16)
+        qacc[low, :] += mm(ds, ks[at, :])
+        dkt[:, at] = mm(q_t[:, low], ds)
+        dvt[:, at] = mm(g_t[:, low], p.astype(BF16))
+
+    def no_rows(at):
+        dkt[:, at] = jnp.zeros((DH, WIDE), F32)
+        dvt[:, at] = jnp.zeros((DH, WIDE), F32)
+
+    sweep(back_step, no_rows)
+    dq = (qacc[...] * F32(SCALE)).astype(BF16)
+    for k in range(per_part):
+        to = block_rows(sblk[k])
+        stage_q[to, :DH] = att[k * BLK:(k + 1) * BLK, :]
+        stage_q[to, DH:] = dq[k * BLK:(k + 1) * BLK, :]
 
     for t in range(ks.shape[0] // DH):
         at = slice(t * DH, (t + 1) * DH)
@@ -203,12 +202,16 @@
             pltpu.VMEM((seq, DH), BF16),
             pltpu.VMEM((rows, DH), BF16),
             pltpu.VMEM((rows, DH), BF16),
-            pltpu.VMEM((ROWS, seq), F32),
+            pltpu.VMEM((rows, seq), F32),
             pltpu.VMEM((DH, seq), F32),
             pltpu.VMEM((DH, seq), F32),
-            pltpu.VMEM((ROWS, DH), F32),
-            pltpu.VMEM((ROWS, DH), F32),
-            pltpu.VMEM((ROWS, DH), jnp.int32),
+            pltpu.VMEM((rows, DH), F32),
+            pltpu.VMEM((rows, DH), F32),
+            pltpu.VMEM((rows, DH), F32),
+            pltpu.VMEM((rows, DH), F32),
+            pltpu.VMEM((DH, rows), BF16),
+            pltpu.VMEM((DH, rows), BF16),
+            pltpu.VMEM((rows, DH), jnp.int32),
             pltpu.SMEM((rows // BLK,), jnp.int32),
             pltpu.SMEM((rows // BLK,), jnp.int32),
             pltpu.VMEM((rows, 2 * DH), BF16),
@@ -221,7 +224,7 @@
             pltpu.SemaphoreType.DMA((8,)),
             pltpu.SemaphoreType.DMA((9,)),
         ],
-        compiler_params=pltpu.CompilerParams(vmem_limit_bytes=36 * 2**20),
+        compiler_params=pltpu.CompilerParams(vmem_limit_bytes=48 * 2**20),
         name="attention",
     )(me, kv, *near, *far, qg)
 

time: 116 us -> 115 us (level); the launches traced: 115 us -> 115 us
  starting transfers between devices: 48.5 us -> 47.2 us
    all_to_all x3, starting transfers between devices: 31.9 us -> 29.7 us  [exchange(): lax.all_to_all(v, ('z', 'kv'), 0, 0, axis_index_groups=groups, tiled=True)]
    ppermute x1, waiting for transfers between devices: 3.54 us -> 1.47 us  [shards(): r1a = lax.ppermute(o1a, 'x', to(-1))]
    ppermute x1, waiting for transfers between devices: 2.04 us -> 3.79 us  [shards(): r3b = lax.ppermute(o3b, 'x', to(1))]
    ppermute x1, starting transfers between devices: 0.86 us -> 2.23 us  [shards(): r1a = lax.ppermute(o1a, 'x', to(-1))]
where the time goes in v6:
time: 115 us
  starting transfers between devices  47.2 us (41%)
  waiting for transfers between devices  33.8 us (29%)
  blocking collectives  19.4 us (17%)
  Pallas kernels  10.8 us (9%)
  between operations  1.57 us (1%)
  local copies, waits for them, and re-layouts  1.48 us (1%)
    all_to_all x3, starting transfers between devices, exchange(): lax.all_to_all(v, ('z', 'kv'), 0, 0, axis_index_groups=groups, tiled=True)  29.7 us
    all_to_all x1, blocking collectives, exchange(): lax.all_to_all(v, ('z', 'kv'), 0, 0, axis_index_groups=groups, tiled=True)  19.4 us
    all_to_all x3, waiting for transfers between devices, exchange(): lax.all_to_all(v, ('z', 'kv'), 0, 0, axis_index_groups=groups, tiled=True)  12 us
    ppermute x1, waiting for transfers between devices, shards(): r3a = lax.ppermute(o3a + via_right, 'x', to(1))  5.62 us
    ppermute x1, waiting for transfers between devices, shards(): far_a = lax.ppermute(right_a, 'x', to(1))  5.01 us
    pallas_call x1, Pallas kernels, attention(): pl.pallas_call(lambda *refs: attention_kernel(nz, nx, *refs), out_shape=(...  4.83 us
    ppermute x1, waiting for transfers between devices, shards(): right_a = lax.ppermute(kva, 'x', to(1))  4.34 us
    pallas_call x2, Pallas kernels, by_head(): pl.pallas_call(kernel, out_shape=(pltpu.HBM((slots, rows, 2 * DH), BF16),...  3.87 us
  transfers between devices with their start and end apart: 15, of which 9 were waited for; matrix products, arithmetic and copies ran while one was open for 1% of the time, Pallas kernels for 2%

profile of v6, /device:TPU:8, one launch (start us, length us, event | category | flops | bytes accessed | tf_op | source)
XLA Modules:
  0.0 115.4 jit_solution(14525278248407328661)
XLA Ops:
  0.6 1.9 %by_head.2 = bf16[8,128,256]{2,1,0:T(8,128)(2,1)} custom-call(bf16[128,768]{1,0:T(8,128)(2,1)} %bitcast.27, bf16[128,768]{1,0:T(8,128)(2,1)} %bitcast.28), custom_call_target="tpu_custom_call" | custom-call | tf_op jit(solution)/shard_map/by_head/pallas_call | solution.py:261
  2.6 8.5 %all-to-all-start = ((bf16[8,128,256]{2,1,0:T(8,128)(2,1)}), bf16[8,128,256]{2,1,0:T(8,128)(2,1)S(1)}, u32[]{:S(2)}, u32[]{:S(2)}) async-start(bf16[8,128,256]{2,1,0:T(8,128)(2,1)} %by_head.2), calls=%async_computation | async-start | bytes 1048576 | tf_op jit(solution)/shard_map/all_to_all | solution.py:329
  11.1 1.9 %by_head.3 = bf16[8,128,256]{2,1,0:T(8,128)(2,1)} custom-call(bf16[128,768]{1,0:T(8,128)(2,1)} %bitcast.29, bf16[128,768]{1,0:T(8,128)(2,1)} %bitcast.30), custom_call_target="tpu_custom_call" | custom-call | tf_op jit(solution)/shard_map/by_head/pallas_call | solution.py:261
  13.0 12.0 %all-to-all-done = bf16[8,128,256]{2,1,0:T(8,128)(2,1)S(1)} async-done(((bf16[8,128,256]{2,1,0:T(8,128)(2,1)}), bf16[8,128,256]{2,1,0:T(8,128)(2,1)S(1)}, u32[]{:S(2)}, u32[]{:S(2)}) %all-to-all-start) | async-done | bytes 524320 | tf_op jit(solution)/shard_map/all_to_all | solution.py:329
  25.0 5.4 %all-to-all-start.1 = ((bf16[8,128,256]{2,1,0:T(8,128)(2,1)}), bf16[8,128,256]{2,1,0:T(8,128)(2,1)S(1)}, u32[]{:S(2)}, u32[]{:S(2)}) async-start(bf16[8,128,256]{2,1,0:T(8,128)(2,1)} %by_head.3), calls=%async_computation.1 | async-start | bytes 1048576 | tf_op jit(solution)/shard_map/all_to_all | solution.py:329
  30.5 1.6 %collective-permute-start = (bf16[512,256]{1,0:T(8,128)(2,1)S(1)}, bf16[512,256]{1,0:T(8,128)(2,1)S(1)}, u32[]{:S(2)}, u32[]{:S(2)}) collective-permute-start(bf16[512,256]{1,0:T(8,128)(2,1)S(1)} %bitcast.25), channel_id=1, source_target_pairs={{0,8},{8,16},{16,24},{24,0},{1,9},{9,17},{17,25},{25,1},{2,10},{10... | collective-permute-start | bytes 786440 | tf_op jit(solution)/shard_map/ppermute | solution.py:339
  32.1 1.7 %collective-permute-start.3 = (bf16[512,256]{1,0:T(8,128)(2,1)S(1)}, bf16[512,256]{1,0:T(8,128)(2,1)S(1)}, u32[]{:S(2)}, u32[]{:S(2)}) collective-permute-start(bf16[512,256]{1,0:T(8,128)(2,1)S(1)} %bitcast.23), channel_id=1, source_target_pairs={{0,24},{8,0},{16,8},{24,16},{1,25},{9,1},{17,9},{25,17},{2,26},{10... | collective-permute-start | bytes 786440 | tf_op jit(solution)/shard_map/ppermute | solution.py:340
  33.8 1.5 %collective-permute-start.2 = (bf16[512,256]{1,0:T(8,128)(2,1)S(1)}, bf16[512,256]{1,0:T(8,128)(2,1)S(1)}, u32[]{:S(2)}, u32[]{:S(2)}) collective-permute-start(bf16[512,256]{1,0:T(8,128)(2,1)S(1)} %bitcast.26), channel_id=1, source_target_pairs={{0,24},{8,0},{16,8},{24,16},{1,25},{9,1},{17,9},{25,17},{2,26},{10... | collective-permute-start | bytes 786440 | tf_op jit(solution)/shard_map/ppermute | solution.py:342
  35.9 4.3 %collective-permute-done.refs_2_ = bf16[512,256]{1,0:T(8,128)(2,1)S(1)} collective-permute-done((bf16[512,256]{1,0:T(8,128)(2,1)S(1)}, bf16[512,256]{1,0:T(8,128)(2,1)S(1)}, u32[]{:S(2)}, u32[]{:S(2)}) %collective-permute-start) | collective-permute-done | bytes 262176 | tf_op jit(solution)/shard_map/ppermute | solution.py:339
  40.8 3.0 %collective-permute-start.5 = (bf16[512,256]{1,0:T(8,128)(2,1)S(1)}, bf16[512,256]{1,0:T(8,128)(2,1)S(1)}, u32[]{:S(2)}, u32[]{:S(2)}) collective-permute-start(bf16[512,256]{1,0:T(8,128)(2,1)S(1)} %collective-permute-done.3.refs_5_), channel_id=1, source_target_pairs={{0,24},{8,0},{16,8},{24,16},{1,25},{9,1},{17,9},{25,17},{2,26},{10... | collective-permute-start | bytes 786440 | tf_op jit(solution)/shard_map/ppermute | solution.py:344
  45.1 0.6 copy-done.4
  46.4 5.0 %collective-permute-done.4.refs_6_ = bf16[512,256]{1,0:T(8,128)(2,1)S(1)} collective-permute-done((bf16[512,256]{1,0:T(8,128)(2,1)S(1)}, bf16[512,256]{1,0:T(8,128)(2,1)S(1)}, u32[]{:S(2)}, u32[]{:S(2)}) %collective-permute-start.4) | collective-permute-done | bytes 262176 | tf_op jit(solution)/shard_map/ppermute | solution.py:343
  52.0 4.8 %attention.1 = (bf16[1024,256]{1,0:T(8,128)(2,1)}, bf16[1024,256]{1,0:T(8,128)(2,1)}, bf16[512,256]{1,0:T(8,128)(2,1)}, bf16[512,256]{1,0:T(8,128)(2,1)}, bf16[5...) custom-call(s32[74]{0:T(128)S(1)} %pad_add_fusion.refs_0_, ...), custom_call_target="tpu_custom_call" | custom-call | tf_op jit(solution)/shard_map/attention/pallas_call | solution.py:195
  56.9 1.6 %collective-permute-start.7 = (bf16[512,256]{1,0:T(8,128)(2,1)}, bf16[512,256]{1,0:T(8,128)(2,1)S(1)}, u32[]{:S(2)}, u32[]{:S(2)}) collective-permute-start(bf16[512,256]{1,0:T(8,128)(2,1)} %get-tuple-element.20), channel_id=1, source_target_pairs={{0,8},{8,16},{16,24},{24,0},{1,9},{9,17},{17,25},{25,1},{2,10},{10... | collective-permute-start | bytes 786440 | tf_op jit(solution)/shard_map/ppermute | solution.py:353
  58.4 1.7 %collective-permute-start.9 = (bf16[512,256]{1,0:T(8,128)(2,1)}, bf16[512,256]{1,0:T(8,128)(2,1)S(1)}, u32[]{:S(2)}, u32[]{:S(2)}) collective-permute-start(bf16[512,256]{1,0:T(8,128)(2,1)} %get-tuple-element.22), channel_id=1, source_target_pairs={{0,24},{8,0},{16,8},{24,16},{1,25},{9,1},{17,9},{25,17},{2,26},{10... | collective-permute-start | bytes 786440 | tf_op jit(solution)/shard_map/ppermute | solution.py:354
  60.2 15.7 %all-to-all-start.2 = ((bf16[8,128,256]{2,1,0:T(8,128)(2,1)}), bf16[8,128,256]{2,1,0:T(8,128)(2,1)S(1)}, u32[]{:S(2)}, u32[]{:S(2)}) async-start(bf16[8,128,256]{2,1,0:T(8,128)(2,1)} %bitcast.22), calls=%async_computation.2 | async-start | bytes 1048576 | tf_op jit(solution)/shard_map/all_to_all | solution.py:329
  75.9 2.2 %collective-permute-start.6 = (bf16[512,256]{1,0:T(8,128)(2,1)S(1)}, bf16[512,256]{1,0:T(8,128)(2,1)S(1)}, u32[]{:S(2)}, u32[]{:S(2)}) collective-permute-start(bf16[512,256]{1,0:T(8,128)(2,1)S(1)} %copy-done.7), channel_id=1, source_target_pairs={{0,24},{8,0},{16,8},{24,16},{1,25},{9,1},{17,9},{25,17},{2,26},{10... | collective-permute-start | bytes 786440 | tf_op jit(solution)/shard_map/ppermute | solution.py:356
  78.5 0.8 copy-done.2
  79.3 3.2 %collective-permute-start.10 = (bf16[512,256]{1,0:T(8,128)(2,1)S(1)}, bf16[512,256]{1,0:T(8,128)(2,1)S(1)}, u32[]{:S(2)}, u32[]{:S(2)}) collective-permute-start(bf16[512,256]{1,0:T(8,128)(2,1)S(1)} %add.25), channel_id=1, source_target_pairs={{0,24},{8,0},{16,8},{24,16},{1,25},{9,1},{17,9},{25,17},{2,26},{10... | collective-permute-start | bytes 786440 | tf_op jit(solution)/shard_map/ppermute | solution.py:358
  82.5 1.5 %collective-permute-done.6 = bf16[512,256]{1,0:T(8,128)(2,1)S(1)} collective-permute-done((bf16[512,256]{1,0:T(8,128)(2,1)S(1)}, bf16[512,256]{1,0:T(8,128)(2,1)S(1)}, u32[]{:S(2)}, u32[]{:S(2)}) %collective-permute-start.6) | collective-permute-done | bytes 262176 | tf_op jit(solution)/shard_map/ppermute | solution.py:356
  84.0 3.8 %collective-permute-done.11 = bf16[512,256]{1,0:T(8,128)(2,1)S(1)} collective-permute-done((bf16[512,256]{1,0:T(8,128)(2,1)S(1)}, bf16[512,256]{1,0:T(8,128)(2,1)S(1)}, u32[]{:S(2)}, u32[]{:S(2)}) %collective-permute-start.11) | collective-permute-done | bytes 262176 | tf_op jit(solution)/shard_map/ppermute | solution.py:355
  87.8 5.6 %collective-permute-done.8 = bf16[512,256]{1,0:T(8,128)(2,1)S(1)} collective-permute-done((bf16[512,256]{1,0:T(8,128)(2,1)S(1)}, bf16[512,256]{1,0:T(8,128)(2,1)S(1)}, u32[]{:S(2)}, u32[]{:S(2)}) %collective-permute-start.8) | collective-permute-done | bytes 262176 | tf_op jit(solution)/shard_map/ppermute | solution.py:357
  93.7 19.4 %all_to_all.20.late_ref = bf16[8,128,256]{2,1,0:T(8,128)(2,1)S(1)} all-to-all(bf16[8,128,256]{2,1,0:T(8,128)(2,1)S(1)} %bitcast.21), channel_id=1, replica_groups={{0,64,128,192,224,160,96,32},{132,196,228,164,100,36,4,68},{1,65,129,19..., dimensions={0} | all-to-all | bytes 1048576 | tf_op jit(solution)/shard_map/all_to_all | solution.py:329
  113.1 2.1 %from_heads.1 = (bf16[128,768]{1,0:T(8,128)(2,1)}, bf16[128,768]{1,0:T(8,128)(2,1)}, bf16[128,768]{1,0:T(8,128)(2,1)}, bf16[128,768]{1,0:T(8,128)(2,1)}) custom-call(bf16[8,128,256]{2,1,0:T(8,128)(2,1)} %copy-done, bf16[8,128,256]{2,1,0:T(8,128)(2,1)S(1)} %all_to_all.20.late_ref), custom_call_target="tpu_custom_call" | custom-call | tf_op jit(solution)/shard_map/from_heads/pallas_call | solution.py:302
  (35 shorter events, 3.7 us)
Async XLA Ops:
  2.6 22.5 %all-to-all-start = ((bf16[8,128,256]{2,1,0:T(8,128)(2,1)}), bf16[8,128,256]{2,1,0:T(8,128)(2,1)S(1)}, u32[]{:S(2)}, u32[]{:S(2)}) async-start(bf16[8,128,256]{2,1,0:T(8,128)(2,1)} %by_head.2), calls=%async_computation | async-start | bytes 1048576 | tf_op jit(solution)/shard_map/all_to_all | solution.py:329
  25.0 20.7 %all-to-all-start.1 = ((bf16[8,128,256]{2,1,0:T(8,128)(2,1)}), bf16[8,128,256]{2,1,0:T(8,128)(2,1)S(1)}, u32[]{:S(2)}, u32[]{:S(2)}) async-start(bf16[8,128,256]{2,1,0:T(8,128)(2,1)} %by_head.3), calls=%async_computation.1 | async-start | bytes 1048576 | tf_op jit(solution)/shard_map/all_to_all | solution.py:329
  30.5 9.7 %collective-permute-start = (bf16[512,256]{1,0:T(8,128)(2,1)S(1)}, bf16[512,256]{1,0:T(8,128)(2,1)S(1)}, u32[]{:S(2)}, u32[]{:S(2)}) collective-permute-start(bf16[512,256]{1,0:T(8,128)(2,1)S(1)} %bitcast.25), channel_id=1, source_target_pairs={{0,8},{8,16},{16,24},{24,0},{1,9},{9,17},{17,25},{25,1},{2,10},{10... | collective-permute-start | bytes 786440 | tf_op jit(solution)/shard_map/ppermute | solution.py:339
  32.1 8.7 %collective-permute-start.3 = (bf16[512,256]{1,0:T(8,128)(2,1)S(1)}, bf16[512,256]{1,0:T(8,128)(2,1)S(1)}, u32[]{:S(2)}, u32[]{:S(2)}) collective-permute-start(bf16[512,256]{1,0:T(8,128)(2,1)S(1)} %bitcast.23), channel_id=1, source_target_pairs={{0,24},{8,0},{16,8},{24,16},{1,25},{9,1},{17,9},{25,17},{2,26},{10... | collective-permute-start | bytes 786440 | tf_op jit(solution)/shard_map/ppermute | solution.py:340
  33.8 9.9 %copy-start.5 = (s32[2,8]{1,0:T(2,128)S(1)}, s32[2,8]{1,0:T(2,128)}, u32[]{:S(2)}) copy-start(s32[2,8]{1,0:T(2,128)} %constant.25.clone) | copy-start | bytes 196
  33.8 12.6 %collective-permute-start.2 = (bf16[512,256]{1,0:T(8,128)(2,1)S(1)}, bf16[512,256]{1,0:T(8,128)(2,1)S(1)}, u32[]{:S(2)}, u32[]{:S(2)}) collective-permute-start(bf16[512,256]{1,0:T(8,128)(2,1)S(1)} %bitcast.26), channel_id=1, source_target_pairs={{0,24},{8,0},{16,8},{24,16},{1,25},{9,1},{17,9},{25,17},{2,26},{10... | collective-permute-start | bytes 786440 | tf_op jit(solution)/shard_map/ppermute | solution.py:342
  35.4 11.0 %collective-permute-start.1 = (bf16[512,256]{1,0:T(8,128)(2,1)S(1)}, bf16[512,256]{1,0:T(8,128)(2,1)S(1)}, u32[]{:S(2)}, u32[]{:S(2)}) collective-permute-start(bf16[512,256]{1,0:T(8,128)(2,1)S(1)} %bitcast.24), channel_id=1, source_target_pairs={{0,8},{8,16},{16,24},{24,0},{1,9},{9,17},{17,25},{25,1},{2,10},{10... | collective-permute-start | bytes 786440 | tf_op jit(solution)/shard_map/ppermute | solution.py:341
  40.2 11.2 %collective-permute-start.4 = (bf16[512,256]{1,0:T(8,128)(2,1)S(1)}, bf16[512,256]{1,0:T(8,128)(2,1)S(1)}, u32[]{:S(2)}, u32[]{:S(2)}) collective-permute-start(bf16[512,256]{1,0:T(8,128)(2,1)S(1)} %collective-permute-done.refs_2_), channel_id=1, source_target_pairs={{0,8},{8,16},{16,24},{24,0},{1,9},{9,17},{17,25},{25,1},{2,10},{10... | collective-permute-start | bytes 786440 | tf_op jit(solution)/shard_map/ppermute | solution.py:343
  40.8 11.2 %collective-permute-start.5 = (bf16[512,256]{1,0:T(8,128)(2,1)S(1)}, bf16[512,256]{1,0:T(8,128)(2,1)S(1)}, u32[]{:S(2)}, u32[]{:S(2)}) collective-permute-start(bf16[512,256]{1,0:T(8,128)(2,1)S(1)} %collective-permute-done.3.refs_5_), channel_id=1, source_target_pairs={{0,24},{8,0},{16,8},{24,16},{1,25},{9,1},{17,9},{25,17},{2,26},{10... | collective-permute-start | bytes 786440 | tf_op jit(solution)/shard_map/ppermute | solution.py:344
  45.0 0.7 copy-start.4
  56.9 21.4 %collective-permute-start.7 = (bf16[512,256]{1,0:T(8,128)(2,1)}, bf16[512,256]{1,0:T(8,128)(2,1)S(1)}, u32[]{:S(2)}, u32[]{:S(2)}) collective-permute-start(bf16[512,256]{1,0:T(8,128)(2,1)} %get-tuple-element.20), channel_id=1, source_target_pairs={{0,8},{8,16},{16,24},{24,0},{1,9},{9,17},{17,25},{25,1},{2,10},{10... | collective-permute-start | bytes 786440 | tf_op jit(solution)/shard_map/ppermute | solution.py:353
  58.4 20.0 %collective-permute-start.9 = (bf16[512,256]{1,0:T(8,128)(2,1)}, bf16[512,256]{1,0:T(8,128)(2,1)S(1)}, u32[]{:S(2)}, u32[]{:S(2)}) collective-permute-start(bf16[512,256]{1,0:T(8,128)(2,1)} %get-tuple-element.22), channel_id=1, source_target_pairs={{0,24},{8,0},{16,8},{24,16},{1,25},{9,1},{17,9},{25,17},{2,26},{10... | collective-permute-start | bytes 786440 | tf_op jit(solution)/shard_map/ppermute | solution.py:354
  60.2 15.8 %copy-start.7 = (bf16[512,256]{1,0:T(8,128)(2,1)S(1)}, bf16[512,256]{1,0:T(8,128)(2,1)}, u32[]{:S(2)}) copy-start(bf16[512,256]{1,0:T(8,128)(2,1)} %get-tuple-element.18) | copy-start | bytes 786436
  60.2 18.0 %copy-start.6 = (bf16[512,256]{1,0:T(8,128)(2,1)S(1)}, bf16[512,256]{1,0:T(8,128)(2,1)}, u32[]{:S(2)}) copy-start(bf16[512,256]{1,0:T(8,128)(2,1)} %get-tuple-element.23) | copy-start | bytes 786436
  60.2 18.1 %copy-start.3 = (bf16[512,256]{1,0:T(8,128)(2,1)S(1)}, bf16[512,256]{1,0:T(8,128)(2,1)}, u32[]{:S(2)}) copy-start(bf16[512,256]{1,0:T(8,128)(2,1)} %get-tuple-element.19) | copy-start | bytes 786436
  60.2 33.5 %all-to-all-start.2 = ((bf16[8,128,256]{2,1,0:T(8,128)(2,1)}), bf16[8,128,256]{2,1,0:T(8,128)(2,1)S(1)}, u32[]{:S(2)}, u32[]{:S(2)}) async-start(bf16[8,128,256]{2,1,0:T(8,128)(2,1)} %bitcast.22), calls=%async_computation.2 | async-start | bytes 1048576 | tf_op jit(solution)/shard_map/all_to_all | solution.py:329
  75.9 8.1 %collective-permute-start.6 = (bf16[512,256]{1,0:T(8,128)(2,1)S(1)}, bf16[512,256]{1,0:T(8,128)(2,1)S(1)}, u32[]{:S(2)}, u32[]{:S(2)}) collective-permute-start(bf16[512,256]{1,0:T(8,128)(2,1)S(1)} %copy-done.7), channel_id=1, source_target_pairs={{0,24},{8,0},{16,8},{24,16},{1,25},{9,1},{17,9},{25,17},{2,26},{10... | collective-permute-start | bytes 786440 | tf_op jit(solution)/shard_map/ppermute | solution.py:356
  78.2 9.6 %collective-permute-start.11 = (bf16[512,256]{1,0:T(8,128)(2,1)S(1)}, bf16[512,256]{1,0:T(8,128)(2,1)S(1)}, u32[]{:S(2)}, u32[]{:S(2)}) collective-permute-start(bf16[512,256]{1,0:T(8,128)(2,1)S(1)} %copy-done.6), channel_id=1, source_target_pairs={{0,8},{8,16},{16,24},{24,0},{1,9},{9,17},{17,25},{25,1},{2,10},{10... | collective-permute-start | bytes 786440 | tf_op jit(solution)/shard_map/ppermute | solution.py:355
  78.3 1.0 copy-start.2
  78.3 15.1 %copy-start.1 = (bf16[1024,256]{1,0:T(8,128)(2,1)S(1)}, bf16[1024,256]{1,0:T(8,128)(2,1)}, u32[]{:S(2)}) copy-start(bf16[1024,256]{1,0:T(8,128)(2,1)} %get-tuple-element.17) | copy-start | bytes 1572868
  78.3 15.0 %collective-permute-start.8 = (bf16[512,256]{1,0:T(8,128)(2,1)S(1)}, bf16[512,256]{1,0:T(8,128)(2,1)S(1)}, u32[]{:S(2)}, u32[]{:S(2)}) collective-permute-start(bf16[512,256]{1,0:T(8,128)(2,1)S(1)} %add.23), channel_id=1, source_target_pairs={{0,8},{8,16},{16,24},{24,0},{1,9},{9,17},{17,25},{25,1},{2,10},{10... | collective-permute-start | bytes 786440 | tf_op jit(solution)/shard_map/ppermute | solution.py:357
  79.3 14.1 %collective-permute-start.10 = (bf16[512,256]{1,0:T(8,128)(2,1)S(1)}, bf16[512,256]{1,0:T(8,128)(2,1)S(1)}, u32[]{:S(2)}, u32[]{:S(2)}) collective-permute-start(bf16[512,256]{1,0:T(8,128)(2,1)S(1)} %add.25), channel_id=1, source_target_pairs={{0,24},{8,0},{16,8},{24,16},{1,25},{9,1},{17,9},{25,17},{2,26},{10... | collective-permute-start | bytes 786440 | tf_op jit(solution)/shard_map/ppermute | solution.py:358
  93.6 19.4 %copy-start = (bf16[8,128,256]{2,1,0:T(8,128)(2,1)}, bf16[8,128,256]{2,1,0:T(8,128)(2,1)S(1)}, u32[]{:S(2)}) copy-start(bf16[8,128,256]{2,1,0:T(8,128)(2,1)S(1)} %all-to-all-done.2.early_ref) | copy-start | bytes 1572868
